TPU v7x, 32 devices: a whole 2x2x4 slice. The times are simulated.
32 devices in a mesh: dp: 8 (over z, y), tensor: 4 (over x, core).
Axes of the slice: x: 2, y: 2, z: 4, core: 2. Of those that a mesh axis runs over, the one named last changes fastest.
Arguments:
- tokens: bfloat16 [16384, 768], P('dp'), may hold values from -6 to 6
- cotangent: bfloat16 [16384, 768], P('dp'), may hold values from -6 to 6
- row_lengths: int32 [32], P('dp'), may hold values from 64 to 512
- present: int32 [32, 64], P('dp'), may hold values 0 or 1
- groups: int32 [32, 512], P('dp'), may hold values from 0 to 63, never falling along the last dimension, each value on 1 to 16 neighbouring positions
- attn_weight: float32 [3, 768, 768], P(None, 'dp', 'tensor'), may hold values from -0.21875 to 0.21875
- attn_first: float32 [3, 768, 768], P(None, 'dp', 'tensor'), may hold values from -24 to 24
- attn_second: float32 [3, 768, 768], P(None, 'dp', 'tensor'), may hold values from 64 to 256
- mix_weight: float32 [768, 768], P('tensor', 'dp'), may hold values from -2.5 to 2.5
- mix_first: float32 [768, 768], P('tensor', 'dp'), may hold values from -32 to 32
- mix_second: float32 [768, 768], P('tensor', 'dp'), may hold values from 128 to 512
- up_weight: float32 [768, 3072], P('dp', 'tensor'), may hold values from -0.21875 to 0.21875
- up_first: float32 [768, 3072], P('dp', 'tensor'), may hold values from -96 to 96
- up_second: float32 [768, 3072], P('dp', 'tensor'), may hold values from 1024 to 4096
- down_weight: float32 [3072, 768], P('tensor', 'dp'), may hold values from -0.109375 to 0.109375
- down_first: float32 [3072, 768], P('tensor', 'dp'), may hold values from -192 to 192
- down_second: float32 [3072, 768], P('tensor', 'dp'), may hold values from 4096 to 16384
- head_bias: float32 [2, 768], P(None, ('tensor', 'dp')), may hold values from -4 to 4
- head_first: float32 [2, 768], P(None, ('tensor', 'dp')), may hold values from -512 to 512
- head_second: float32 [2, 768], P(None, ('tensor', 'dp')), may hold values from 8192 to 32768
- wide_bias: float32 [3072], P(('tensor', 'dp')), may hold values from -4 to 4
- wide_first: float32 [3072], P(('tensor', 'dp')), may hold values from -512 to 512
- wide_second: float32 [3072], P(('tensor', 'dp')), may hold values from 8192 to 32768
- norm_gains: float32 [2, 768], P(None, 'dp'), may hold values from 0.5 to 1.5
- gain_first: float32 [2, 768], P(None, 'dp'), may hold values from -512 to 512
- gain_second: float32 [2, 768], P(None, 'dp'), may hold values from 8192 to 32768
- shift_bias: float32 [4, 768], P(None, 'dp'), may hold values from -4 to 4
- shift_first: float32 [4, 768], P(None, 'dp'), may hold values from -512 to 512
- shift_second: float32 [4, 768], P(None, 'dp'), may hold values from 8192 to 32768
Outputs:
- layer_out: bfloat16 [16384, 768], P('dp')
- tokens_grad: bfloat16 [16384, 768], P('dp')
- attn_weight_new: float32 [3, 768, 768], P(None, 'dp', 'tensor')
- attn_first_new: float32 [3, 768, 768], P(None, 'dp', 'tensor')
- attn_second_new: float32 [3, 768, 768], P(None, 'dp', 'tensor')
- mix_weight_new: float32 [768, 768], P('tensor', 'dp')
- mix_first_new: float32 [768, 768], P('tensor', 'dp')
- mix_second_new: float32 [768, 768], P('tensor', 'dp')
- up_weight_new: float32 [768, 3072], P('dp', 'tensor')
- up_first_new: float32 [768, 3072], P('dp', 'tensor')
- up_second_new: float32 [768, 3072], P('dp', 'tensor')
- down_weight_new: float32 [3072, 768], P('tensor', 'dp')
- down_first_new: float32 [3072, 768], P('tensor', 'dp')
- down_second_new: float32 [3072, 768], P('tensor', 'dp')
- head_bias_new: float32 [2, 768], P(None, ('tensor', 'dp'))
- head_first_new: float32 [2, 768], P(None, ('tensor', 'dp'))
- head_second_new: float32 [2, 768], P(None, ('tensor', 'dp'))
- wide_bias_new: float32 [3072], P(('tensor', 'dp'))
- wide_first_new: float32 [3072], P(('tensor', 'dp'))
- wide_second_new: float32 [3072], P(('tensor', 'dp'))
- norm_gains_new: float32 [2, 768], P(None, 'dp')
- gain_first_new: float32 [2, 768], P(None, 'dp')
- gain_second_new: float32 [2, 768], P(None, 'dp')
- shift_bias_new: float32 [4, 768], P(None, 'dp')
- shift_first_new: float32 [4, 768], P(None, 'dp')
- shift_second_new: float32 [4, 768], P(None, 'dp')
- norm_pairs: float32 [2, 15], replicated
Inputs may be any that keep to these rules, and one draw needn't show every extreme that they name: Along a row the group ids never fall; every one of the 64 groups holds 1 to 16 slots.
All inputs are finite; a program needn't handle non-finite values. No bound on the sum of `present` on one device may be relied on, other than what follows from the above.
Results may differ from a plain program's by a relative error of at most 0.023.
Values may be sent and summed in bfloat16 or wider, within the bound.
No kernel may reach another device: no remote copies, remote signals or barrier semaphores. Data moves between devices by JAX's collectives and lax.ppermute only.
A program may use at most 128 MiB of HBM per device.

v0:
```python
import functools

import jax
import jax.numpy as jnp
from jax import lax
from jax.experimental import pallas as pl
from jax.experimental.pallas import tpu as pltpu
from jax.sharding import PartitionSpec as P

HEAD = 64
BF = jnp.bfloat16
F32 = jnp.float32
NN = (((1,), (0,)), ((), ()))
NT = (((1,), (1,)), ((), ()))
TN = (((0,), (0,)), ((), ()))
VMEM_LIMIT = 58 << 20
EXTRA = 64
COST = 0.5e9


def mm(a, b, dims):
    return lax.dot_general(a, b, dims, preferred_element_type=F32)


def full(*shape):
    return pl.BlockSpec(shape, lambda i: (0,) * len(shape))


def per(*shape):
    return pl.BlockSpec((1,) + shape, lambda i: (i,) + (0,) * len(shape))


ANY = pl.BlockSpec(memory_space=pl.ANY)
SCALARS = pl.BlockSpec(memory_space=pltpu.SMEM)


def out(shape, dtype=F32):
    return jax.ShapeDtypeStruct(shape, dtype)


def call(kernel, grid, in_specs, out_specs, out_shape, scratch=(), us=2.0):
    return pl.pallas_call(
        kernel,
        grid=(grid,),
        in_specs=in_specs,
        out_specs=out_specs,
        out_shape=out_shape,
        scratch_shapes=list(scratch),
        compiler_params=pltpu.CompilerParams(vmem_limit_bytes=VMEM_LIMIT),
        cost_estimate=pl.CostEstimate(
            flops=int(us * COST), bytes_accessed=1000, transcendentals=0
        ),
    )


class Pieces:
    def __init__(self, arrays, plan, where, blocks, rows, lanes, group=None):
        self.arrays, self.plan, self.where, self.group = arrays, plan, where, group
        self.blocks, self.rows, self.lanes = blocks, rows, lanes

    def scratch(self):
        if self.group is not None:
            shape, count = (self.blocks, 8, self.rows // 8, self.lanes), 1
        elif self.plan is None:
            shape, count = (self.blocks, self.rows, self.lanes), 1
        else:
            shape, count = (self.blocks, 4, 2, self.rows // 8, self.lanes), 4
        return [pltpu.VMEM(shape, BF), pltpu.SemaphoreType.DMA((self.blocks, count))]

    def start(self, refs, where_ref, buffer, sems, ps=None):
        for p in range(self.blocks) if ps is None else ps:
            if self.group is not None:
                source = refs[0].at[:, where_ref[2] ^ p, self.group]
                pltpu.make_async_copy(source, buffer.at[p], sems.at[p, 0]).start()
                continue
            if self.plan is None:
                pltpu.make_async_copy(refs[0].at[p], buffer.at[p], sems.at[p, 0]).start()
                continue
            for number, (array, y_rel, pair_rel) in enumerate(self.plan[p]):
                pair = (where_ref[0] // 2) ^ pair_rel
                target = buffer.at[p, pl.ds(pair * 2, 2), where_ref[1] ^ y_rel]
                pltpu.make_async_copy(refs[array], target, sems.at[p, number]).start()

    def wait(self, refs, p, buffer, sems):
        if self.group is not None:
            source = refs[0].at[:, 0, self.group]
            pltpu.make_async_copy(source, buffer.at[p], sems.at[p, 0]).wait()
            return
        if self.plan is None:
            pltpu.make_async_copy(refs[0].at[0], buffer.at[p], sems.at[p, 0]).wait()
            return
        for number in range(4):
            target = buffer.at[p, pl.ds(0, 2), 0]
            pltpu.make_async_copy(refs[0], target, sems.at[p, number]).wait()

    def read(self, buffer, p, first, last):
        if self.group is not None:
            return buffer[p, :, :, first:last].reshape(self.rows, last - first)
        if self.plan is None:
            return buffer[p, :, first:last]
        return buffer[p, :, :, :, first:last].reshape(self.rows, last - first)


def tie(array, deps):
    return lax.optimization_barrier((array, tuple(deps)))[0] if deps else array


class GenericComm:
    small_inside = False

    def __init__(self, dp, tensor):
        self.dp, self.tensor = dp, tensor
        self.where = jnp.zeros((2,), jnp.int32)

    def gather(self, shard):
        return GenericGather(self, shard)

    def gather_stacked(self, shard):
        rows = shard.shape[0] // 2
        return [GenericGather(self, part).core() for part in (shard[:rows], shard[rows:])]

    def gather_small(self, vector):
        return lax.all_gather(lax.all_gather(vector, "dp", axis=0), "tensor", axis=0)

    def scatter_small(self, vectors):
        own = lax.psum_scatter(vectors, "tensor", scatter_dimension=0)
        return lax.psum_scatter(own, "dp", scatter_dimension=0)

    def total(self, values):
        return lax.psum(values, ("dp", "tensor"))

    def reduction(self, lefts):
        return GenericReduction(self, lefts)

    def block_sets(self):
        return [range(self.tensor)]


class GenericGather:
    def __init__(self, comm, shard):
        self.comm, self.shard = comm, shard

    def z(self, deps):
        return []

    def xy(self, deps):
        return []

    def diagonal(self, deps):
        pass

    def core(self):
        rows = lax.all_gather(self.shard, "dp", axis=0, tiled=True)
        blocks = lax.all_gather(rows, "tensor", axis=0)
        return Pieces([blocks], None, self.comm.where, *blocks.shape)


class GenericReduction:
    def __init__(self, comm, lefts):
        self.comm, self.lefts = comm, lefts

    def core(self, rights, extra=None):
        self.rights = rights
        return []


    def last(self):
        stacked = grads(list(zip(self.lefts, self.rights)), range(self.comm.tensor))
        own = lax.psum_scatter(stacked, "tensor", scatter_dimension=0)
        return [lax.psum_scatter(own, "dp", scatter_dimension=0, tiled=True).astype(F32)]


class GridComm:
    small_inside = True

    def __init__(self):
        self.z = lax.axis_index("dp") // 2
        self.y = lax.axis_index("dp") % 2
        rank = lax.axis_index("tensor")
        self.where = jnp.stack([self.z, self.y, rank]).astype(jnp.int32)

    @staticmethod
    def send(array, dp_xor, tensor_xor):
        pairs = [
            (d * 4 + t, (d ^ dp_xor) * 4 + (t ^ tensor_xor)) for d in range(8) for t in range(4)
        ]
        return lax.ppermute(array, ("dp", "tensor"), pairs)

    def send_core(self, array):
        return self.send(array, 0, 1)

    def send_x(self, array):
        return self.send(array, 0, 2)

    def send_y(self, array):
        return self.send(array, 1, 0)

    def send_z(self, array, k):
        return self.send(array, 2 * k, 0)

    def gather(self, shard):
        return GridGather(self, shard)

    def gather_stacked(self, shard):
        rows, lanes = shard.shape[0] // 2, shard.shape[1]
        everything = lax.all_gather(shard, ("dp", "tensor"), axis=0, tiled=True)
        everything = everything.reshape(8, 4, 2, rows, lanes)
        return [Pieces([everything], None, self.where, 4, 8 * rows, lanes, g) for g in range(2)]

    def total(self, values):
        values = values + self.send_core(values)
        sent = self.send_x(values), self.send_y(values), self.send(values, 1, 2)
        values = values + sent[0] + (sent[1] + sent[2])
        sent = [self.send_z(values, k) for k in (1, 2, 3)]
        return values + sent[0] + (sent[1] + sent[2])

    def reduction(self, lefts):
        return Reduction(self, lefts)

    def block_sets(self):
        return [(1, 3), (0, 2)]


class GridGather:
    def __init__(self, comm, shard):
        self.comm, self.shard = comm, shard

    def z(self, deps):
        shard = tie(self.shard, deps)
        self.by_z = [shard] + [self.comm.send_z(shard, k) for k in (1, 2, 3)]
        return self.by_z[1:]

    def xy(self, deps):
        low = pair(self.by_z[0], self.by_z[1], self.comm.where)
        high = pair(self.by_z[2], self.by_z[3], self.comm.where)
        low, high = tie(low, deps), tie(high, deps)
        x_low, y_low = self.comm.send_x(low), self.comm.send_y(low)
        x_high, y_high = self.comm.send_x(high), self.comm.send_y(high)
        self.near, self.far = [low, high, y_low, y_high], [x_low, x_high]
        return [x_high, y_high]

    def diagonal(self, deps):
        y_low, x_high = tie(self.near[2], deps), tie(self.far[1], deps)
        self.far += [self.comm.send_x(y_low), self.comm.send_y(x_high)]

    def core(self):
        near_core = [self.comm.send_core(a) for a in self.near]
        far_core = [self.comm.send_core(a) for a in self.far]
        arrays = self.near + near_core + self.far + far_core
        plan = [[(4 * p + c, c // 2, c % 2) for c in range(4)] for p in range(4)]
        rows, lanes = self.shard.shape
        return Pieces(arrays, plan, self.comm.where, 4, 8 * rows, lanes)


class Reduction:
    def __init__(self, comm, lefts):
        self.comm, self.lefts = comm, lefts

    def core(self, rights, extra=None):
        odd = grads(list(zip(self.lefts, rights)), (1, 3), extra)
        self.core_got = self.comm.send_core(odd)
        return [odd]

    def split(self, rights, extra=None, deps=()):
        terms = list(zip(self.lefts, rights))
        split = grads_split(terms, tie(self.core_got, deps), self.comm.where, extra)
        x_first, y_first, self.x_second, self.y_second, self.mine = split
        self.x_got, self.y_got = self.comm.send_x(x_first), self.comm.send_y(y_first)
        return [self.mine]

    def neighbour(self, deps=()):
        x_second, y_second = add_low(
            tie(self.x_second, deps), self.y_second, self.x_got, self.y_got
        )
        self.x_got2, self.y_got2 = self.comm.send_x(x_second), self.comm.send_y(y_second)
        return [x_second, y_second]

    def last(self, deps=(), us=2.8):
        mine = tie(self.mine, deps)[None]
        low = [(mine, 0), (self.x_got[None], 2), (self.y_got2[None], 0)]
        high = [(mine, 2), (self.y_got[None], 2), (self.x_got2[None], 0)]
        parts = combine([low, high], None, self.comm.where, us)
        self.done = [parts[0]]
        return [parts[0]] + [self.comm.send_z(parts[k], k) for k in (1, 2, 3)]


def pair(first, second, where):
    rows, lanes = first.shape

    def kernel(where_ref, first_ref, second_ref, out_ref):
        odd = where_ref[0] % 2
        out_ref[odd] = first_ref[...]
        out_ref[1 - odd] = second_ref[...]

    return call(
        kernel, 1, [SCALARS, full(rows, lanes), full(rows, lanes)], full(2, rows, lanes),
        out((2, rows, lanes), BF), us=1.8,
    )(where, first, second)


def add_low(x_second, y_second, x_got, y_got):
    half = x_second.shape

    def kernel(x_ref, y_ref, xg_ref, yg_ref, xo_ref, yo_ref):
        xo_ref[...] = (x_ref[...].astype(F32) + yg_ref[...].astype(F32)).astype(BF)
        yo_ref[...] = (y_ref[...].astype(F32) + xg_ref[...].astype(F32)).astype(BF)

    return call(
        kernel, 1, [full(*half)] * 4, [full(*half)] * 2, [out(half, BF), out(half, BF)],
        us=2.0,
    )(x_second, y_second, x_got, y_got)


def block_of(right, p):
    if not isinstance(right, list):
        return right, p
    for ps, array in right:
        if p in ps:
            return array, list(ps).index(p)
    raise KeyError(p)


def grads(terms, ps, extra=None):
    ps = list(ps)
    d, n = terms[0][0].shape
    firsts = [block_of(right, ps[0]) for _, right in terms]
    steps = [block_of(right, ps[1])[1] - first for (_, right), (_, first) in zip(terms, firsts)]
    lanes = [array.shape[2] for array, _ in firsts]

    def kernel(*refs):
        at = 0
        for number, width in enumerate(lanes):
            left, right = refs[2 * number], refs[2 * number + 1]
            refs[-1][0, :, at : at + width] = mm(left[...], right[0], NN).astype(BF)
            at += width
        if at < wide:
            refs[-1][0, :, at:] = jnp.zeros((d, wide - at), BF)
        if extra is not None:
            for c in range(8):
                refs[-1][0, c * (d // 8) : c * (d // 8) + 16, at:] = refs[-2][0, c]

    specs, args = [], []
    for (left, _), (array, first), step, wide in zip(terms, firsts, steps, lanes):
        specs.append(full(d, n))
        specs.append(
            pl.BlockSpec((1, n, wide), lambda i, first=first, step=step: (first + step * i, 0, 0))
        )
        args += [left, array]
    wide = sum(lanes)
    if extra is not None:
        specs.append(per(8, 16, EXTRA))
        args.append(extra)
    wide += -wide % 128
    return call(
        kernel, len(ps), specs, per(d, wide), out((len(ps), d, wide), BF),
        us=4.5,
    )(*args)


def split_call(terms, got, where, write, outs, extra=None):
    d, n = terms[0][0].shape
    rows = d // 8
    count = len(terms)
    evens = [[block_of(right, p) for p in (0, 2)] for _, right in terms]
    lanes = [pair[0][0].shape[2] for pair in evens]
    wide = got.shape[2]

    def kernel(where_ref, *refs):
        got_ref = refs[3 * count]
        y = where_ref[1]

        def part(p, y_at):
            at = 0
            columns = []
            for number, width in enumerate(lanes):
                left, right = refs[3 * number], refs[3 * number + 1 + p // 2]
                lhs = left[:, y_at].reshape(4 * rows, n)
                value = mm(lhs, right[0], NN).reshape(4, rows, width)
                value = value + got_ref[p // 2, :, y_at, :, at : at + width].astype(F32)
                columns.append((at, width, value.astype(BF)))
                at += width
            if extra is not None:
                value = got_ref[p // 2, :, y_at, :, at:].astype(F32)
                top = value[:, 0:16] + refs[3 * count + 1][p // 2, :, y_at].astype(F32)
                value = jnp.concatenate([top, value[:, 16:]], axis=1)
                columns.append((at, EXTRA, value.astype(BF)))
            elif at < wide:
                columns.append((at, wide - at, jnp.zeros((4, rows, wide - at), BF)))
            return columns

        write(part, y, refs[3 * count + 1 + (extra is not None) :])

    specs, args = [SCALARS], [where]
    for (left, _), pair, width in zip(terms, evens, lanes):
        specs.append(full(4, 2, rows, n))
        args.append(left.reshape(4, 2, rows, n))
        for array, index in pair:
            specs.append(pl.BlockSpec((1, n, width), lambda i, index=index: (index, 0, 0)))
            args.append(array)
    specs.append(full(2, 4, 2, rows, wide))
    args.append(got.reshape(2, 4, 2, rows, wide))
    if extra is not None:
        specs.append(full(2, 4, 2, 16, EXTRA))
        args.append(extra.reshape(2, 4, 2, 16, EXTRA))
    shapes = [shape + (rows, wide) for shape in outs]
    return call(
        kernel, 1, specs, [full(*shape) for shape in shapes], [out(shape, BF) for shape in shapes],
        us=5.0,
    )(*args)


def grads_split(terms, got, where, extra=None):
    def write(part, y, refs):
        x_first, y_first, x_second, y_second, mine = refs
        for at, width, value in part(2, 1 - y):
            x_first[0:2, :, at : at + width] = value[0:2]
            y_first[0:2, :, at : at + width] = value[2:4]
        for at, width, value in part(2, y):
            x_first[2:4, :, at : at + width] = value[0:2]
            x_second[:, :, at : at + width] = value[2:4]
        for at, width, value in part(0, 1 - y):
            y_first[2:4, :, at : at + width] = value[2:4]
            y_second[:, :, at : at + width] = value[0:2]
        for at, width, value in part(0, y):
            mine[:, :, at : at + width] = value

    return split_call(terms, got, where, write, [(4,), (4,), (2,), (2,), (4,)], extra)


def pack_vectors(ps, qkv_sum, wide_grad, sums_one, sums_two, sizes):
    head_own, wide_own, gain_own, dp_size = sizes
    width = qkv_sum.shape[2] // 3
    stride = ps[1] - ps[0]

    def kernel(qkv_ref, wide_ref, one_ref, two_ref, out_ref, rows_ref):
        rows_ref[...] = jnp.zeros_like(rows_ref)
        rows = [
            wide_ref[0], one_ref[0:1], two_ref[0:1], one_ref[2:3], one_ref[1:2], two_ref[2:3],
            two_ref[1:2],
        ]
        for c in range(dp_size):
            for number, first in enumerate((0, 2 * width)):
                first += c * head_own
                rows_ref[c, number : number + 1, 0:head_own] = qkv_ref[0, :, first : first + head_own]
            for number, row in enumerate(rows):
                own = gain_own if number else wide_own
                at, first = 2 + 2 * number, c * own
                rows_ref[c, at : at + 1, :] = row[:, first : first + EXTRA]
                rest = own - EXTRA
                rows_ref[c, at + 1 : at + 2, 0:rest] = row[:, first + EXTRA : first + own]
        out_ref[0] = rows_ref[...].astype(BF)

    return call(
        kernel, 2,
        [
            per(1, 3 * width), pl.BlockSpec((1, 1, wide_own * dp_size), lambda i: (ps[0] + stride * i, 0, 0)),
            full(*sums_one.shape), full(*sums_two.shape),
        ],
        per(dp_size, 16, EXTRA), out((2, dp_size, 16, EXTRA), BF),
        [pltpu.VMEM((dp_size, 16, EXTRA), F32)], us=1.7,
    )(qkv_sum, wide_grad, sums_one, sums_two)


def combine(halves, rows_of, where, us):
    arrays = []
    for array in [array for half in halves for array, _ in half]:
        if not any(array is other for other in arrays):
            arrays.append(array)
    index = lambda array: [array is other for other in arrays].index(True)
    plans = [
        [(index(array), rows_of[h][0] if rows_of else first) for array, first in half]
        for h, half in enumerate(halves)
    ]
    chunk = arrays[0].shape[2:]

    def kernel(where_ref, *refs):
        o0, o1, o2, o3, total = refs[len(arrays) :]
        for h, plan in enumerate(plans):
            for j in range(2):
                number, first = plan[0]
                value = refs[number][0, first + j].astype(F32)
                for number, first in plan[1:]:
                    value = value + refs[number][0, first + j].astype(F32)
                total[2 * h + j] = value
        z = where_ref[0]
        o0[...] = total[z]
        o1[...] = total[z ^ 1].astype(BF)
        o2[...] = total[z ^ 2].astype(BF)
        o3[...] = total[z ^ 3].astype(BF)

    return call(
        kernel, 1,
        [SCALARS] + [full(1, *a.shape[1:]) for a in arrays],
        [full(*chunk)] * 4,
        [out(chunk), out(chunk, BF), out(chunk, BF), out(chunk, BF)],
        [pltpu.VMEM((4,) + chunk, F32)],
        us=us,
    )(where, *arrays)


def norm(summed):
    center = summed - jnp.mean(summed, axis=-1, keepdims=True)
    spread = jnp.mean(center * center, axis=-1, keepdims=True)
    scaled = lax.rsqrt(spread + 1e-05)
    return (center * scaled, scaled)


def norm_back(upstream, normal, scaled):
    inner_sum = (
        upstream
        - jnp.mean(upstream, axis=-1, keepdims=True)
        - normal * jnp.mean(upstream * normal, axis=-1, keepdims=True)
    )
    return scaled * inner_sum


G1, G2, BO, B1, C2, B2 = range(6)


def attn_fwd(pieces, width, small, tok, groups, key_open):
    n, d = tok.shape
    blocks = pieces.blocks
    heads = width // HEAD
    count = len(pieces.arrays)
    (head_own, wide_own, gain_own, dp_size), given = small
    units = wide_own * dp_size

    def kernel(where_ref, tok_ref, gq_ref, gk_ref, open_ref, *refs):
        w_refs, refs = refs[:count], refs[count:]
        if given is not None:
            bias_in, rows_in, wide_in = refs[:3]
            refs = refs[3:]
        qkv_ref, ctx_ref, e_ref, inv_ref, n1_ref, rstd_ref, low_ref, low_t_ref, tok_t_ref = refs[:9]
        rows_ref, wide_ref, att_ref, mask_ref, w_ref, sems = refs[9:]
        step = pl.program_id(0)

        @pl.when(step == 0)
        def _():
            pieces.start(w_refs, where_ref, w_ref, sems)
            seen = (open_ref[...] == 1) | (gq_ref[...] == gk_ref[...])
            mask_ref[...] = jnp.where(seen, 0.0, -1e30)
            att_ref[...] = jnp.zeros_like(att_ref)
            tok_t_ref[...] = tok_ref[...].T

        pieces.wait(w_refs, step, w_ref, sems)
        if given is None:
            first = 4 * width
            vectors = [
                w_ref[step, c // 2, c % 2, 0:16, first : first + 128].astype(F32)
                for c in range(dp_size)
            ]

            def line(row, used):
                return jnp.concatenate([v[row : row + 1, :used] for v in vectors], axis=1)

            bias_q, bias_v = line(0, head_own), line(1, head_own)
            wide_ref[0] = line(2, wide_own)

            @pl.when(step == 0)
            def _():
                for row in range(6):
                    rows_ref[row : row + 1] = line(3 + row, gain_own)

        else:
            bias_q, bias_v = bias_in[0, 0:1], bias_in[0, 1:2]
            wide_ref[0] = wide_in[0]
            rows_ref[0:6] = rows_in[...]

        qkv = mm(tok_ref[...], pieces.read(w_ref, step, 0, 3 * width), NN)
        lane = lax.broadcasted_iota(jnp.int32, (n, 128), 1)
        q_all = (qkv[:, :width] + bias_q).astype(BF)
        k_all = qkv[:, width : 2 * width].astype(BF)
        v_all = (qkv[:, 2 * width :] + bias_v).astype(BF)
        qkv_ref[0] = jnp.concatenate([q_all, k_all, v_all], axis=1)
        contexts = []
        inv_all = jnp.zeros((n, 128), F32)
        for h in range(heads):
            q = q_all[:, h * HEAD : (h + 1) * HEAD] * jnp.asarray(HEAD**-0.5, BF)
            k = k_all[:, h * HEAD : (h + 1) * HEAD]
            v = v_all[:, h * HEAD : (h + 1) * HEAD]
            s = mm(q, k, NT) + mask_ref[...]
            e = jnp.exp(s - jnp.max(s, axis=-1, keepdims=True)).astype(BF)
            e_ref[0, h] = e
            v_one = jnp.concatenate([v, jnp.ones_like(v)], axis=1)
            r = mm(e, v_one, NN)
            inv = 1.0 / r[:, HEAD : HEAD + 1]
            contexts.append((r[:, :HEAD] * inv).astype(BF))
            inv_all = jnp.where(lane == h, inv, inv_all)
        ctx = jnp.concatenate(contexts, axis=1)
        ctx_ref[0] = ctx
        inv_ref[0] = inv_all
        att_ref[...] += mm(ctx, pieces.read(w_ref, step, 3 * width, 4 * width), NT)

        @pl.when(step == blocks - 1)
        def _():
            summed = tok_ref[...].astype(F32) + (att_ref[...] + rows_ref[BO : BO + 1])
            normal, scaled = norm(summed)
            n1_ref[...] = normal
            rstd_ref[...] = scaled
            normed = normal * rows_ref[G1 : G1 + 1] + rows_ref[B1 : B1 + 1]
            low = normed.astype(BF)
            low_ref[...] = low
            low_t_ref[...] = low.T

    specs = [SCALARS, full(n, d), full(n, 1), full(1, n), full(1, n)] + [ANY] * count
    args = [pieces.where, tok, groups.reshape(n, 1), groups.reshape(1, n), key_open.reshape(1, n)]
    args += pieces.arrays
    if given is not None:
        biases = given[:, :, 0:2, :head_own].transpose(0, 2, 1, 3).reshape(blocks, 2, width)
        wide_low = given[:, :, 2, :wide_own].reshape(blocks, 1, units)
        specs += [per(2, width), full(6, d), per(1, units)]
        args += [
            biases, given[0, :, 3:9, :gain_own].transpose(1, 0, 2).reshape(6, d), wide_low,
        ]
    return call(
        kernel, blocks, specs,
        [
            per(n, 3 * width), per(n, width), per(heads, n, n), per(n, 128),
            full(n, d), full(n, 1), full(n, d), full(d, n), full(d, n), full(8, d), per(1, units),
        ],
        [
            out((blocks, n, 3 * width), BF), out((blocks, n, width), BF),
            out((blocks, heads, n, n), BF), out((blocks, n, 128)),
            out((n, d)), out((n, 1)), out((n, d), BF), out((d, n), BF), out((d, n), BF),
            out((8, d)), out((blocks, 1, units)),
        ],
        [pltpu.VMEM((n, d), F32), pltpu.VMEM((n, n), F32)] + pieces.scratch(),
        us=17,
    )(*args)


def ffn_up(pieces, low, wide_bias):
    n, d = low.shape
    blocks, units, count = pieces.blocks, pieces.lanes, len(pieces.arrays)

    def kernel(where_ref, low_ref, bias_ref, *refs):
        w_refs, (act_ref, slope_ref, w_ref, sems) = refs[:count], refs[count:]
        step = pl.program_id(0)

        @pl.when(step == 0)
        def _():
            pieces.start(w_refs, where_ref, w_ref, sems)

        pieces.wait(w_refs, step, w_ref, sems)
        h = mm(low_ref[...], pieces.read(w_ref, step, 0, units), NN) + bias_ref[0]
        cdf = 0.5 * (1.0 + lax.erf(h * (0.5**0.5)))
        act_ref[0] = (h * cdf).astype(BF)
        density = jnp.exp(h * h * -0.5) * 0.3989422804014327
        slope_ref[0] = (cdf + h * density).astype(BF)

    return call(
        kernel, blocks,
        [SCALARS, full(n, d), per(1, units)] + [ANY] * count,
        [per(n, units), per(n, units)],
        [out((blocks, n, units), BF), out((blocks, n, units), BF)],
        pieces.scratch(),
        us=8.5,
    )(pieces.where, low, wide_bias, *pieces.arrays)


def ffn_down(pieces, act, n1, cot, rows):
    n, d = n1.shape
    blocks, units, count = pieces.blocks, pieces.lanes, len(pieces.arrays)

    def kernel(where_ref, act_ref, n1_ref, cot_ref, rows_ref, *refs):
        w_refs, refs = refs[:count], refs[count:]
        y_ref, ds_ref, df_ref, df_t_ref, sum_ref, acc_ref, w_ref, sems = refs
        step = pl.program_id(0)

        @pl.when(step == 0)
        def _():
            pieces.start(w_refs, where_ref, w_ref, sems)
            normed = n1_ref[...] * rows_ref[G1 : G1 + 1] + rows_ref[B1 : B1 + 1]
            acc_ref[...] = normed + rows_ref[C2 : C2 + 1]

        pieces.wait(w_refs, step, w_ref, sems)
        acc_ref[...] += mm(act_ref[0], pieces.read(w_ref, step, 0, units), NT)

        @pl.when(step == blocks - 1)
        def _():
            normal, scaled = norm(acc_ref[...])
            gain = rows_ref[G2 : G2 + 1]
            y_ref[...] = (normal * gain + rows_ref[B2 : B2 + 1]).astype(BF)
            upstream = cot_ref[...].astype(F32)
            ds = norm_back(upstream * gain, normal, scaled)
            ds_ref[...] = ds
            df = ds.astype(BF)
            df_ref[...] = df
            df_t_ref[...] = df.T
            sum_ref[...] = jnp.zeros_like(sum_ref)
            sum_ref[0:1] = jnp.sum(upstream * normal, axis=0, keepdims=True)
            sum_ref[1:2] = jnp.sum(upstream, axis=0, keepdims=True)
            sum_ref[2:3] = jnp.sum(ds, axis=0, keepdims=True)

    return call(
        kernel, blocks,
        [SCALARS, per(n, units), full(n, d), full(n, d), full(*rows.shape)] + [ANY] * count,
        [full(n, d), full(n, d), full(n, d), full(d, n), full(8, d)],
        [out((n, d), BF), out((n, d)), out((n, d), BF), out((d, n), BF), out((8, d))],
        [pltpu.VMEM((n, d), F32)] + pieces.scratch(),
        us=10.5,
    )(pieces.where, act, n1, cot, rows, *pieces.arrays)


def ffn_bwd(up, down, df, slope, ds2, n1, rstd, rows):
    n, d = n1.shape
    blocks, units = up.blocks, up.lanes
    up_count, down_count = len(up.arrays), len(down.arrays)

    def kernel(where_ref, df_ref, slope_ref, ds2_ref, n1_ref, rstd_ref, rows_ref, *refs):
        up_refs, down_refs = refs[:up_count], refs[up_count : up_count + down_count]
        refs = refs[up_count + down_count :]
        dh_ref, dc_ref, ds_ref, da_ref, da_t_ref, sum_ref = refs[:6]
        acc_ref, wu_ref, sems_u, wd_ref, sems_d = refs[6:]
        step = pl.program_id(0)

        @pl.when(step == 0)
        def _():
            down.start(down_refs, where_ref, wd_ref, sems_d)
            up.start(up_refs, where_ref, wu_ref, sems_u)
            acc_ref[...] = ds2_ref[...]

        down.wait(down_refs, step, wd_ref, sems_d)
        up.wait(up_refs, step, wu_ref, sems_u)
        dact = mm(df_ref[...], down.read(wd_ref, step, 0, units), NN)
        dh = (dact * slope_ref[0].astype(F32)).astype(BF)
        dh_ref[0] = dh
        dc_ref[0] = jnp.sum(dh.astype(F32), axis=0, keepdims=True)
        acc_ref[...] += mm(dh, up.read(wu_ref, step, 0, units), NT)

        @pl.when(step == blocks - 1)
        def _():
            dnormed = acc_ref[...]
            normal = n1_ref[...]
            ds = norm_back(dnormed * rows_ref[G1 : G1 + 1], normal, rstd_ref[...])
            ds_ref[...] = ds
            da = ds.astype(BF)
            da_ref[...] = da
            da_t_ref[...] = da.T
            sum_ref[...] = jnp.zeros_like(sum_ref)
            sum_ref[0:1] = jnp.sum(dnormed * normal, axis=0, keepdims=True)
            sum_ref[1:2] = jnp.sum(dnormed, axis=0, keepdims=True)
            sum_ref[2:3] = jnp.sum(ds, axis=0, keepdims=True)

    return call(
        kernel, blocks,
        [SCALARS, full(n, d), per(n, units), full(n, d), full(n, d), full(n, 1), full(*rows.shape)]
        + [ANY] * (up_count + down_count),
        [per(n, units), per(1, units), full(n, d), full(n, d), full(d, n), full(8, d)],
        [
            out((blocks, n, units), BF), out((blocks, 1, units)), out((n, d)),
            out((n, d), BF), out((d, n), BF), out((8, d)),
        ],
        [pltpu.VMEM((n, d), F32)] + up.scratch() + down.scratch(),
        us=13.5,
    )(up.where, df, slope, ds2, n1, rstd, rows, *up.arrays, *down.arrays)


def attn_bwd(pieces, width, ps, da, qkv, ctx, e, inv, back, last):
    n, d = back.shape
    ps = list(ps)
    count = len(pieces.arrays)
    heads = width // HEAD
    stride = ps[1] - ps[0]
    at = lambda i: ps[0] + stride * i

    def kernel(where_ref, da_ref, qkv_ref, ctx_ref, e_ref, inv_ref, back_ref, *refs):
        w_refs, (dqkv_ref, sum_ref, tg_ref, acc_ref, w_ref, sems) = refs[:count], refs[count:]
        step = pl.program_id(0)

        @pl.when(step == 0)
        def _():
            pieces.start(w_refs, where_ref, w_ref, sems, ps)
            acc_ref[...] = back_ref[...]

        pieces.wait(w_refs, at(step), w_ref, sems)
        dctx = mm(da_ref[...], pieces.read(w_ref, at(step), 3 * width, 4 * width), NN)
        dctx = dctx.astype(BF).astype(F32)
        scale = HEAD**-0.5
        dqs, dks, dvs = [], [], []
        for h in range(heads):
            q = qkv_ref[0, :, h * HEAD : (h + 1) * HEAD]
            k = qkv_ref[0, :, width + h * HEAD : width + (h + 1) * HEAD]
            v = qkv_ref[0, :, 2 * width + h * HEAD : 2 * width + (h + 1) * HEAD]
            e = e_ref[0, h]
            do = dctx[:, h * HEAD : (h + 1) * HEAD] * inv_ref[0, :, h : h + 1]
            ctx = ctx_ref[0, :, h * HEAD : (h + 1) * HEAD].astype(F32)
            delta = jnp.sum(do * ctx, axis=-1, keepdims=True)
            do_low = do.astype(BF)
            dp = mm(do_low, v, NT)
            ds = (e.astype(F32) * (dp - delta)).astype(BF)
            dvs.append(mm(e, do_low, TN))
            dqs.append(mm(ds, k, NN) * scale)
            dks.append(mm(ds, q, TN) * scale)
        dqkv = jnp.concatenate(dqs + dks + dvs, axis=1).astype(BF)
        dqkv_ref[0] = dqkv
        sum_ref[0] = jnp.sum(dqkv.astype(F32), axis=0, keepdims=True)
        acc_ref[...] += mm(dqkv, pieces.read(w_ref, at(step), 0, 3 * width), NT)

        @pl.when(step == len(ps) - 1)
        def _():
            tg_ref[...] = acc_ref[...].astype(tg_ref.dtype)

    def of(*shape):
        return pl.BlockSpec((1,) + shape, lambda i: (at(i),) + (0,) * len(shape))

    return call(
        kernel, len(ps),
        [SCALARS, full(n, d), of(n, 3 * width), of(n, width), of(heads, n, n), of(n, 128), full(n, d)]
        + [ANY] * count,
        [per(n, 3 * width), per(1, 3 * width), full(n, d)],
        [
            out((len(ps), n, 3 * width), BF), out((len(ps), 1, 3 * width)),
            out((n, d), BF if last else F32),
        ],
        [pltpu.VMEM((n, d), F32)] + pieces.scratch(),
        us=14.3,
    )(pieces.where, da, qkv, ctx, e, inv, back, *pieces.arrays)


def lamb(gradient, master, first, second):
    first_new = 0.5 * first + 0.5 * gradient
    second_new = 0.5 * second + 0.5 * gradient * gradient
    update = first_new / (jnp.sqrt(second_new) + 1e-06) + 0.01 * master
    return first_new, second_new, update


def whole_sum(array):
    return jnp.sum(jnp.sum(array * array, axis=1, keepdims=True), axis=0, keepdims=True)


def chunk_sum(refs, lanes):
    total = refs[0][:, lanes[0] : lanes[1]]
    for ref in refs[1:]:
        total = total + ref[:, lanes[0] : lanes[1]].astype(F32)
    return total


def moved(source, target, buffer, sems):
    into = pltpu.make_async_copy(source, buffer, sems.at[0])
    back = pltpu.make_async_copy(buffer, target, sems.at[1])
    into.start()

    def turn():
        into.wait()
        back.start()

    return turn, back.wait


def lamb_matrices(parts, entries, carried=None):
    count = len(parts)
    extra = [] if carried is None else [carried]

    def kernel(*refs):
        part_refs = refs[:count]
        ins, refs = refs[count : count + 3 * len(entries)], refs[count + 3 * len(entries) :]
        if extra:
            turn, end = moved(refs[0], refs[1 + 3 * len(entries) + 1], refs[-2], refs[-1])
            refs = refs[1:]
        sum_ref = refs[3 * len(entries)]
        for number, (lane, turned, master, _, _) in enumerate(entries):
            m_ref, f_ref, s_ref = ins[3 * number : 3 * number + 3]
            fn_ref, sn_ref, u_ref = refs[3 * number : 3 * number + 3]
            gradient = chunk_sum(part_refs, (lane, lane + master.shape[0 if turned else 1]))
            if turned:
                gradient = gradient.T
            fn_ref[...], sn_ref[...], update = lamb(gradient, m_ref[...], f_ref[...], s_ref[...])
            u_ref[...] = update
            at = 2 * number
            sum_ref[at : at + 1] = jnp.broadcast_to(whole_sum(m_ref[...]), (1, 128))
            sum_ref[at + 1 : at + 2] = jnp.broadcast_to(whole_sum(update), (1, 128))
        if extra:
            turn()
            end()

    shapes = [entry[2].shape for entry in entries for _ in range(3)]
    args = list(parts) + [array for entry in entries for array in entry[2:]]
    specs = [full(*a.shape) for a in args] + [ANY] * len(extra)
    outs = [out(shape) for shape in shapes] + [out((8, 128))]
    out_specs = [full(*o.shape) for o in outs] + [ANY] * len(extra)
    outs += [out(a.shape, a.dtype) for a in extra]
    scratch = []
    for a in extra:
        scratch = [pltpu.VMEM(a.shape, a.dtype), pltpu.SemaphoreType.DMA((2,))]
    return call(kernel, 1, specs, out_specs, outs, scratch, us=2.6)(*args, *extra)


def lamb_last(parts, attn, small_grad, small, early, share):
    count = len(parts)
    width = attn[0].shape[2]
    shapes = [group[0].shape for group in small]

    def kernel(*refs):
        part_refs, refs = refs[:count], refs[count:]
        m_ref, f_ref, s_ref = refs[:3]
        small_refs, early_refs, refs = refs[3:15], refs[15:17], refs[17:]
        if small_grad is not None:
            small_ref, refs = refs[0], refs[1:]
        fn_ref, sn_ref, u_ref = refs[:3]
        small_out, su_ref, sum_ref, pack = refs[3:11], refs[11], refs[12], refs[13]
        row = lax.broadcasted_iota(jnp.int32, (8, 128), 0)
        lane = lax.broadcasted_iota(jnp.int32, (8, 128), 1)
        sums = jnp.zeros((8, 128), F32)

        def put(sums, index, weight_sq, update_sq):
            sums = jnp.where((row == 0) & (lane == index), weight_sq, sums)
            return jnp.where((row == 1) & (lane == index), update_sq, sums)

        for k in range(3):
            gradient = chunk_sum(part_refs, (k * width, (k + 1) * width))
            fn, sn, update = lamb(gradient, m_ref[k], f_ref[k], s_ref[k])
            fn_ref[k], sn_ref[k], u_ref[k] = fn, sn, update
            sums = put(sums, k, whole_sum(m_ref[k]), whole_sum(update))
        for index, call_index, at in ((3, 0, 2), (4, 0, 0), (5, 1, 0)):
            ref = early_refs[call_index]
            sums = put(sums, index, ref[at : at + 1, 0:1], ref[at + 1 : at + 2, 0:1])
        pack[...] = jnp.zeros_like(pack)
        at = 0
        for group in range(4):
            count_rows, lanes_used = shapes[group]
            for which in range(3):
                pack[which, at : at + count_rows, 0:lanes_used] = small_refs[3 * group + which][...]
            at += count_rows
        if small_grad is not None:
            pack[3] = small_ref[...]
        else:
            total = chunk_sum([ref.at[0:16] for ref in part_refs], (3 * width, 3 * width + EXTRA))
            pack[3, 0:2, 0:EXTRA] = total[0:2]
            for number in range(7):
                at = 2 + 2 * number
                pack[3, 2 + number : 3 + number, 0:EXTRA] = total[at : at + 1]
                pack[3, 2 + number : 3 + number, EXTRA : 2 * EXTRA] = total[at + 1 : at + 2]
        fn, sn, update = lamb(pack[3], pack[0], pack[1], pack[2])
        su_ref[...] = update
        at = 0
        for group in range(4):
            count_rows, lanes_used = shapes[group]
            small_out[2 * group][...] = fn[at : at + count_rows, 0:lanes_used]
            small_out[2 * group + 1][...] = sn[at : at + count_rows, 0:lanes_used]
            at += count_rows
        weight_rows = jnp.sum(pack[0] * pack[0], axis=1, keepdims=True)
        update_rows = jnp.sum(update * update, axis=1, keepdims=True)
        for index in range(9):
            part = 1.0 if index < 3 else share
            sums = put(
                sums, 6 + index, weight_rows[index : index + 1] * part, update_rows[index : index + 1] * part
            )
        sum_ref[...] = sums

    args = list(parts) + list(attn)
    args += [array for group in small for array in group] + list(early)
    if small_grad is not None:
        args.append(small_grad)
    outs = [out(attn[0].shape)] * 3
    outs += [out(s) for s in shapes for _ in range(2)]
    outs += [out((16, 128)), out((8, 128))]
    return call(
        kernel, 1, [full(*a.shape) for a in args], [full(*o.shape) for o in outs], outs,
        [pltpu.VMEM((4, 16, 128), F32)], us=3.1,
    )(*args)


def finish(sums, matrices, updates, small, small_update, carried):
    shapes = [a.shape for a in small]

    def kernel(*refs):
        sum_ref, refs = refs[0], refs[1:]
        m_refs, u_refs, v_refs, vu_ref = refs[:4], refs[4:8], refs[8:12], refs[12]
        turn, end = moved(refs[13], refs[23], refs[24], refs[25])
        m_outs, v_outs, norm_ref = refs[14:18], refs[18:22], refs[22]
        norms = jnp.sqrt(sum_ref[...])
        trust = 0.5 * (norms[0:1] / (norms[1:2] + 1e-06))
        norm_ref[...] = norms[0:2, 0:15]
        for k in range(3):
            m_outs[0][k] = m_refs[0][k] - trust[:, k : k + 1] * u_refs[0][k]
        for number in range(1, 4):
            at = 2 + number
            m_outs[number][...] = m_refs[number][...] - trust[:, at : at + 1] * u_refs[number][...]
        at = 0
        for group in range(4):
            count_rows, lanes_used = shapes[group]
            for r in range(count_rows):
                factor = trust[:, 6 + at : 7 + at]
                update = vu_ref[at : at + 1, 0:lanes_used]
                v_outs[group][r : r + 1] = v_refs[group][r : r + 1] - factor * update
                at += 1
        turn()
        end()

    args = [sums] + list(matrices) + list(updates) + list(small) + [small_update]
    outs = [out(a.shape) for a in matrices] + [out(s) for s in shapes] + [out((2, 15))]
    return call(
        kernel, 1,
        [full(*a.shape) for a in args] + [ANY],
        [full(*o.shape) for o in outs] + [ANY],
        outs + [out(carried.shape, carried.dtype)],
        [pltpu.VMEM(carried.shape, carried.dtype), pltpu.SemaphoreType.DMA((2,))],
        us=2.6,
    )(*args, carried)


def prepare(attn, mix, up, down_rows, small, inside):
    rows, width = attn.shape[1:]
    units = up.shape[1]
    lanes = 4 * width + (128 if inside else 0)

    def kernel(attn_ref, mix_ref, up_ref, down_ref, *refs):
        attn_out, ffn_out = refs[len(small)], refs[len(small) + 1]
        for k in range(3):
            attn_out[:, k * width : (k + 1) * width] = attn_ref[k].astype(BF)
        attn_out[:, 3 * width : 4 * width] = mix_ref[...].T.astype(BF)
        ffn_out[0:rows] = up_ref[...].astype(BF)
        ffn_out[rows : 2 * rows] = down_ref[...].astype(BF)
        if inside:
            pack = refs[len(small) + 2]
            pack[...] = jnp.zeros_like(pack)
            at = 0
            for ref in refs[: len(small)]:
                pack[at : at + ref.shape[0], 0 : ref.shape[1]] = ref[...]
                at += ref.shape[0]
            attn_out[:, 4 * width :] = pack[...].astype(BF)

    args = [attn, mix, up, down_rows] + list(small)
    outs = [out((rows, lanes), BF), out((2 * rows, units), BF)]
    return call(
        kernel, 1, [full(*a.shape) for a in args], [full(*o.shape) for o in outs], outs,
        [pltpu.VMEM((rows, 128), F32)], us=2.1,
    )(*args)


def pack_rows(arrays):
    rows = [jnp.pad(a, ((0, 0), (0, 128 - a.shape[1]))) for a in arrays]
    total = sum(a.shape[0] for a in arrays)
    rows.append(jnp.zeros((16 - total, 128), F32))
    return jnp.concatenate(rows, axis=0)


def spread_vectors(qkv_sum, wide_grad, sums_one, sums_two, sizes):
    head_own, wide_own, gain_own, dp_size = sizes
    blocks, width = qkv_sum.shape[0], qkv_sum.shape[2] // 3

    def lanes128(array, own):
        array = array.reshape(array.shape[:-1] + (dp_size, own))
        return jnp.pad(array, ((0, 0),) * (array.ndim - 1) + ((0, 128 - own),))

    vectors = jnp.stack(
        [sums_one[0], sums_two[0], sums_one[2], sums_one[1], sums_two[2], sums_two[1]]
    )
    vectors = jnp.broadcast_to(
        lanes128(vectors, gain_own).transpose(1, 0, 2)[None], (blocks, dp_size, 6, 128)
    )
    return jnp.concatenate(
        [
            lanes128(qkv_sum[:, 0, :width], head_own)[:, :, None],
            lanes128(qkv_sum[:, 0, 2 * width :], head_own)[:, :, None],
            lanes128(wide_grad[:, 0], wide_own)[:, :, None],
            vectors,
            jnp.zeros((blocks, dp_size, 7, 128), F32),
        ],
        axis=2,
    )


def on_device(
    dp_size, tensor_size,
    tokens, cotangent, row_lengths, present, groups,
    attn_weight, attn_first, attn_second,
    mix_weight, mix_first, mix_second,
    up_weight, up_first, up_second,
    down_weight, down_first, down_second,
    head_bias, head_first, head_second,
    wide_bias, wide_first, wide_second,
    norm_gains, gain_first, gain_second,
    shift_bias, shift_first, shift_second,
):
    comm = GridComm() if (dp_size, tensor_size) == (8, 4) else GenericComm(dp_size, tensor_size)
    rank = lax.axis_index("tensor")
    row_count, n = groups.shape
    assert row_count == tensor_size
    d = tokens.shape[1]
    width, units = attn_weight.shape[2], up_weight.shape[1]
    head_own, wide_own, gain_own = head_bias.shape[1], wide_bias.shape[0], norm_gains.shape[1]
    small_arrays = [
        (head_bias, head_first, head_second),
        tuple(a.reshape(1, -1) for a in (wide_bias, wide_first, wide_second)),
        (norm_gains, gain_first, gain_second),
        (shift_bias, shift_first, shift_second),
    ]

    down_rows = down_weight.T
    small_masters = [group[0] for group in small_arrays]
    small_all = None
    if not comm.small_inside:
        small_all = comm.gather_small(pack_rows(small_masters).astype(BF).astype(F32))
    attn_shard, ffn_shard = prepare(
        attn_weight, mix_weight, up_weight, down_rows, small_masters, comm.small_inside
    )
    attn_g = comm.gather(attn_shard)
    attn_g.z([])
    attn_g.xy([])
    attn_g.diagonal([])
    attn_w = attn_g.core()
    up_w, down_w = comm.gather_stacked(ffn_shard)

    tok = lax.dynamic_slice_in_dim(tokens, rank * n, n, 0)
    cot = lax.dynamic_slice_in_dim(cotangent, rank * n, n, 0)
    group_row = lax.dynamic_index_in_dim(groups, rank, 0, keepdims=False)
    present_row = lax.dynamic_index_in_dim(present, rank, 0, keepdims=False)
    length = lax.dynamic_index_in_dim(row_lengths, rank, 0, keepdims=False)
    feature_ids = jnp.arange(present_row.shape[0])
    present_key = jnp.sum(
        (group_row[:, None] == feature_ids[None, :]) * present_row[None, :], axis=1
    )
    key_open = ((jnp.arange(n) < length) & (present_key == 1)).astype(jnp.int32)

    qkv, ctx, e, inv, n1, rstd, low, low_t, tok_t, rows, wide_low = attn_fwd(
        attn_w, width, ((head_own, wide_own, gain_own, dp_size), small_all), tok, group_row, key_open
    )
    act, slope = ffn_up(up_w, low, wide_low)
    layer_out, ds2, df, df_t, sums_two = ffn_down(down_w, act, n1, cot, rows)
    layer_out_all = lax.all_gather(layer_out, "tensor", axis=0, tiled=True)

    down_red = comm.reduction([df_t])
    df = tie(df, down_red.core([act]))
    dh, wide_grad, ds1, da, da_t, sums_one = ffn_bwd(up_w, down_w, df, slope, ds2, n1, rstd, rows)
    up_red = comm.reduction([low_t, da_t])
    attn_red = comm.reduction([tok_t])
    sizes = (head_own, wide_own, gain_own, dp_size)
    small_sum = None
    down_lamb = lambda parts: lamb_matrices(
        parts, [(0, False, down_rows, down_first.T, down_second.T)], layer_out_all
    )
    up_lamb = lambda parts: lamb_matrices(
        parts,
        [
            (0, False, up_weight, up_first, up_second),
            (units, True, mix_weight, mix_first, mix_second),
        ],
    )
    if comm.small_inside:
        done = down_red.split([act], deps=[da])
        done = up_red.core([tie(dh, done), ctx])
        da = tie(da, done)
        odd, odd_sum, back = attn_bwd(attn_w, width, (1, 3), da, qkv, ctx, e, inv, ds1, False)
        done = down_red.neighbour([odd])
        done = up_red.split([dh, ctx], deps=done)
        extra = pack_vectors((1, 3), odd_sum, wide_grad, sums_one, sums_two, sizes)
        done = attn_red.core([[([1, 3], odd)]], tie(extra, done))
        da = tie(da, done)
        even, even_sum, back = attn_bwd(attn_w, width, (0, 2), da, qkv, ctx, e, inv, back, True)
        extra = pack_vectors((0, 2), even_sum, wide_grad, sums_one, sums_two, sizes)
        done = attn_red.split([[([0, 2], even)]], extra)
        done = up_red.neighbour(done)
        down_parts = down_red.last(done)
        done = attn_red.neighbour(down_red.done)
        tokens_grad_all = lax.all_gather(tie(back, done), "tensor", axis=0, tiled=True)
        up_parts = up_red.last(done)
        down_parts[1] = tie(down_parts[1], up_red.done)
        down_done = down_lamb(down_parts)
        attn_parts = attn_red.last([down_done[3]])
        up_parts[1] = tie(up_parts[1], attn_red.done)
        up_done = up_lamb(up_parts)
        attn_parts[1] = tie(attn_parts[1], [tokens_grad_all])
    else:
        blocks = range(tensor_size)
        dqkv, dqkv_sum, back = attn_bwd(attn_w, width, blocks, da, qkv, ctx, e, inv, ds1, True)
        tokens_grad_all = lax.all_gather(back, "tensor", axis=0, tiled=True)
        up_red.core([dh, ctx])
        attn_red.core([dqkv])
        down_done, up_done = down_lamb(down_red.last()), up_lamb(up_red.last())
        attn_parts = attn_red.last()
        small_sum = comm.scatter_small(
            spread_vectors(dqkv_sum, wide_grad, sums_one, sums_two, sizes)
        )

    last = lamb_last(
        attn_parts, (attn_weight, attn_first, attn_second), small_sum, small_arrays,
        (up_done[6], down_done[3]), 1.0 / tensor_size,
    )
    small_moments, small_u, sums = last[3:11], last[11], last[12]
    done = finish(
        comm.total(sums),
        (attn_weight, mix_weight, up_weight, down_rows),
        (last[2], up_done[5], up_done[2], down_done[2]),
        small_masters,
        small_u,
        tokens_grad_all,
    )
    moments = [last[0:2], up_done[3:5], up_done[0:2], down_done[0:2]]
    moments += [small_moments[2 * k : 2 * k + 2] for k in range(4)]
    result = [down_done[4], done[9]]
    for number, (first_new, second_new) in enumerate(moments):
        group = [done[number], first_new, second_new]
        if number == 3:
            group = [a.T for a in group]
        result += [a.reshape(-1) for a in group] if number == 5 else group
    return tuple(result) + (done[8],)


def solution(mesh):
    rows = P("dp", None)
    attn, mix, up = P(None, "dp", "tensor"), P("tensor", "dp"), P("dp", "tensor")
    head, wide, col = P(None, ("tensor", "dp")), P(("tensor", "dp")), P(None, "dp")
    params = tuple(spec for spec in (attn, mix, up, mix, head, wide, col, col) for _ in range(3))
    return jax.shard_map(
        functools.partial(on_device, mesh.shape["dp"], mesh.shape["tensor"]),
        mesh=mesh,
        in_specs=(rows, rows, P("dp"), rows, rows) + params,
        out_specs=(rows, rows) + params + (P(),),
        check_vma=False,
    )
```

profile of v0, /device:TPU:0, one launch (start us, length us, event | category | flops | bytes accessed | tf_op | source)
XLA Modules:
  0.0 322.9 jit_solution(7390150657332672694)
XLA Ops:
  9.6 4.1 %collective-permute-start.1 = (bf16[96,896]{1,0:T(8,128)(2,1)}, bf16[96,896]{1,0:T(8,128)(2,1)S(1)}, u32[]{:S(2)}, u32[]{:S(2)}) collective-permute-start(bf16[96,896]{1,0:T(8,128)(2,1)} %get-tuple-element.144.first_ref), channel_id=1, source_target_pairs={{0,16},{1,17},{2,18},{3,19},{4,20},{5,21},{6,22},{7,23},{8,24},{9,... | collective-permute-start | bytes 516104 | tf_op jit(solution)/shard_map/ppermute | solution.py:187
  15.9 10.7 %collective-permute-done.1.first_ref = bf16[96,896]{1,0:T(8,128)(2,1)S(1)} collective-permute-done((bf16[96,896]{1,0:T(8,128)(2,1)}, bf16[96,896]{1,0:T(8,128)(2,1)S(1)}, u32[]{:S(2)}, u32[]{:S(2)}) %collective-permute-start.1) | collective-permute-done | bytes 172064 | tf_op jit(solution)/shard_map/ppermute | solution.py:187
  35.6 5.4 %collective-permute-done.10.refs_9_ = bf16[2,96,896]{2,1,0:T(8,128)(2,1)} collective-permute-done((bf16[2,96,896]{2,1,0:T(8,128)(2,1)}, bf16[2,96,896]{2,1,0:T(8,128)(2,1)}, u32[]{:S(2)}, u32[]{:S(2)}) %collective-permute-start.10) | collective-permute-done | bytes 344096 | tf_op jit(solution)/shard_map/ppermute | solution.py:187
  47.0 9.2 %collective-permute-done.4.refs_3_ = bf16[2,96,896]{2,1,0:T(8,128)(2,1)} collective-permute-done((bf16[2,96,896]{2,1,0:T(8,128)(2,1)S(1)}, bf16[2,96,896]{2,1,0:T(8,128)(2,1)}, u32[]{:S(2)}, u32[]{:S(2)}) %collective-permute-start.4) | collective-permute-done | bytes 344096 | tf_op jit(solution)/shard_map/ppermute | solution.py:187
  60.1 6.9 %collective-permute-done.11.refs_10_ = bf16[2,96,896]{2,1,0:T(8,128)(2,1)} collective-permute-done((bf16[2,96,896]{2,1,0:T(8,128)(2,1)}, bf16[2,96,896]{2,1,0:T(8,128)(2,1)}, u32[]{:S(2)}, u32[]{:S(2)}) %collective-permute-start.11) | collective-permute-done | bytes 344096 | tf_op jit(solution)/shard_map/ppermute | solution.py:187
  73.6 17.5 %shard_map.487 = (bf16[4,512,576]{2,1,0:T(8,128)(2,1)}, bf16[4,512,192]{2,1,0:T(8,128)(2,1)}, bf16[4,3,512,512]{3,2,1,0:T(8,128)(2,1)}, f32[4,512,128]{2,1,0:T(8...) custom-call(s32[3]{0:T(128)} %pad_add_fusion.where_ref, ...), custom_call_target="tpu_custom_call" | custom-call | flops 8499999744 | bytes 1000 | tf_op jit(solution)/shard_map/pallas_call | solution.py:615
  91.2 15.5 %all-gather.4.cloned.1.call-done = bf16[6144,768]{1,0:T(8,128)(2,1)} async-done(((bf16[192,768]{1,0:T(8,128)(2,1)}), bf16[6144,768]{1,0:T(8,128)(2,1)}) %all-gather.4.cloned.1.call-update) | async-done | bytes 9437200 | tf_op jit(solution)/shard_map/all_gather | solution.py:206
  106.7 8.5 %shard_map.488 = (bf16[4,512,768]{2,1,0:T(8,128)(2,1)}, bf16[4,512,768]{2,1,0:T(8,128)(2,1)}) custom-call(s32[3]{0:T(128)} %pad_add_fusion.where_ref, bf16[512,768]{1,0:T(8,128)(2,1)} %get-tuple-element.145.low_ref, f32[4,1,768]{2,1,0:T(1,128)} %get-tuple-element.146.bias_ref, bf16[8,4,2,96,768]{4,3,2,1,0:T(8,128)(2,1)} %bitcast.45), custom_call_target="tpu_custom_call" | custom-call | flops 4249999872 | bytes 1000 | tf_op jit(solution)/shard_map/pallas_call | solution.py:651
  115.2 10.4 %shard_map.489 = (bf16[512,768]{1,0:T(8,128)(2,1)}, f32[512,768]{1,0:T(8,128)}, bf16[512,768]{1,0:T(8,128)(2,1)}, bf16[768,512]{1,0:T(8,128)(2,1)}, f32[8,768]{1,0:T(8,128)}) custom-call(s32[3]{0:T(128)} %pad_add_fusion.where_ref, bf16[4,512,768]{2,1,0:T(8,128)(2,1)} %get-tuple-element.148.act_ref.refs_1_.refs_2_, f32[512,768]{1,0:T(8,128)} %get-tuple-element.149.n1_ref, ...), custom_call_target="tpu_custom_call" | custom-call | flops 5249999872 | bytes 1000 | tf_op jit(solution)/shard_map/pallas_call | solution.py:695
  125.5 4.1 %shard_map.490 = bf16[2,768,768]{2,1,0:T(8,128)(2,1)} custom-call(bf16[768,512]{1,0:T(8,128)(2,1)} %get-tuple-element.151.refs_0_, bf16[4,512,768]{2,1,0:T(8,128)(2,1)} %get-tuple-element.148.act_ref.refs_1_.refs_2_), custom_call_target="tpu_custom_call" | custom-call | flops 2249999872 | bytes 1000 | tf_op jit(solution)/shard_map/pallas_call | solution.py:354
  129.9 13.4 %shard_map.491 = (bf16[4,512,768]{2,1,0:T(8,128)(2,1)}, f32[4,1,768]{2,1,0:T(1,128)}, f32[512,768]{1,0:T(8,128)}, bf16[512,768]{1,0:T(8,128)(2,1)}, bf16[768,512]{1,0:T(8,128)(2,1)}, /*index=5*/f32[8,768]{1,0:T(8,128)}) custom-call(s32[3]{0:T(128)} %pad_add_fusion.where_ref, bf16[512,768]{1,0:T(8,128)(2,1)} %get-tuple-element.153.df_ref, ...), custom_call_target="tpu_custom_call" | custom-call | flops 6750000128 | bytes 1000 | tf_op jit(solution)/shard_map/pallas_call | solution.py:745
  144.7 5.0 %shard_map.492 = (bf16[4,96,768]{2,1,0:T(8,128)(2,1)}, bf16[4,96,768]{2,1,0:T(8,128)(2,1)}, bf16[2,96,768]{2,1,0:T(8,128)(2,1)}, bf16[2,96,768]{2,1,0:T(8,128)(2,1)}, bf16[4,96,768]{2,1,0:T(8,128)(2,1)}) custom-call(s32[3]{0:T(128)} %pad_add_fusion.where_ref, bf16[4,2,96,512]{3,2,1,0:T(8,128)(2,1)} %bitcast.53, ...), custom_call_target="tpu_custom_call" | custom-call | flops 2500000000 | bytes 1000 | tf_op jit(solution)/shard_map/pallas_call | solution.py:406
  149.7 4.8 %shard_map.493 = bf16[2,768,1024]{2,1,0:T(8,128)(2,1)} custom-call(bf16[768,512]{1,0:T(8,128)(2,1)} %get-tuple-element.160.refs_0_, bf16[4,512,768]{2,1,0:T(8,128)(2,1)} %get-tuple-element.164.refs_1_.refs_2_, bf16[768,512]{1,0:T(8,128)(2,1)} %get-tuple-element.162.refs_2_, bf16[4,512,192]{2,1,0:T(8,128)(2,1)} %get-tuple-element.163.refs_3_.ctx_ref.refs_4_.refs_5_), custom_call_target="tpu_custom_call" | custom-call | flops 2249999872 | bytes 1000 | tf_op jit(solution)/shard_map/pallas_call | solution.py:354
  156.9 14.4 %shard_map.494 = (bf16[2,512,576]{2,1,0:T(8,128)(2,1)}, f32[2,1,576]{2,1,0:T(1,128)}, f32[512,768]{1,0:T(8,128)}) custom-call(s32[3]{0:T(128)} %pad_add_fusion.where_ref, bf16[512,768]{1,0:T(8,128)(2,1)} %get-tuple-element.187.da_ref, bf16[4,512,576]{2,1,0:T(8,128)(2,1)} %get-tuple-element.167.qkv_ref, ...), custom_call_target="tpu_custom_call" | custom-call | flops 7150000128 | bytes 1000 | tf_op jit(solution)/shard_map/pallas_call | solution.py:807
  173.1 5.1 %collective-permute-done.19.xg_ref = bf16[4,96,768]{2,1,0:T(8,128)(2,1)S(1)} collective-permute-done((bf16[4,96,768]{2,1,0:T(8,128)(2,1)}, bf16[4,96,768]{2,1,0:T(8,128)(2,1)S(1)}, u32[]{:S(2)}, u32[]{:S(2)}) %collective-permute-start.19) | collective-permute-done | bytes 589856 | tf_op jit(solution)/shard_map/ppermute | solution.py:187
  183.1 6.2 %shard_map.496 = (bf16[4,96,1024]{2,1,0:T(8,128)(2,1)}, bf16[4,96,1024]{2,1,0:T(8,128)(2,1)}, bf16[2,96,1024]{2,1,0:T(8,128)(2,1)}, bf16[2,96,1024]{2,1,0:T(8,128)(2,1)}, bf16[4,96,1024]{2,1,0:T(8,128)(2,1)}) custom-call(s32[3]{0:T(128)} %pad_add_fusion.where_ref, bf16[4,2,96,512]{3,2,1,0:T(8,128)(2,1)} %bitcast.49, ...), custom_call_target="tpu_custom_call" | custom-call | flops 2500000000 | bytes 1000 | tf_op jit(solution)/shard_map/pallas_call | solution.py:406
  189.3 4.2 %shard_map.498 = bf16[2,768,640]{2,1,0:T(8,128)(2,1)} custom-call(bf16[768,512]{1,0:T(8,128)(2,1)} %get-tuple-element.180.refs_0_, bf16[2,512,576]{2,1,0:T(8,128)(2,1)} %get-tuple-element.171.refs_1_, bf16[2,8,16,64]{3,2,1,0:T(8,128)(2,1)} %shard_map.497.refs_2_), custom_call_target="tpu_custom_call" | custom-call | flops 2249999872 | bytes 1000 | tf_op jit(solution)/shard_map/pallas_call | solution.py:354
  195.9 13.9 %shard_map.499 = (bf16[2,512,576]{2,1,0:T(8,128)(2,1)}, f32[2,1,576]{2,1,0:T(1,128)}, bf16[512,768]{1,0:T(8,128)(2,1)}) custom-call(s32[3]{0:T(128)} %pad_add_fusion.where_ref, bf16[512,768]{1,0:T(8,128)(2,1)} %get-tuple-element.187.da_ref, bf16[4,512,576]{2,1,0:T(8,128)(2,1)} %get-tuple-element.167.qkv_ref, ...), custom_call_target="tpu_custom_call" | custom-call | flops 7150000128 | bytes 1000 | tf_op jit(solution)/shard_map/pallas_call | solution.py:807
  212.9 4.8 %shard_map.501 = (bf16[4,96,640]{2,1,0:T(8,128)(2,1)}, bf16[4,96,640]{2,1,0:T(8,128)(2,1)}, bf16[2,96,640]{2,1,0:T(8,128)(2,1)}, bf16[2,96,640]{2,1,0:T(8,128)(2,1)}, bf16[4,96,640]{2,1,0:T(8,128)(2,1)}) custom-call(s32[3]{0:T(128)} %pad_add_fusion.where_ref, bf16[4,2,96,512]{3,2,1,0:T(8,128)(2,1)} %bitcast.82, ...), custom_call_target="tpu_custom_call" | custom-call | flops 2500000000 | bytes 1000 | tf_op jit(solution)/shard_map/pallas_call | solution.py:406
  225.0 12.9 %collective-permute-done.24 = bf16[2,96,768]{2,1,0:T(8,128)(2,1)S(1)} collective-permute-done((bf16[2,96,768]{2,1,0:T(8,128)(2,1)S(1)}, bf16[2,96,768]{2,1,0:T(8,128)(2,1)S(1)}, u32[]{:S(2)}, u32[]{:S(2)}) %collective-permute-start.24) | collective-permute-done | bytes 294944 | tf_op jit(solution)/shard_map/ppermute | solution.py:187
  256.1 5.8 %collective-permute-done.30 = bf16[2,96,1024]{2,1,0:T(8,128)(2,1)S(1)} collective-permute-done((bf16[2,96,1024]{2,1,0:T(8,128)(2,1)S(1)}, bf16[2,96,1024]{2,1,0:T(8,128)(2,1)S(1)}, u32[]{:S(2)}, u32[]{:S(2)}) %collective-permute-start.30) | collective-permute-done | bytes 393248 | tf_op jit(solution)/shard_map/ppermute | solution.py:187
  268.0 4.0 %collective-permute-start.40 = (bf16[96,1024]{1,0:T(8,128)(2,1)}, bf16[96,1024]{1,0:T(8,128)(2,1)S(1)}, u32[]{:S(2)}, u32[]{:S(2)}) collective-permute-start(bf16[96,1024]{1,0:T(8,128)(2,1)} %get-tuple-element.227), channel_id=1, source_target_pairs={{0,24},{1,25},{2,26},{3,27},{4,28},{5,29},{6,30},{7,31},{8,16},{9,... | collective-permute-start | bytes 589832 | tf_op jit(solution)/shard_map/ppermute | solution.py:187
  272.1 6.0 %shard_map.506 = (f32[96,768]{1,0:T(8,128)}, f32[96,768]{1,0:T(8,128)}, f32[96,768]{1,0:T(8,128)}, f32[8,128]{1,0:T(8,128)}, bf16[2048,768]{1,0:T(8,128)(2,1)}) custom-call(f32[96,768]{1,0:T(8,128)} %get-tuple-element.199.refs_0_, bf16[96,768]{1,0:T(8,128)(2,1)} %copy-done.39, bf16[96,768]{1,0:T(8,128)(2,1)} %copy-done.40, bf16[96,768]{1,0:T(8,128)(2,1)} %copy-done.41, ...), custom_call_target="tpu_custom_call" | custom-call | flops 1300000000 | bytes 1000 | tf_op jit(solution)/shard_map/pallas_call | solution.py:886
  310.3 6.1 %shard_map.510 = (f32[3,96,192]{2,1,0:T(8,128)}, f32[192,96]{1,0:T(8,128)}, f32[96,768]{1,0:T(8,128)}, f32[96,768]{1,0:T(8,128)}, f32[2,24]{1,0:T(2,128)}, /*ind...) custom-call(f32[8,128]{1,0:T(8,128)} %add_add_fusion.refs_0_, ...), custom_call_target="tpu_custom_call" | custom-call | flops 1300000000 | bytes 1000 | tf_op jit(solution)/shard_map/pallas_call | solution.py:993
  (214 shorter events, 109.7 us)
Async XLA Ops:
  7.2 99.4 %all-gather.4.cloned.1.call-start = ((), (), s32[]{:S(2)}) async-start(), calls=%async_computation | async-start | bytes 9732096 | tf_op jit(solution)/shard_map/all_gather | solution.py:206
  9.5 262.5 %all-gather.6.cloned.1.call-start = ((), (), s32[]{:S(2)}) async-start(), calls=%async_computation.1 | async-start | bytes 3932160 | tf_op jit(solution)/shard_map/all_gather | solution.py:1122
  9.6 16.9 %collective-permute-start.1 = (bf16[96,896]{1,0:T(8,128)(2,1)}, bf16[96,896]{1,0:T(8,128)(2,1)S(1)}, u32[]{:S(2)}, u32[]{:S(2)}) collective-permute-start(bf16[96,896]{1,0:T(8,128)(2,1)} %get-tuple-element.144.first_ref), channel_id=1, source_target_pairs={{0,16},{1,17},{2,18},{3,19},{4,20},{5,21},{6,22},{7,23},{8,24},{9,... | collective-permute-start | bytes 516104 | tf_op jit(solution)/shard_map/ppermute | solution.py:187
  34.9 21.4 %collective-permute-start.4 = (bf16[2,96,896]{2,1,0:T(8,128)(2,1)S(1)}, bf16[2,96,896]{2,1,0:T(8,128)(2,1)}, u32[]{:S(2)}, u32[]{:S(2)}) collective-permute-start(bf16[2,96,896]{2,1,0:T(8,128)(2,1)S(1)} %copy-done.19), channel_id=1, source_target_pairs={{0,4},{1,5},{2,6},{3,7},{4,0},{5,1},{6,2},{7,3},{8,12},{9,13},{10,... | collective-permute-start | bytes 1032200 | tf_op jit(solution)/shard_map/ppermute | solution.py:187
  35.3 20.9 %collective-permute-start.9 = (bf16[2,96,896]{2,1,0:T(8,128)(2,1)}, bf16[2,96,896]{2,1,0:T(8,128)(2,1)}, u32[]{:S(2)}, u32[]{:S(2)}) collective-permute-start(bf16[2,96,896]{2,1,0:T(8,128)(2,1)} %shard_map.485.refs_0_), channel_id=1, source_target_pairs={{0,2},{1,3},{2,0},{3,1},{4,6},{5,7},{6,4},{7,5},{8,10},{9,11},{10,... | collective-permute-start | bytes 1032200 | tf_op jit(solution)/shard_map/ppermute | solution.py:187
  35.5 23.1 %collective-permute-start.6 = (bf16[2,96,896]{2,1,0:T(8,128)(2,1)S(1)}, bf16[2,96,896]{2,1,0:T(8,128)(2,1)}, u32[]{:S(2)}, u32[]{:S(2)}) collective-permute-start(bf16[2,96,896]{2,1,0:T(8,128)(2,1)S(1)} %copy-done.19), channel_id=1, source_target_pairs={{0,1},{1,0},{2,3},{3,2},{4,5},{5,4},{6,7},{7,6},{8,9},{9,8},{10,11... | collective-permute-start | bytes 1032200 | tf_op jit(solution)/shard_map/ppermute | solution.py:187
  41.0 18.1 %collective-permute-start.5 = (bf16[2,96,896]{2,1,0:T(8,128)(2,1)}, bf16[2,96,896]{2,1,0:T(8,128)(2,1)}, u32[]{:S(2)}, u32[]{:S(2)}) collective-permute-start(bf16[2,96,896]{2,1,0:T(8,128)(2,1)} %shard_map.485.refs_0_), channel_id=1, source_target_pairs={{0,1},{1,0},{2,3},{3,2},{4,5},{5,4},{6,7},{7,6},{8,9},{9,8},{10,11... | collective-permute-start | bytes 1032200 | tf_op jit(solution)/shard_map/ppermute | solution.py:187
  154.5 26.9 %collective-permute-start.18 = (bf16[2,768,1024]{2,1,0:T(8,128)(2,1)}, bf16[2,768,1024]{2,1,0:T(8,128)(2,1)S(1)}, u32[]{:S(2)}, u32[]{:S(2)}) collective-permute-start(bf16[2,768,1024]{2,1,0:T(8,128)(2,1)} %shard_map.493), channel_id=1, source_target_pairs={{0,1},{1,0},{2,3},{3,2},{4,5},{5,4},{6,7},{7,6},{8,9},{9,8},{10,11... | collective-permute-start | bytes 9437192 | tf_op jit(solution)/shard_map/ppermute | solution.py:187
  154.8 135.4 %all-gather.8.cloned.1.call-start = ((), (), s32[]{:S(2)}) async-start(), calls=%async_computation.2 | async-start | bytes 3932160 | tf_op jit(solution)/shard_map/all_gather | solution.py:1157
  154.8 23.4 %collective-permute-start.19 = (bf16[4,96,768]{2,1,0:T(8,128)(2,1)}, bf16[4,96,768]{2,1,0:T(8,128)(2,1)S(1)}, u32[]{:S(2)}, u32[]{:S(2)}) collective-permute-start(bf16[4,96,768]{2,1,0:T(8,128)(2,1)} %get-tuple-element.174), channel_id=1, source_target_pairs={{0,2},{1,3},{2,0},{3,1},{4,6},{5,7},{6,4},{7,5},{8,10},{9,11},{10,... | collective-permute-start | bytes 1769480 | tf_op jit(solution)/shard_map/ppermute | solution.py:187
  156.3 21.9 %collective-permute-start.20 = (bf16[4,96,768]{2,1,0:T(8,128)(2,1)}, bf16[4,96,768]{2,1,0:T(8,128)(2,1)S(1)}, u32[]{:S(2)}, u32[]{:S(2)}) collective-permute-start(bf16[4,96,768]{2,1,0:T(8,128)(2,1)} %get-tuple-element.175), channel_id=1, source_target_pairs={{0,4},{1,5},{2,6},{3,7},{4,0},{5,1},{6,2},{7,3},{8,12},{9,13},{10,... | collective-permute-start | bytes 1769480 | tf_op jit(solution)/shard_map/ppermute | solution.py:187
  193.5 18.1 %collective-permute-start.21 = (bf16[2,768,640]{2,1,0:T(8,128)(2,1)}, bf16[2,768,640]{2,1,0:T(8,128)(2,1)S(1)}, u32[]{:S(2)}, u32[]{:S(2)}) collective-permute-start(bf16[2,768,640]{2,1,0:T(8,128)(2,1)} %shard_map.498), channel_id=1, source_target_pairs={{0,1},{1,0},{2,3},{3,2},{4,5},{5,4},{6,7},{7,6},{8,9},{9,8},{10,11... | collective-permute-start | bytes 5898248 | tf_op jit(solution)/shard_map/ppermute | solution.py:187
  193.5 27.3 %collective-permute-start.22 = (bf16[4,96,1024]{2,1,0:T(8,128)(2,1)S(1)}, bf16[4,96,1024]{2,1,0:T(8,128)(2,1)S(1)}, u32[]{:S(2)}, u32[]{:S(2)}) collective-permute-start(bf16[4,96,1024]{2,1,0:T(8,128)(2,1)S(1)} %copy-done.10), channel_id=1, source_target_pairs={{0,2},{1,3},{2,0},{3,1},{4,6},{5,7},{6,4},{7,5},{8,10},{9,11},{10,... | collective-permute-start | bytes 2359304 | tf_op jit(solution)/shard_map/ppermute | solution.py:187
  195.9 26.0 %collective-permute-start.23 = (bf16[4,96,1024]{2,1,0:T(8,128)(2,1)S(1)}, bf16[4,96,1024]{2,1,0:T(8,128)(2,1)S(1)}, u32[]{:S(2)}, u32[]{:S(2)}) collective-permute-start(bf16[4,96,1024]{2,1,0:T(8,128)(2,1)S(1)} %copy-done.9), channel_id=1, source_target_pairs={{0,4},{1,5},{2,6},{3,7},{4,0},{5,1},{6,2},{7,3},{8,12},{9,13},{10,... | collective-permute-start | bytes 2359304 | tf_op jit(solution)/shard_map/ppermute | solution.py:187
  217.7 23.8 %collective-permute-start.27 = (bf16[4,96,640]{2,1,0:T(8,128)(2,1)}, bf16[4,96,640]{2,1,0:T(8,128)(2,1)S(1)}, u32[]{:S(2)}, u32[]{:S(2)}) collective-permute-start(bf16[4,96,640]{2,1,0:T(8,128)(2,1)} %get-tuple-element.204), channel_id=1, source_target_pairs={{0,2},{1,3},{2,0},{3,1},{4,6},{5,7},{6,4},{7,5},{8,10},{9,11},{10,... | collective-permute-start | bytes 1474568 | tf_op jit(solution)/shard_map/ppermute | solution.py:187
  218.7 22.9 %collective-permute-start.28 = (bf16[4,96,640]{2,1,0:T(8,128)(2,1)}, bf16[4,96,640]{2,1,0:T(8,128)(2,1)S(1)}, u32[]{:S(2)}, u32[]{:S(2)}) collective-permute-start(bf16[4,96,640]{2,1,0:T(8,128)(2,1)} %get-tuple-element.205), channel_id=1, source_target_pairs={{0,4},{1,5},{2,6},{3,7},{4,0},{5,1},{6,2},{7,3},{8,12},{9,13},{10,... | collective-permute-start | bytes 1474568 | tf_op jit(solution)/shard_map/ppermute | solution.py:187
  219.8 18.2 %collective-permute-start.24 = (bf16[2,96,768]{2,1,0:T(8,128)(2,1)S(1)}, bf16[2,96,768]{2,1,0:T(8,128)(2,1)S(1)}, u32[]{:S(2)}, u32[]{:S(2)}) collective-permute-start(bf16[2,96,768]{2,1,0:T(8,128)(2,1)S(1)} %copy-done.26), channel_id=1, source_target_pairs={{0,4},{1,5},{2,6},{3,7},{4,0},{5,1},{6,2},{7,3},{8,12},{9,13},{10,... | collective-permute-start | bytes 884744 | tf_op jit(solution)/shard_map/ppermute | solution.py:187
  220.7 17.2 %collective-permute-start.25 = (bf16[2,96,768]{2,1,0:T(8,128)(2,1)S(1)}, bf16[2,96,768]{2,1,0:T(8,128)(2,1)S(1)}, u32[]{:S(2)}, u32[]{:S(2)}) collective-permute-start(bf16[2,96,768]{2,1,0:T(8,128)(2,1)S(1)} %copy-done.25), channel_id=1, source_target_pairs={{0,2},{1,3},{2,0},{3,1},{4,6},{5,7},{6,4},{7,5},{8,10},{9,11},{10,... | collective-permute-start | bytes 884744 | tf_op jit(solution)/shard_map/ppermute | solution.py:187
  247.8 19.8 %collective-permute-start.26 = (bf16[96,768]{1,0:T(8,128)(2,1)S(1)}, bf16[96,768]{1,0:T(8,128)(2,1)S(1)}, u32[]{:S(2)}, u32[]{:S(2)}) collective-permute-start(bf16[96,768]{1,0:T(8,128)(2,1)S(1)} %copy-done.38), channel_id=1, source_target_pairs={{0,8},{1,9},{2,10},{3,11},{4,12},{5,13},{6,14},{7,15},{8,0},{9,1},... | collective-permute-start | bytes 442376 | tf_op jit(solution)/shard_map/ppermute | solution.py:187
  248.9 19.1 %collective-permute-start.31 = (bf16[96,768]{1,0:T(8,128)(2,1)S(1)}, bf16[96,768]{1,0:T(8,128)(2,1)S(1)}, u32[]{:S(2)}, u32[]{:S(2)}) collective-permute-start(bf16[96,768]{1,0:T(8,128)(2,1)S(1)} %copy-done.37), channel_id=1, source_target_pairs={{0,16},{1,17},{2,18},{3,19},{4,20},{5,21},{6,22},{7,23},{8,24},{9,... | collective-permute-start | bytes 442376 | tf_op jit(solution)/shard_map/ppermute | solution.py:187
  249.0 19.0 %collective-permute-start.32 = (bf16[96,768]{1,0:T(8,128)(2,1)S(1)}, bf16[96,768]{1,0:T(8,128)(2,1)S(1)}, u32[]{:S(2)}, u32[]{:S(2)}) collective-permute-start(bf16[96,768]{1,0:T(8,128)(2,1)S(1)} %copy-done.36), channel_id=1, source_target_pairs={{0,24},{1,25},{2,26},{3,27},{4,28},{5,29},{6,30},{7,31},{8,16},{9,... | collective-permute-start | bytes 442376 | tf_op jit(solution)/shard_map/ppermute | solution.py:187
  254.5 23.6 %collective-permute-start.33 = (bf16[2,96,640]{2,1,0:T(8,128)(2,1)}, bf16[2,96,640]{2,1,0:T(8,128)(2,1)S(1)}, u32[]{:S(2)}, u32[]{:S(2)}) collective-permute-start(bf16[2,96,640]{2,1,0:T(8,128)(2,1)} %get-tuple-element.207), channel_id=1, source_target_pairs={{0,4},{1,5},{2,6},{3,7},{4,0},{5,1},{6,2},{7,3},{8,12},{9,13},{10,... | collective-permute-start | bytes 737288 | tf_op jit(solution)/shard_map/ppermute | solution.py:187
  268.0 17.8 %collective-permute-start.39 = (bf16[96,1024]{1,0:T(8,128)(2,1)}, bf16[96,1024]{1,0:T(8,128)(2,1)S(1)}, u32[]{:S(2)}, u32[]{:S(2)}) collective-permute-start(bf16[96,1024]{1,0:T(8,128)(2,1)} %get-tuple-element.226), channel_id=1, source_target_pairs={{0,16},{1,17},{2,18},{3,19},{4,20},{5,21},{6,22},{7,23},{8,24},{9,... | collective-permute-start | bytes 589832 | tf_op jit(solution)/shard_map/ppermute | solution.py:187
  268.0 17.8 %collective-permute-start.40 = (bf16[96,1024]{1,0:T(8,128)(2,1)}, bf16[96,1024]{1,0:T(8,128)(2,1)S(1)}, u32[]{:S(2)}, u32[]{:S(2)}) collective-permute-start(bf16[96,1024]{1,0:T(8,128)(2,1)} %get-tuple-element.227), channel_id=1, source_target_pairs={{0,24},{1,25},{2,26},{3,27},{4,28},{5,29},{6,30},{7,31},{8,16},{9,... | collective-permute-start | bytes 589832 | tf_op jit(solution)/shard_map/ppermute | solution.py:187
  (73 other events, 554.2 us)
Sparse Core Ops, SparseCore 0:
  11.5 95.0 all-gather.3
  154.9 34.0 all-gather.5
  244.8 34.7 all-gather.7
where the time goes:
time: 324 us; the launch traced here: 323 us
  Pallas kernels  149 us (46%)
  waiting for transfers between devices  85.5 us (26%)
  starting transfers between devices  51.4 us (16%)
  local copies, waits for them, and re-layouts  19.1 us (6%)
  between operations  14.2 us (4%)
    ppermute x48, waiting for transfers between devices, send(): return lax.ppermute(array, ('dp', 'tensor'), pairs)  69.9 us
    ppermute x48, starting transfers between devices, send(): return lax.ppermute(array, ('dp', 'tensor'), pairs)  51.3 us
    pallas_call x2, Pallas kernels, attn_bwd(): call(kernel, len(ps), [SCALARS, full(n, d), of(n, 3 * width), of(n, width...  28.4 us
    pallas_call x1, Pallas kernels, attn_fwd(): call(kernel, blocks, specs, [per(n, 3 * width), per(n, width), per(heads,...  17.5 us
    pallas_call x3, Pallas kernels, split_call(): call(kernel, 1, specs, [full(*shape) for shape in shapes], [out(shape, BF...  15.9 us
    all_gather x1, waiting for transfers between devices, gather_stacked(): everything = lax.all_gather(shard, ('dp', 'tensor'), axis=0, tiled=True)  15.5 us
    unnamed x92, local copies, waits for them, and re-layouts  13.9 us
    pallas_call x1, Pallas kernels, ffn_bwd(): call(kernel, blocks, [SCALARS, full(n, d), per(n, units), full(n, d), ful...  13.4 us
  transfers between devices with their start and end apart: 51, of which 18 were waited for; matrix products, arithmetic and copies ran while one was open for 2% of the time, Pallas kernels for 33%

commit v1 on v0

--- a/solution.py
+++ b/solution.py
@@ -159,7 +159,7 @@
     def __init__(self, comm, lefts):
         self.comm, self.lefts = comm, lefts
 
-    def core(self, rights, extra=None):
+    def core(self, rights):
         self.rights = rights
         return []
 
@@ -256,8 +256,10 @@
     def __init__(self, comm, lefts):
         self.comm, self.lefts = comm, lefts
 
-    def core(self, rights, extra=None):
-        odd = grads(list(zip(self.lefts, rights)), (1, 3), extra)
+    def core(self, rights):
+        return self.send_odd(grads(list(zip(self.lefts, rights)), (1, 3)))
+
+    def send_odd(self, odd):
         self.core_got = self.comm.send_core(odd)
         return [odd]
 
@@ -268,14 +270,14 @@
         self.x_got, self.y_got = self.comm.send_x(x_first), self.comm.send_y(y_first)
         return [self.mine]
 
-    def neighbour(self, deps=()):
+    def neighbour(self, deps=(), us=0.01):
         x_second, y_second = add_low(
-            tie(self.x_second, deps), self.y_second, self.x_got, self.y_got
+            tie(self.x_second, deps), self.y_second, self.x_got, self.y_got, us
         )
         self.x_got2, self.y_got2 = self.comm.send_x(x_second), self.comm.send_y(y_second)
         return [x_second, y_second]
 
-    def last(self, deps=(), us=2.8):
+    def last(self, deps=(), us=0.01):
         mine = tie(self.mine, deps)[None]
         low = [(mine, 0), (self.x_got[None], 2), (self.y_got2[None], 0)]
         high = [(mine, 2), (self.y_got[None], 2), (self.x_got2[None], 0)]
@@ -298,7 +300,7 @@
     )(where, first, second)
 
 
-def add_low(x_second, y_second, x_got, y_got):
+def add_low(x_second, y_second, x_got, y_got, us):
     half = x_second.shape
 
     def kernel(x_ref, y_ref, xg_ref, yg_ref, xo_ref, yo_ref):
@@ -307,7 +309,7 @@
 
     return call(
         kernel, 1, [full(*half)] * 4, [full(*half)] * 2, [out(half, BF), out(half, BF)],
-        us=2.0,
+        us=us,
     )(x_second, y_second, x_got, y_got)
 
 
@@ -320,7 +322,7 @@
     raise KeyError(p)
 
 
-def grads(terms, ps, extra=None):
+def grads(terms, ps):
     ps = list(ps)
     d, n = terms[0][0].shape
     firsts = [block_of(right, ps[0]) for _, right in terms]
@@ -335,9 +337,6 @@
             at += width
         if at < wide:
             refs[-1][0, :, at:] = jnp.zeros((d, wide - at), BF)
-        if extra is not None:
-            for c in range(8):
-                refs[-1][0, c * (d // 8) : c * (d // 8) + 16, at:] = refs[-2][0, c]
 
     specs, args = [], []
     for (left, _), (array, first), step, wide in zip(terms, firsts, steps, lanes):
@@ -347,13 +346,10 @@
         )
         args += [left, array]
     wide = sum(lanes)
-    if extra is not None:
-        specs.append(per(8, 16, EXTRA))
-        args.append(extra)
     wide += -wide % 128
     return call(
         kernel, len(ps), specs, per(d, wide), out((len(ps), d, wide), BF),
-        us=4.5,
+        us=0.01,
     )(*args)
 
 
@@ -405,7 +401,7 @@
     shapes = [shape + (rows, wide) for shape in outs]
     return call(
         kernel, 1, specs, [full(*shape) for shape in shapes], [out(shape, BF) for shape in shapes],
-        us=5.0,
+        us=0.01,
     )(*args)
 
 
@@ -425,40 +421,6 @@
             mine[:, :, at : at + width] = value
 
     return split_call(terms, got, where, write, [(4,), (4,), (2,), (2,), (4,)], extra)
-
-
-def pack_vectors(ps, qkv_sum, wide_grad, sums_one, sums_two, sizes):
-    head_own, wide_own, gain_own, dp_size = sizes
-    width = qkv_sum.shape[2] // 3
-    stride = ps[1] - ps[0]
-
-    def kernel(qkv_ref, wide_ref, one_ref, two_ref, out_ref, rows_ref):
-        rows_ref[...] = jnp.zeros_like(rows_ref)
-        rows = [
-            wide_ref[0], one_ref[0:1], two_ref[0:1], one_ref[2:3], one_ref[1:2], two_ref[2:3],
-            two_ref[1:2],
-        ]
-        for c in range(dp_size):
-            for number, first in enumerate((0, 2 * width)):
-                first += c * head_own
-                rows_ref[c, number : number + 1, 0:head_own] = qkv_ref[0, :, first : first + head_own]
-            for number, row in enumerate(rows):
-                own = gain_own if number else wide_own
-                at, first = 2 + 2 * number, c * own
-                rows_ref[c, at : at + 1, :] = row[:, first : first + EXTRA]
-                rest = own - EXTRA
-                rows_ref[c, at + 1 : at + 2, 0:rest] = row[:, first + EXTRA : first + own]
-        out_ref[0] = rows_ref[...].astype(BF)
-
-    return call(
-        kernel, 2,
-        [
-            per(1, 3 * width), pl.BlockSpec((1, 1, wide_own * dp_size), lambda i: (ps[0] + stride * i, 0, 0)),
-            full(*sums_one.shape), full(*sums_two.shape),
-        ],
-        per(dp_size, 16, EXTRA), out((2, dp_size, 16, EXTRA), BF),
-        [pltpu.VMEM((dp_size, 16, EXTRA), F32)], us=1.7,
-    )(qkv_sum, wide_grad, sums_one, sums_two)
 
 
 def combine(halves, rows_of, where, us):
@@ -702,14 +664,22 @@
     )(pieces.where, act, n1, cot, rows, *pieces.arrays)
 
 
-def ffn_bwd(up, down, df, slope, ds2, n1, rstd, rows):
+def ffn_bwd(up, down, df, slope, ds2, n1, rstd, rows, odd=None):
     n, d = n1.shape
     blocks, units = up.blocks, up.lanes
     up_count, down_count = len(up.arrays), len(down.arrays)
+    wide = 0
+    if odd is not None:
+        width = odd[1].shape[2]
+        wide = units + width + -(units + width) % 128
 
     def kernel(where_ref, df_ref, slope_ref, ds2_ref, n1_ref, rstd_ref, rows_ref, *refs):
+        if odd is not None:
+            low_t_ref, ctx_ref, refs = refs[0], refs[1], refs[2:]
         up_refs, down_refs = refs[:up_count], refs[up_count : up_count + down_count]
         refs = refs[up_count + down_count :]
+        if odd is not None:
+            odd_ref, refs = refs[0], refs[1:]
         dh_ref, dc_ref, ds_ref, da_ref, da_t_ref, sum_ref = refs[:6]
         acc_ref, wu_ref, sems_u, wd_ref, sems_d = refs[6:]
         step = pl.program_id(0)
@@ -721,12 +691,17 @@
             acc_ref[...] = ds2_ref[...]
 
         down.wait(down_refs, step, wd_ref, sems_d)
-        up.wait(up_refs, step, wu_ref, sems_u)
         dact = mm(df_ref[...], down.read(wd_ref, step, 0, units), NN)
         dh = (dact * slope_ref[0].astype(F32)).astype(BF)
         dh_ref[0] = dh
         dc_ref[0] = jnp.sum(dh.astype(F32), axis=0, keepdims=True)
+        up.wait(up_refs, step, wu_ref, sems_u)
         acc_ref[...] += mm(dh, up.read(wu_ref, step, 0, units), NT)
+        if odd is not None:
+
+            @pl.when(step % 2 == 1)
+            def _():
+                odd_ref[step // 2, :, 0:units] = mm(low_t_ref[...], dh, NN).astype(BF)
 
         @pl.when(step == blocks - 1)
         def _():
@@ -736,27 +711,57 @@
             ds_ref[...] = ds
             da = ds.astype(BF)
             da_ref[...] = da
-            da_t_ref[...] = da.T
+            da_t = da.T
+            da_t_ref[...] = da_t
             sum_ref[...] = jnp.zeros_like(sum_ref)
             sum_ref[0:1] = jnp.sum(dnormed * normal, axis=0, keepdims=True)
             sum_ref[1:2] = jnp.sum(dnormed, axis=0, keepdims=True)
             sum_ref[2:3] = jnp.sum(ds, axis=0, keepdims=True)
-
+            if odd is not None:
+                for k in range(2):
+                    part = mm(da_t, ctx_ref[2 * k + 1], NN).astype(BF)
+                    odd_ref[k, :, units : units + width] = part
+                    odd_ref[k, :, units + width :] = jnp.zeros((d, wide - units - width), BF)
+
+    specs = [SCALARS, full(n, d), per(n, units), full(n, d), full(n, d), full(n, 1), full(*rows.shape)]
+    args = [up.where, df, slope, ds2, n1, rstd, rows]
+    outs = [
+        out((blocks, n, units), BF), out((blocks, 1, units)), out((n, d)),
+        out((n, d), BF), out((d, n), BF), out((8, d)),
+    ]
+    out_specs = [per(n, units), per(1, units), full(n, d), full(n, d), full(d, n), full(8, d)]
+    if odd is not None:
+        specs += [full(*a.shape) for a in odd]
+        args += list(odd)
+        outs = [out((2, d, wide), BF)] + outs
+        out_specs = [full(2, d, wide)] + out_specs
     return call(
-        kernel, blocks,
-        [SCALARS, full(n, d), per(n, units), full(n, d), full(n, d), full(n, 1), full(*rows.shape)]
-        + [ANY] * (up_count + down_count),
-        [per(n, units), per(1, units), full(n, d), full(n, d), full(d, n), full(8, d)],
-        [
-            out((blocks, n, units), BF), out((blocks, 1, units)), out((n, d)),
-            out((n, d), BF), out((d, n), BF), out((8, d)),
-        ],
+        kernel, blocks, specs + [ANY] * (up_count + down_count), out_specs, outs,
         [pltpu.VMEM((n, d), F32)] + up.scratch() + down.scratch(),
-        us=13.5,
-    )(up.where, df, slope, ds2, n1, rstd, rows, *up.arrays, *down.arrays)
-
-
-def attn_bwd(pieces, width, ps, da, qkv, ctx, e, inv, back, last):
+        us=100,
+    )(*args, *up.arrays, *down.arrays)
+
+
+def fill_rows(rows_ref, qkv_sum, wide_row, one_ref, two_ref, sizes):
+    head_own, wide_own, gain_own, dp_size = sizes
+    width = qkv_sum.shape[1] // 3
+    rows_ref[...] = jnp.zeros_like(rows_ref)
+    rows = [
+        wide_row, one_ref[0:1], two_ref[0:1], one_ref[2:3], one_ref[1:2], two_ref[2:3], two_ref[1:2],
+    ]
+    for c in range(dp_size):
+        for number, first in enumerate((0, 2 * width)):
+            first += c * head_own
+            rows_ref[c, number : number + 1, 0:head_own] = qkv_sum[:, first : first + head_own]
+        for number, row in enumerate(rows):
+            own = gain_own if number else wide_own
+            at, first = 2 + 2 * number, c * own
+            rows_ref[c, at : at + 1, :] = row[:, first : first + EXTRA]
+            rest = own - EXTRA
+            rows_ref[c, at + 1 : at + 2, 0:rest] = row[:, first + EXTRA : first + own]
+
+
+def attn_bwd(pieces, width, ps, da, qkv, ctx, e, inv, back, last, vectors=None, tok_t=None):
     n, d = back.shape
     ps = list(ps)
     count = len(pieces.arrays)
@@ -765,7 +770,14 @@
     at = lambda i: ps[0] + stride * i
 
     def kernel(where_ref, da_ref, qkv_ref, ctx_ref, e_ref, inv_ref, back_ref, *refs):
-        w_refs, (dqkv_ref, sum_ref, tg_ref, acc_ref, w_ref, sems) = refs[:count], refs[count:]
+        if vectors is not None:
+            wide_ref, one_ref, two_ref, refs = refs[0], refs[1], refs[2], refs[3:]
+        if tok_t is not None:
+            tok_t_ref, refs = refs[0], refs[1:]
+        w_refs, refs = refs[:count], refs[count:]
+        if vectors is not None:
+            first_ref, rows_ref, refs = refs[0], refs[-1], refs[1:-1]
+        dqkv_ref, sum_ref, tg_ref, acc_ref, w_ref, sems = refs
         step = pl.program_id(0)
 
         @pl.when(step == 0)
@@ -777,25 +789,42 @@
         dctx = mm(da_ref[...], pieces.read(w_ref, at(step), 3 * width, 4 * width), NN)
         dctx = dctx.astype(BF).astype(F32)
         scale = HEAD**-0.5
+        dos, deltas = [], []
+        for h in range(heads):
+            do = dctx[:, h * HEAD : (h + 1) * HEAD] * inv_ref[0, :, h : h + 1]
+            ctx = ctx_ref[0, :, h * HEAD : (h + 1) * HEAD].astype(F32)
+            deltas.append(jnp.sum(do * ctx, axis=-1, keepdims=True))
+            dos.append(do.astype(BF))
+        do_t = jnp.concatenate(dos, axis=1).T
+        q_t = qkv_ref[0, :, 0:width].T
         dqs, dks, dvs = [], [], []
         for h in range(heads):
-            q = qkv_ref[0, :, h * HEAD : (h + 1) * HEAD]
             k = qkv_ref[0, :, width + h * HEAD : width + (h + 1) * HEAD]
             v = qkv_ref[0, :, 2 * width + h * HEAD : 2 * width + (h + 1) * HEAD]
             e = e_ref[0, h]
-            do = dctx[:, h * HEAD : (h + 1) * HEAD] * inv_ref[0, :, h : h + 1]
-            ctx = ctx_ref[0, :, h * HEAD : (h + 1) * HEAD].astype(F32)
-            delta = jnp.sum(do * ctx, axis=-1, keepdims=True)
-            do_low = do.astype(BF)
-            dp = mm(do_low, v, NT)
-            ds = (e.astype(F32) * (dp - delta)).astype(BF)
-            dvs.append(mm(e, do_low, TN))
+            dp = mm(dos[h], v, NT)
+            ds = (e.astype(F32) * (dp - deltas[h])).astype(BF)
+            dvs.append(mm(do_t[h * HEAD : (h + 1) * HEAD], e, NN))
             dqs.append(mm(ds, k, NN) * scale)
-            dks.append(mm(ds, q, TN) * scale)
-        dqkv = jnp.concatenate(dqs + dks + dvs, axis=1).astype(BF)
+            dks.append(mm(q_t[h * HEAD : (h + 1) * HEAD], ds, NN) * scale)
+        dk = jnp.concatenate(dks, axis=0).astype(BF).T
+        dv = jnp.concatenate(dvs, axis=0).astype(BF).T
+        dqkv = jnp.concatenate([jnp.concatenate(dqs, axis=1).astype(BF), dk, dv], axis=1)
         dqkv_ref[0] = dqkv
-        sum_ref[0] = jnp.sum(dqkv.astype(F32), axis=0, keepdims=True)
+        sums = jnp.sum(dqkv.astype(F32), axis=0, keepdims=True)
+        sum_ref[0] = sums
         acc_ref[...] += mm(dqkv, pieces.read(w_ref, at(step), 0, 3 * width), NT)
+        if vectors is not None:
+            fill_rows(rows_ref, sums, wide_ref[0], one_ref, two_ref, vectors[3])
+            rows = rows_ref[...].astype(BF)
+            if tok_t is None:
+                first_ref[0] = rows
+            else:
+                first_ref[0, :, 0 : 3 * width] = mm(tok_t_ref[...], dqkv, NN).astype(BF)
+                first_ref[0, :, 3 * width :] = jnp.zeros((d, EXTRA), BF)
+                for c in range(8):
+                    first = c * (d // 8)
+                    first_ref[0, first : first + 16, 3 * width :] = rows[c]
 
         @pl.when(step == len(ps) - 1)
         def _():
@@ -804,18 +833,27 @@
     def of(*shape):
         return pl.BlockSpec((1,) + shape, lambda i: (at(i),) + (0,) * len(shape))
 
+    specs = [SCALARS, full(n, d), of(n, 3 * width), of(n, width), of(heads, n, n), of(n, 128), full(n, d)]
+    args = [pieces.where, da, qkv, ctx, e, inv, back]
+    out_specs = [per(n, 3 * width), per(1, 3 * width), full(n, d)]
+    outs = [
+        out((len(ps), n, 3 * width), BF), out((len(ps), 1, 3 * width)), out((n, d), BF if last else F32),
+    ]
+    scratch = [pltpu.VMEM((n, d), F32)] + pieces.scratch()
+    if vectors is not None:
+        specs += [of(1, vectors[0].shape[2]), full(*vectors[1].shape), full(*vectors[2].shape)]
+        args += list(vectors[:3])
+        scratch.append(pltpu.VMEM((8, 16, EXTRA), F32))
+        first = (8, 16, EXTRA)
+        if tok_t is not None:
+            specs.append(full(d, n))
+            args.append(tok_t)
+            first = (d, 3 * width + EXTRA)
+        out_specs = [per(*first)] + out_specs
+        outs = [out((len(ps),) + first, BF)] + outs
     return call(
-        kernel, len(ps),
-        [SCALARS, full(n, d), of(n, 3 * width), of(n, width), of(heads, n, n), of(n, 128), full(n, d)]
-        + [ANY] * count,
-        [per(n, 3 * width), per(1, 3 * width), full(n, d)],
-        [
-            out((len(ps), n, 3 * width), BF), out((len(ps), 1, 3 * width)),
-            out((n, d), BF if last else F32),
-        ],
-        [pltpu.VMEM((n, d), F32)] + pieces.scratch(),
-        us=14.3,
-    )(pieces.where, da, qkv, ctx, e, inv, back, *pieces.arrays)
+        kernel, len(ps), specs + [ANY] * count, out_specs, outs, scratch, us=100,
+    )(*args, *pieces.arrays)
 
 
 def lamb(gradient, master, first, second):
@@ -883,7 +921,7 @@
     scratch = []
     for a in extra:
         scratch = [pltpu.VMEM(a.shape, a.dtype), pltpu.SemaphoreType.DMA((2,))]
-    return call(kernel, 1, specs, out_specs, outs, scratch, us=2.6)(*args, *extra)
+    return call(kernel, 1, specs, out_specs, outs, scratch, us=0.01)(*args, *extra)
 
 
 def lamb_last(parts, attn, small_grad, small, early, share):
@@ -961,14 +999,13 @@
     )(*args)
 
 
-def finish(sums, matrices, updates, small, small_update, carried):
+def finish(sums, matrices, updates, small, small_update):
     shapes = [a.shape for a in small]
 
     def kernel(*refs):
         sum_ref, refs = refs[0], refs[1:]
         m_refs, u_refs, v_refs, vu_ref = refs[:4], refs[4:8], refs[8:12], refs[12]
-        turn, end = moved(refs[13], refs[23], refs[24], refs[25])
-        m_outs, v_outs, norm_ref = refs[14:18], refs[18:22], refs[22]
+        m_outs, v_outs, norm_ref = refs[13:17], refs[17:21], refs[21]
         norms = jnp.sqrt(sum_ref[...])
         trust = 0.5 * (norms[0:1] / (norms[1:2] + 1e-06))
         norm_ref[...] = norms[0:2, 0:15]
@@ -985,19 +1022,14 @@
                 update = vu_ref[at : at + 1, 0:lanes_used]
                 v_outs[group][r : r + 1] = v_refs[group][r : r + 1] - factor * update
                 at += 1
-        turn()
-        end()
 
     args = [sums] + list(matrices) + list(updates) + list(small) + [small_update]
     outs = [out(a.shape) for a in matrices] + [out(s) for s in shapes] + [out((2, 15))]
     return call(
         kernel, 1,
-        [full(*a.shape) for a in args] + [ANY],
-        [full(*o.shape) for o in outs] + [ANY],
-        outs + [out(carried.shape, carried.dtype)],
-        [pltpu.VMEM(carried.shape, carried.dtype), pltpu.SemaphoreType.DMA((2,))],
-        us=2.6,
-    )(*args, carried)
+        [full(*a.shape) for a in args], [full(*o.shape) for o in outs], outs,
+        us=0.01,
+    )(*args)
 
 
 def prepare(attn, mix, up, down_rows, small, inside):
@@ -1123,52 +1155,52 @@
 
     down_red = comm.reduction([df_t])
     df = tie(df, down_red.core([act]))
-    dh, wide_grad, ds1, da, da_t, sums_one = ffn_bwd(up_w, down_w, df, slope, ds2, n1, rstd, rows)
-    up_red = comm.reduction([low_t, da_t])
+    up_red = comm.reduction([low_t, None])
     attn_red = comm.reduction([tok_t])
     sizes = (head_own, wide_own, gain_own, dp_size)
     small_sum = None
-    down_lamb = lambda parts: lamb_matrices(
-        parts, [(0, False, down_rows, down_first.T, down_second.T)], layer_out_all
-    )
-    up_lamb = lambda parts: lamb_matrices(
-        parts,
-        [
-            (0, False, up_weight, up_first, up_second),
-            (units, True, mix_weight, mix_first, mix_second),
-        ],
-    )
+    ffn_args = (up_w, down_w, df, slope, ds2, n1, rstd, rows)
+    down_entries = [(0, False, down_rows, down_first.T, down_second.T)]
+    up_entries = [
+        (0, False, up_weight, up_first, up_second),
+        (units, True, mix_weight, mix_first, mix_second),
+    ]
     if comm.small_inside:
+        odd, dh, wide_grad, ds1, da, da_t, sums_one = ffn_bwd(*ffn_args, (low_t, ctx))
+        up_red.lefts[1] = da_t
+        up_red.send_odd(odd)
         done = down_red.split([act], deps=[da])
-        done = up_red.core([tie(dh, done), ctx])
-        da = tie(da, done)
-        odd, odd_sum, back = attn_bwd(attn_w, width, (1, 3), da, qkv, ctx, e, inv, ds1, False)
-        done = down_red.neighbour([odd])
-        done = up_red.split([dh, ctx], deps=done)
-        extra = pack_vectors((1, 3), odd_sum, wide_grad, sums_one, sums_two, sizes)
-        done = attn_red.core([[([1, 3], odd)]], tie(extra, done))
-        da = tie(da, done)
-        even, even_sum, back = attn_bwd(attn_w, width, (0, 2), da, qkv, ctx, e, inv, back, True)
-        extra = pack_vectors((0, 2), even_sum, wide_grad, sums_one, sums_two, sizes)
-        done = attn_red.split([[([0, 2], even)]], extra)
-        done = up_red.neighbour(done)
+        vectors = (wide_grad, sums_one, sums_two, sizes)
+        odd, dqkv_odd, _, back = attn_bwd(
+            attn_w, width, (1, 3), tie(da, done), qkv, ctx, e, inv, ds1, False, vectors, tok_t
+        )
+        attn_red.send_odd(odd)
+        done = down_red.neighbour([odd, layer_out_all], us=100)
+        done = up_red.split([dh, ctx], deps=done + [attn_red.core_got])
         down_parts = down_red.last(done)
-        done = attn_red.neighbour(down_red.done)
+        extra, dqkv, _, back = attn_bwd(
+            attn_w, width, (0, 2), tie(da, down_red.done), qkv, ctx, e, inv, back, True, vectors
+        )
+        done = attn_red.split([[([0, 2], dqkv)]], extra)
+        down_parts[1] = tie(down_parts[1], done)
+        down_done = lamb_matrices(down_parts, down_entries, layer_out_all)
+        done = up_red.neighbour(down_done[3:4], us=100)
+        done = attn_red.neighbour(done)
         tokens_grad_all = lax.all_gather(tie(back, done), "tensor", axis=0, tiled=True)
         up_parts = up_red.last(done)
-        down_parts[1] = tie(down_parts[1], up_red.done)
-        down_done = down_lamb(down_parts)
-        attn_parts = attn_red.last([down_done[3]])
+        attn_parts = attn_red.last(up_red.done)
         up_parts[1] = tie(up_parts[1], attn_red.done)
-        up_done = up_lamb(up_parts)
-        attn_parts[1] = tie(attn_parts[1], [tokens_grad_all])
+        up_done = lamb_matrices(up_parts, up_entries, tokens_grad_all)
     else:
         blocks = range(tensor_size)
+        dh, wide_grad, ds1, da, da_t, sums_one = ffn_bwd(*ffn_args)
+        up_red.lefts[1] = da_t
         dqkv, dqkv_sum, back = attn_bwd(attn_w, width, blocks, da, qkv, ctx, e, inv, ds1, True)
         tokens_grad_all = lax.all_gather(back, "tensor", axis=0, tiled=True)
         up_red.core([dh, ctx])
         attn_red.core([dqkv])
-        down_done, up_done = down_lamb(down_red.last()), up_lamb(up_red.last())
+        down_done = lamb_matrices(down_red.last(), down_entries, layer_out_all)
+        up_done = lamb_matrices(up_red.last(), up_entries, tokens_grad_all)
         attn_parts = attn_red.last()
         small_sum = comm.scatter_small(
             spread_vectors(dqkv_sum, wide_grad, sums_one, sums_two, sizes)
@@ -1185,11 +1217,10 @@
         (last[2], up_done[5], up_done[2], down_done[2]),
         small_masters,
         small_u,
-        tokens_grad_all,
     )
     moments = [last[0:2], up_done[3:5], up_done[0:2], down_done[0:2]]
     moments += [small_moments[2 * k : 2 * k + 2] for k in range(4)]
-    result = [down_done[4], done[9]]
+    result = [down_done[4], up_done[7]]
     for number, (first_new, second_new) in enumerate(moments):
         group = [done[number], first_new, second_new]
         if number == 3:

time: 324 us -> 302 us (0.932)
  Pallas kernels: 149 us -> 141 us
  waiting for transfers between devices: 85.5 us -> 78.2 us
    pallas_call x3 -> x1, Pallas kernels: 13.1 us -> 4.03 us  [grads(): call(kernel, len(ps), specs, per(d, wide), out((len(ps), d, wide), BF), u...]
    ppermute x48, waiting for transfers between devices: 69.9 us -> 62.5 us  [send(): return lax.ppermute(array, ('dp', 'tensor'), pairs)]
    unnamed x92 -> x66, local copies, waits for them, and re-layouts: 13.9 us -> 11 us
    pallas_call x8 -> x6, Pallas kernels: 60.3 us -> 60.6 us  [the longest x2 27.4 us: attn_bwd(): call(kernel, len(ps), specs + [ANY] * count, out_specs, outs, scratch, us...]
  transfers between devices with their start and end apart: 51 -> 51, of which waited for: 18 -> 17; matrix products, arithmetic and copies ran while one was open for 2% -> 2% of each run, Pallas kernels for 33% -> 36%
where the time goes in v1:
time: 302 us; the launch traced here: 301 us
  Pallas kernels  141 us (47%)
  waiting for transfers between devices  78.2 us (26%)
  starting transfers between devices  48.6 us (16%)
  local copies, waits for them, and re-layouts  16.2 us (5%)
  between operations  14.2 us (5%)
  other arithmetic  3.2 us (1%)
    ppermute x48, waiting for transfers between devices, send(): return lax.ppermute(array, ('dp', 'tensor'), pairs)  62.5 us
    ppermute x48, starting transfers between devices, send(): return lax.ppermute(array, ('dp', 'tensor'), pairs)  48.3 us
    pallas_call x2, Pallas kernels, attn_bwd(): call(kernel, len(ps), specs + [ANY] * count, out_specs, outs, scratch, us...  27.4 us
    pallas_call x1, Pallas kernels, ffn_bwd(): call(kernel, blocks, specs + [ANY] * (up_count + down_count), out_specs,...  18.5 us
    pallas_call x1, Pallas kernels, attn_fwd(): call(kernel, blocks, specs, [per(n, 3 * width), per(n, width), per(heads,...  17.5 us
    pallas_call x3, Pallas kernels, split_call(): call(kernel, 1, specs, [full(*shape) for shape in shapes], [out(shape, BF...  15.7 us
    all_gather x1, waiting for transfers between devices, gather_stacked(): everything = lax.all_gather(shard, ('dp', 'tensor'), axis=0, tiled=True)  15.6 us
    pallas_call x2, Pallas kernels, lamb_matrices(): call(kernel, 1, specs, out_specs, outs, scratch, us=0.01)(*args, *extra)  12.1 us
  transfers between devices with their start and end apart: 51, of which 17 were waited for; matrix products, arithmetic and copies ran while one was open for 2% of the time, Pallas kernels for 36%

profile of v1, /device:TPU:0, one launch (start us, length us, event | category | flops | bytes accessed | tf_op | source)
XLA Modules:
  0.0 301.0 jit_solution(14827144064978730690)
XLA Ops:
  9.6 4.1 %collective-permute-start.1 = (bf16[96,896]{1,0:T(8,128)(2,1)}, bf16[96,896]{1,0:T(8,128)(2,1)S(1)}, u32[]{:S(2)}, u32[]{:S(2)}) collective-permute-start(bf16[96,896]{1,0:T(8,128)(2,1)} %get-tuple-element.141.first_ref), channel_id=1, source_target_pairs={{0,16},{1,17},{2,18},{3,19},{4,20},{5,21},{6,22},{7,23},{8,24},{9,... | collective-permute-start | bytes 516104 | tf_op jit(solution)/shard_map/ppermute | solution.py:187
  15.9 10.7 %collective-permute-done.1.first_ref = bf16[96,896]{1,0:T(8,128)(2,1)S(1)} collective-permute-done((bf16[96,896]{1,0:T(8,128)(2,1)}, bf16[96,896]{1,0:T(8,128)(2,1)S(1)}, u32[]{:S(2)}, u32[]{:S(2)}) %collective-permute-start.1) | collective-permute-done | bytes 172064 | tf_op jit(solution)/shard_map/ppermute | solution.py:187
  35.6 5.4 %collective-permute-done.10.refs_9_.refs_13_.refs_12_ = bf16[2,96,896]{2,1,0:T(8,128)(2,1)} collective-permute-done((bf16[2,96,896]{2,1,0:T(8,128)(2,1)}, bf16[2,96,896]{2,1,0:T(8,128)(2,1)}, u32[]{:S(2)}, u32[]{:S(2)}) %collective-permute-start.10) | collective-permute-done | bytes 344096 | tf_op jit(solution)/shard_map/ppermute | solution.py:187
  41.0 3.7 %collective-permute-done.3.refs_2_.refs_6_.refs_5_ = bf16[2,96,896]{2,1,0:T(8,128)(2,1)} collective-permute-done((bf16[2,96,896]{2,1,0:T(8,128)(2,1)}, bf16[2,96,896]{2,1,0:T(8,128)(2,1)}, u32[]{:S(2)}, u32[]{:S(2)}) %collective-permute-start.3) | collective-permute-done | bytes 344096 | tf_op jit(solution)/shard_map/ppermute | solution.py:187
  47.0 9.2 %collective-permute-done.4.refs_3_.refs_7_.refs_6_ = bf16[2,96,896]{2,1,0:T(8,128)(2,1)} collective-permute-done((bf16[2,96,896]{2,1,0:T(8,128)(2,1)S(1)}, bf16[2,96,896]{2,1,0:T(8,128)(2,1)}, u32[]{:S(2)}, u32[]{:S(2)}) %collective-permute-start.4) | collective-permute-done | bytes 344096 | tf_op jit(solution)/shard_map/ppermute | solution.py:187
  60.1 6.9 %collective-permute-done.11.refs_10_.refs_14_.refs_13_ = bf16[2,96,896]{2,1,0:T(8,128)(2,1)} collective-permute-done((bf16[2,96,896]{2,1,0:T(8,128)(2,1)}, bf16[2,96,896]{2,1,0:T(8,128)(2,1)}, u32[]{:S(2)}, u32[]{:S(2)}) %collective-permute-start.11) | collective-permute-done | bytes 344096 | tf_op jit(solution)/shard_map/ppermute | solution.py:187
  73.6 17.5 %shard_map.487 = (bf16[4,512,576]{2,1,0:T(8,128)(2,1)}, bf16[4,512,192]{2,1,0:T(8,128)(2,1)}, bf16[4,3,512,512]{3,2,1,0:T(8,128)(2,1)}, f32[4,512,128]{2,1,0:T(8...) custom-call(s32[3]{0:T(128)} %pad_add_fusion.where_ref, ...), custom_call_target="tpu_custom_call" | custom-call | flops 8499999744 | bytes 1000 | tf_op jit(solution)/shard_map/pallas_call | solution.py:577
  91.1 15.6 %all-gather.4.cloned.1.call-done = bf16[6144,768]{1,0:T(8,128)(2,1)} async-done(((bf16[192,768]{1,0:T(8,128)(2,1)}), bf16[6144,768]{1,0:T(8,128)(2,1)}) %all-gather.4.cloned.1.call-update) | async-done | bytes 9437200 | tf_op jit(solution)/shard_map/all_gather | solution.py:206
  106.7 8.5 %shard_map.488 = (bf16[4,512,768]{2,1,0:T(8,128)(2,1)}, bf16[4,512,768]{2,1,0:T(8,128)(2,1)}) custom-call(s32[3]{0:T(128)} %pad_add_fusion.where_ref, bf16[512,768]{1,0:T(8,128)(2,1)} %get-tuple-element.142.low_ref, f32[4,1,768]{2,1,0:T(1,128)} %get-tuple-element.143.bias_ref, bf16[8,4,2,96,768]{4,3,2,1,0:T(8,128)(2,1)} %bitcast.73), custom_call_target="tpu_custom_call" | custom-call | flops 4249999872 | bytes 1000 | tf_op jit(solution)/shard_map/pallas_call | solution.py:613
  115.2 10.3 %shard_map.489 = (bf16[512,768]{1,0:T(8,128)(2,1)}, f32[512,768]{1,0:T(8,128)}, bf16[512,768]{1,0:T(8,128)(2,1)}, bf16[768,512]{1,0:T(8,128)(2,1)}, f32[8,768]{1,0:T(8,128)}) custom-call(s32[3]{0:T(128)} %pad_add_fusion.where_ref, bf16[4,512,768]{2,1,0:T(8,128)(2,1)} %get-tuple-element.145.act_ref.refs_1_.refs_2_, f32[512,768]{1,0:T(8,128)} %get-tuple-element.146.n1_ref, ...), custom_call_target="tpu_custom_call" | custom-call | flops 5249999872 | bytes 1000 | tf_op jit(solution)/shard_map/pallas_call | solution.py:657
  125.5 4.0 %shard_map.490 = bf16[2,768,768]{2,1,0:T(8,128)(2,1)} custom-call(bf16[768,512]{1,0:T(8,128)(2,1)} %get-tuple-element.148.refs_0_, bf16[4,512,768]{2,1,0:T(8,128)(2,1)} %get-tuple-element.145.act_ref.refs_1_.refs_2_), custom_call_target="tpu_custom_call" | custom-call | flops 5000000 | bytes 1000 | tf_op jit(solution)/shard_map/pallas_call | solution.py:350
  130.0 18.5 %shard_map.491 = (bf16[2,768,1024]{2,1,0:T(8,128)(2,1)}, bf16[4,512,768]{2,1,0:T(8,128)(2,1)}, f32[4,1,768]{2,1,0:T(1,128)}, f32[512,768]{1,0:T(8,128)}, bf16[51...) custom-call(s32[3]{0:T(128)} %pad_add_fusion.where_ref, ...), custom_call_target="tpu_custom_call" | custom-call | flops 49999998976 | bytes 1000 | tf_op jit(solution)/shard_map/pallas_call | solution.py:738
  148.9 5.0 %shard_map.492 = (bf16[4,96,768]{2,1,0:T(8,128)(2,1)}, bf16[4,96,768]{2,1,0:T(8,128)(2,1)}, bf16[2,96,768]{2,1,0:T(8,128)(2,1)}, bf16[2,96,768]{2,1,0:T(8,128)(2,1)}, bf16[4,96,768]{2,1,0:T(8,128)(2,1)}) custom-call(s32[3]{0:T(128)} %pad_add_fusion.where_ref, bf16[4,2,96,512]{3,2,1,0:T(8,128)(2,1)} %bitcast.45, ...), custom_call_target="tpu_custom_call" | custom-call | flops 5000000 | bytes 1000 | tf_op jit(solution)/shard_map/pallas_call | solution.py:402
  155.9 14.3 %shard_map.493 = (bf16[2,768,640]{2,1,0:T(8,128)(2,1)}, bf16[2,512,576]{2,1,0:T(8,128)(2,1)}, f32[2,1,576]{2,1,0:T(1,128)}, f32[512,768]{1,0:T(8,128)}) custom-call(s32[3]{0:T(128)} %pad_add_fusion.where_ref, bf16[512,768]{1,0:T(8,128)(2,1)} %get-tuple-element.185.da_ref, bf16[4,512,576]{2,1,0:T(8,128)(2,1)} %get-tuple-element.164.qkv_ref, ...), custom_call_target="tpu_custom_call" | custom-call | flops 49999998976 | bytes 1000 | tf_op jit(solution)/shard_map/pallas_call | solution.py:854
  176.6 6.0 %shard_map.495 = (bf16[4,96,1024]{2,1,0:T(8,128)(2,1)}, bf16[4,96,1024]{2,1,0:T(8,128)(2,1)}, bf16[2,96,1024]{2,1,0:T(8,128)(2,1)}, bf16[2,96,1024]{2,1,0:T(8,128)(2,1)}, bf16[4,96,1024]{2,1,0:T(8,128)(2,1)}) custom-call(s32[3]{0:T(128)} %pad_add_fusion.where_ref, bf16[4,2,96,512]{3,2,1,0:T(8,128)(2,1)} %bitcast.52, ...), custom_call_target="tpu_custom_call" | custom-call | flops 5000000 | bytes 1000 | tf_op jit(solution)/shard_map/pallas_call | solution.py:402
  192.5 13.1 %shard_map.497 = (bf16[2,8,16,64]{3,2,1,0:T(8,128)(2,1)}, bf16[2,512,576]{2,1,0:T(8,128)(2,1)}, f32[2,1,576]{2,1,0:T(1,128)}, bf16[512,768]{1,0:T(8,128)(2,1)}) custom-call(s32[3]{0:T(128)} %pad_add_fusion.where_ref, bf16[512,768]{1,0:T(8,128)(2,1)} %get-tuple-element.185.da_ref, bf16[4,512,576]{2,1,0:T(8,128)(2,1)} %get-tuple-element.164.qkv_ref, ...), custom_call_target="tpu_custom_call" | custom-call | flops 49999998976 | bytes 1000 | tf_op jit(solution)/shard_map/pallas_call | solution.py:854
  205.7 4.7 %shard_map.498 = (bf16[4,96,640]{2,1,0:T(8,128)(2,1)}, bf16[4,96,640]{2,1,0:T(8,128)(2,1)}, bf16[2,96,640]{2,1,0:T(8,128)(2,1)}, bf16[2,96,640]{2,1,0:T(8,128)(2,1)}, bf16[4,96,640]{2,1,0:T(8,128)(2,1)}) custom-call(s32[3]{0:T(128)} %pad_add_fusion.where_ref, bf16[4,2,96,512]{3,2,1,0:T(8,128)(2,1)} %bitcast.54, ...), custom_call_target="tpu_custom_call" | custom-call | flops 5000000 | bytes 1000 | tf_op jit(solution)/shard_map/pallas_call | solution.py:402
  213.2 5.9 %shard_map.499 = (f32[96,768]{1,0:T(8,128)}, f32[96,768]{1,0:T(8,128)}, f32[96,768]{1,0:T(8,128)}, f32[8,128]{1,0:T(8,128)}, bf16[2048,768]{1,0:T(8,128)(2,1)}) custom-call(f32[96,768]{1,0:T(8,128)} %get-tuple-element.183.refs_0_, bf16[96,768]{1,0:T(8,128)(2,1)} %copy-done.16, bf16[96,768]{1,0:T(8,128)(2,1)} %copy-done.17, bf16[96,768]{1,0:T(8,128)(2,1)} %copy-done.18, ...), custom_call_target="tpu_custom_call" | custom-call | flops 5000000 | bytes 1000 | tf_op jit(solution)/shard_map/pallas_call | solution.py:924
  230.1 7.1 %collective-permute-done.31 = bf16[2,96,1024]{2,1,0:T(8,128)(2,1)S(1)} collective-permute-done((bf16[2,96,1024]{2,1,0:T(8,128)(2,1)}, bf16[2,96,1024]{2,1,0:T(8,128)(2,1)S(1)}, u32[]{:S(2)}, u32[]{:S(2)}) %collective-permute-start.31) | collective-permute-done | bytes 393248 | tf_op jit(solution)/shard_map/ppermute | solution.py:187
  237.2 5.2 %collective-permute-done.32 = bf16[2,96,1024]{2,1,0:T(8,128)(2,1)S(1)} collective-permute-done((bf16[2,96,1024]{2,1,0:T(8,128)(2,1)}, bf16[2,96,1024]{2,1,0:T(8,128)(2,1)S(1)}, u32[]{:S(2)}, u32[]{:S(2)}) %collective-permute-start.32) | collective-permute-done | bytes 393248 | tf_op jit(solution)/shard_map/ppermute | solution.py:187
  247.4 3.3 %collective-permute-start.37 = (bf16[96,1024]{1,0:T(8,128)(2,1)}, bf16[96,1024]{1,0:T(8,128)(2,1)S(1)}, u32[]{:S(2)}, u32[]{:S(2)}) collective-permute-start(bf16[96,1024]{1,0:T(8,128)(2,1)} %get-tuple-element.216), channel_id=1, source_target_pairs={{0,24},{1,25},{2,26},{3,27},{4,28},{5,29},{6,30},{7,31},{8,16},{9,... | collective-permute-start | bytes 589832 | tf_op jit(solution)/shard_map/ppermute | solution.py:187
  255.1 3.3 %collective-permute-start.40 = (bf16[96,640]{1,0:T(8,128)(2,1)}, bf16[96,640]{1,0:T(8,128)(2,1)S(1)}, u32[]{:S(2)}, u32[]{:S(2)}) collective-permute-start(bf16[96,640]{1,0:T(8,128)(2,1)} %get-tuple-element.222), channel_id=1, source_target_pairs={{0,24},{1,25},{2,26},{3,27},{4,28},{5,29},{6,30},{7,31},{8,16},{9,... | collective-permute-start | bytes 368648 | tf_op jit(solution)/shard_map/ppermute | solution.py:187
  258.4 4.8 %collective-permute-done.36.refs_2_ = bf16[96,1024]{1,0:T(8,128)(2,1)S(1)} collective-permute-done((bf16[96,1024]{1,0:T(8,128)(2,1)}, bf16[96,1024]{1,0:T(8,128)(2,1)S(1)}, u32[]{:S(2)}, u32[]{:S(2)}) %collective-permute-start.36) | collective-permute-done | bytes 196640 | tf_op jit(solution)/shard_map/ppermute | solution.py:187
  264.0 6.2 %shard_map.504 = (f32[96,768]{1,0:T(8,128)}, f32[96,768]{1,0:T(8,128)}, f32[96,768]{1,0:T(8,128)}, f32[192,96]{1,0:T(8,128)}, f32[192,96]{1,0:T(8,128)}, /*index...) custom-call(f32[96,1024]{1,0:T(8,128)} %get-tuple-element.210.refs_0_, bf16[96,1024]{1,0:T(8,128)(2,1)} %copy-done.13, ...), custom_call_target="tpu_custom_call" | custom-call | flops 5000000 | bytes 1000 | tf_op jit(solution)/shard_map/pallas_call | solution.py:924
  (184 shorter events, 93.5 us)
Async XLA Ops:
  7.2 99.4 %all-gather.4.cloned.1.call-start = ((), (), s32[]{:S(2)}) async-start(), calls=%async_computation | async-start | bytes 9732096 | tf_op jit(solution)/shard_map/all_gather | solution.py:206
  9.5 160.7 %all-gather.6.cloned.1.call-start = ((), (), s32[]{:S(2)}) async-start(), calls=%async_computation.1 | async-start | bytes 3932160 | tf_op jit(solution)/shard_map/all_gather | solution.py:1154
  9.6 16.9 %collective-permute-start.1 = (bf16[96,896]{1,0:T(8,128)(2,1)}, bf16[96,896]{1,0:T(8,128)(2,1)S(1)}, u32[]{:S(2)}, u32[]{:S(2)}) collective-permute-start(bf16[96,896]{1,0:T(8,128)(2,1)} %get-tuple-element.141.first_ref), channel_id=1, source_target_pairs={{0,16},{1,17},{2,18},{3,19},{4,20},{5,21},{6,22},{7,23},{8,24},{9,... | collective-permute-start | bytes 516104 | tf_op jit(solution)/shard_map/ppermute | solution.py:187
  15.0 16.5 %collective-permute-start = (bf16[96,896]{1,0:T(8,128)(2,1)}, bf16[96,896]{1,0:T(8,128)(2,1)}, u32[]{:S(2)}, u32[]{:S(2)}) collective-permute-start(bf16[96,896]{1,0:T(8,128)(2,1)} %get-tuple-element.141.first_ref), channel_id=1, source_target_pairs={{0,8},{1,9},{2,10},{3,11},{4,12},{5,13},{6,14},{7,15},{8,0},{9,1},... | collective-permute-start | bytes 516104 | tf_op jit(solution)/shard_map/ppermute | solution.py:187
  34.9 21.4 %collective-permute-start.4 = (bf16[2,96,896]{2,1,0:T(8,128)(2,1)S(1)}, bf16[2,96,896]{2,1,0:T(8,128)(2,1)}, u32[]{:S(2)}, u32[]{:S(2)}) collective-permute-start(bf16[2,96,896]{2,1,0:T(8,128)(2,1)S(1)} %copy-done.21), channel_id=1, source_target_pairs={{0,4},{1,5},{2,6},{3,7},{4,0},{5,1},{6,2},{7,3},{8,12},{9,13},{10,... | collective-permute-start | bytes 1032200 | tf_op jit(solution)/shard_map/ppermute | solution.py:187
  35.3 20.9 %collective-permute-start.9 = (bf16[2,96,896]{2,1,0:T(8,128)(2,1)}, bf16[2,96,896]{2,1,0:T(8,128)(2,1)}, u32[]{:S(2)}, u32[]{:S(2)}) collective-permute-start(bf16[2,96,896]{2,1,0:T(8,128)(2,1)} %shard_map.485.refs_0_.refs_4_.refs_3_), channel_id=1, source_target_pairs={{0,2},{1,3},{2,0},{3,1},{4,6},{5,7},{6,4},{7,5},{8,10},{9,11},{10,... | collective-permute-start | bytes 1032200 | tf_op jit(solution)/shard_map/ppermute | solution.py:187
  35.5 23.1 %collective-permute-start.6 = (bf16[2,96,896]{2,1,0:T(8,128)(2,1)S(1)}, bf16[2,96,896]{2,1,0:T(8,128)(2,1)}, u32[]{:S(2)}, u32[]{:S(2)}) collective-permute-start(bf16[2,96,896]{2,1,0:T(8,128)(2,1)S(1)} %copy-done.21), channel_id=1, source_target_pairs={{0,1},{1,0},{2,3},{3,2},{4,5},{5,4},{6,7},{7,6},{8,9},{9,8},{10,11... | collective-permute-start | bytes 1032200 | tf_op jit(solution)/shard_map/ppermute | solution.py:187
  41.0 18.1 %collective-permute-start.5 = (bf16[2,96,896]{2,1,0:T(8,128)(2,1)}, bf16[2,96,896]{2,1,0:T(8,128)(2,1)}, u32[]{:S(2)}, u32[]{:S(2)}) collective-permute-start(bf16[2,96,896]{2,1,0:T(8,128)(2,1)} %shard_map.485.refs_0_.refs_4_.refs_3_), channel_id=1, source_target_pairs={{0,1},{1,0},{2,3},{3,2},{4,5},{5,4},{6,7},{7,6},{8,9},{9,8},{10,11... | collective-permute-start | bytes 1032200 | tf_op jit(solution)/shard_map/ppermute | solution.py:187
  129.5 19.4 %collective-permute-start.17 = (bf16[2,768,768]{2,1,0:T(8,128)(2,1)}, bf16[2,768,768]{2,1,0:T(8,128)(2,1)}, u32[]{:S(2)}, u32[]{:S(2)}) collective-permute-start(bf16[2,768,768]{2,1,0:T(8,128)(2,1)} %shard_map.490), channel_id=1, source_target_pairs={{0,1},{1,0},{2,3},{3,2},{4,5},{5,4},{6,7},{7,6},{8,9},{9,8},{10,11... | collective-permute-start | bytes 7077896 | tf_op jit(solution)/shard_map/ppermute | solution.py:187
  129.8 133.5 %all-gather.8.cloned.1.call-start = ((), (), s32[]{:S(2)}) async-start(), calls=%async_computation.2 | async-start | bytes 3932160 | tf_op jit(solution)/shard_map/all_gather | solution.py:1189
  148.6 26.4 %collective-permute-start.18 = (bf16[2,768,1024]{2,1,0:T(8,128)(2,1)}, bf16[2,768,1024]{2,1,0:T(8,128)(2,1)S(1)}, u32[]{:S(2)}, u32[]{:S(2)}) collective-permute-start(bf16[2,768,1024]{2,1,0:T(8,128)(2,1)} %get-tuple-element.161), channel_id=1, source_target_pairs={{0,1},{1,0},{2,3},{3,2},{4,5},{5,4},{6,7},{7,6},{8,9},{9,8},{10,11... | collective-permute-start | bytes 9437192 | tf_op jit(solution)/shard_map/ppermute | solution.py:187
  153.8 16.4 %collective-permute-start.19 = (bf16[4,96,768]{2,1,0:T(8,128)(2,1)}, bf16[4,96,768]{2,1,0:T(8,128)(2,1)}, u32[]{:S(2)}, u32[]{:S(2)}) collective-permute-start(bf16[4,96,768]{2,1,0:T(8,128)(2,1)} %get-tuple-element.176), channel_id=1, source_target_pairs={{0,2},{1,3},{2,0},{3,1},{4,6},{5,7},{6,4},{7,5},{8,10},{9,11},{10,... | collective-permute-start | bytes 1769480 | tf_op jit(solution)/shard_map/ppermute | solution.py:187
  182.7 36.5 %collective-permute-start.27 = (bf16[4,96,1024]{2,1,0:T(8,128)(2,1)}, bf16[4,96,1024]{2,1,0:T(8,128)(2,1)S(1)}, u32[]{:S(2)}, u32[]{:S(2)}) collective-permute-start(bf16[4,96,1024]{2,1,0:T(8,128)(2,1)} %get-tuple-element.199), channel_id=1, source_target_pairs={{0,2},{1,3},{2,0},{3,1},{4,6},{5,7},{6,4},{7,5},{8,10},{9,11},{10,... | collective-permute-start | bytes 2359304 | tf_op jit(solution)/shard_map/ppermute | solution.py:187
  183.5 35.6 %collective-permute-start.28 = (bf16[4,96,1024]{2,1,0:T(8,128)(2,1)}, bf16[4,96,1024]{2,1,0:T(8,128)(2,1)S(1)}, u32[]{:S(2)}, u32[]{:S(2)}) collective-permute-start(bf16[4,96,1024]{2,1,0:T(8,128)(2,1)} %get-tuple-element.200), channel_id=1, source_target_pairs={{0,4},{1,5},{2,6},{3,7},{4,0},{5,1},{6,2},{7,3},{8,12},{9,13},{10,... | collective-permute-start | bytes 2359304 | tf_op jit(solution)/shard_map/ppermute | solution.py:187
  188.2 22.2 %collective-permute-start.24 = (bf16[96,768]{1,0:T(8,128)(2,1)}, bf16[96,768]{1,0:T(8,128)(2,1)S(1)}, u32[]{:S(2)}, u32[]{:S(2)}) collective-permute-start(bf16[96,768]{1,0:T(8,128)(2,1)} %get-tuple-element.184), channel_id=1, source_target_pairs={{0,8},{1,9},{2,10},{3,11},{4,12},{5,13},{6,14},{7,15},{8,0},{9,1},... | collective-permute-start | bytes 442376 | tf_op jit(solution)/shard_map/ppermute | solution.py:187
  189.6 21.8 %collective-permute-start.25 = (bf16[96,768]{1,0:T(8,128)(2,1)}, bf16[96,768]{1,0:T(8,128)(2,1)S(1)}, u32[]{:S(2)}, u32[]{:S(2)}) collective-permute-start(bf16[96,768]{1,0:T(8,128)(2,1)} %get-tuple-element.191), channel_id=1, source_target_pairs={{0,16},{1,17},{2,18},{3,19},{4,20},{5,21},{6,22},{7,23},{8,24},{9,... | collective-permute-start | bytes 442376 | tf_op jit(solution)/shard_map/ppermute | solution.py:187
  190.7 21.9 %collective-permute-start.26 = (bf16[96,768]{1,0:T(8,128)(2,1)}, bf16[96,768]{1,0:T(8,128)(2,1)S(1)}, u32[]{:S(2)}, u32[]{:S(2)}) collective-permute-start(bf16[96,768]{1,0:T(8,128)(2,1)} %get-tuple-element.192), channel_id=1, source_target_pairs={{0,24},{1,25},{2,26},{3,27},{4,28},{5,29},{6,30},{7,31},{8,16},{9,... | collective-permute-start | bytes 442376 | tf_op jit(solution)/shard_map/ppermute | solution.py:187
  226.8 15.6 %collective-permute-start.32 = (bf16[2,96,1024]{2,1,0:T(8,128)(2,1)}, bf16[2,96,1024]{2,1,0:T(8,128)(2,1)S(1)}, u32[]{:S(2)}, u32[]{:S(2)}) collective-permute-start(bf16[2,96,1024]{2,1,0:T(8,128)(2,1)} %get-tuple-element.201), channel_id=1, source_target_pairs={{0,2},{1,3},{2,0},{3,1},{4,6},{5,7},{6,4},{7,5},{8,10},{9,11},{10,... | collective-permute-start | bytes 1179656 | tf_op jit(solution)/shard_map/ppermute | solution.py:187
  228.0 22.7 %collective-permute-start.34 = (bf16[2,96,640]{2,1,0:T(8,128)(2,1)}, bf16[2,96,640]{2,1,0:T(8,128)(2,1)S(1)}, u32[]{:S(2)}, u32[]{:S(2)}) collective-permute-start(bf16[2,96,640]{2,1,0:T(8,128)(2,1)} %get-tuple-element.208), channel_id=1, source_target_pairs={{0,4},{1,5},{2,6},{3,7},{4,0},{5,1},{6,2},{7,3},{8,12},{9,13},{10,... | collective-permute-start | bytes 737288 | tf_op jit(solution)/shard_map/ppermute | solution.py:187
  228.7 22.0 %collective-permute-start.35 = (bf16[2,96,640]{2,1,0:T(8,128)(2,1)}, bf16[2,96,640]{2,1,0:T(8,128)(2,1)S(1)}, u32[]{:S(2)}, u32[]{:S(2)}) collective-permute-start(bf16[2,96,640]{2,1,0:T(8,128)(2,1)} %get-tuple-element.207), channel_id=1, source_target_pairs={{0,2},{1,3},{2,0},{3,1},{4,6},{5,7},{6,4},{7,5},{8,10},{9,11},{10,... | collective-permute-start | bytes 737288 | tf_op jit(solution)/shard_map/ppermute | solution.py:187
  246.3 16.9 %collective-permute-start.36 = (bf16[96,1024]{1,0:T(8,128)(2,1)}, bf16[96,1024]{1,0:T(8,128)(2,1)S(1)}, u32[]{:S(2)}, u32[]{:S(2)}) collective-permute-start(bf16[96,1024]{1,0:T(8,128)(2,1)} %get-tuple-element.215), channel_id=1, source_target_pairs={{0,16},{1,17},{2,18},{3,19},{4,20},{5,21},{6,22},{7,23},{8,24},{9,... | collective-permute-start | bytes 589832 | tf_op jit(solution)/shard_map/ppermute | solution.py:187
  247.4 15.8 %collective-permute-start.37 = (bf16[96,1024]{1,0:T(8,128)(2,1)}, bf16[96,1024]{1,0:T(8,128)(2,1)S(1)}, u32[]{:S(2)}, u32[]{:S(2)}) collective-permute-start(bf16[96,1024]{1,0:T(8,128)(2,1)} %get-tuple-element.216), channel_id=1, source_target_pairs={{0,24},{1,25},{2,26},{3,27},{4,28},{5,29},{6,30},{7,31},{8,16},{9,... | collective-permute-start | bytes 589832 | tf_op jit(solution)/shard_map/ppermute | solution.py:187
  254.0 16.1 %collective-permute-start.38 = (bf16[96,640]{1,0:T(8,128)(2,1)}, bf16[96,640]{1,0:T(8,128)(2,1)S(1)}, u32[]{:S(2)}, u32[]{:S(2)}) collective-permute-start(bf16[96,640]{1,0:T(8,128)(2,1)} %get-tuple-element.220), channel_id=1, source_target_pairs={{0,8},{1,9},{2,10},{3,11},{4,12},{5,13},{6,14},{7,15},{8,0},{9,1},... | collective-permute-start | bytes 368648 | tf_op jit(solution)/shard_map/ppermute | solution.py:187
  254.0 16.2 %collective-permute-start.39 = (bf16[96,640]{1,0:T(8,128)(2,1)}, bf16[96,640]{1,0:T(8,128)(2,1)S(1)}, u32[]{:S(2)}, u32[]{:S(2)}) collective-permute-start(bf16[96,640]{1,0:T(8,128)(2,1)} %get-tuple-element.221), channel_id=1, source_target_pairs={{0,16},{1,17},{2,18},{3,19},{4,20},{5,21},{6,22},{7,23},{8,24},{9,... | collective-permute-start | bytes 368648 | tf_op jit(solution)/shard_map/ppermute | solution.py:187
  (60 other events, 473.5 us)
Sparse Core Ops, SparseCore 0:
  11.5 95.0 all-gather.3
  129.9 27.1 all-gather.5
  226.1 33.1 all-gather.7

commit v2 on v1

--- a/solution.py
+++ b/solution.py
@@ -129,7 +129,7 @@
     def total(self, values):
         return lax.psum(values, ("dp", "tensor"))
 
-    def reduction(self, lefts):
+    def reduction(self, lefts, library=False):
         return GenericReduction(self, lefts)
 
     def block_sets(self):
@@ -201,6 +201,14 @@
     def gather(self, shard):
         return GridGather(self, shard)
 
+    @staticmethod
+    def sum_z(chunks):
+        rows = chunks.reshape((-1, chunks.shape[2]))
+        groups = [[2 * z + y for z in range(4)] for y in range(2)]
+        return lax.psum_scatter(
+            rows, "dp", scatter_dimension=0, axis_index_groups=groups, tiled=True
+        )
+
     def gather_stacked(self, shard):
         rows, lanes = shard.shape[0] // 2, shard.shape[1]
         everything = lax.all_gather(shard, ("dp", "tensor"), axis=0, tiled=True)
@@ -214,8 +222,8 @@
         sent = [self.send_z(values, k) for k in (1, 2, 3)]
         return values + sent[0] + (sent[1] + sent[2])
 
-    def reduction(self, lefts):
-        return Reduction(self, lefts)
+    def reduction(self, lefts, library=False):
+        return Reduction(self, lefts, library)
 
     def block_sets(self):
         return [(1, 3), (0, 2)]
@@ -253,8 +261,8 @@
 
 
 class Reduction:
-    def __init__(self, comm, lefts):
-        self.comm, self.lefts = comm, lefts
+    def __init__(self, comm, lefts, library):
+        self.comm, self.lefts, self.library = comm, lefts, library
 
     def core(self, rights):
         return self.send_odd(grads(list(zip(self.lefts, rights)), (1, 3)))
@@ -281,8 +289,10 @@
         mine = tie(self.mine, deps)[None]
         low = [(mine, 0), (self.x_got[None], 2), (self.y_got2[None], 0)]
         high = [(mine, 2), (self.y_got[None], 2), (self.x_got2[None], 0)]
-        parts = combine([low, high], None, self.comm.where, us)
+        parts = combine([low, high], self.comm.where, us, self.library)
         self.done = [parts[0]]
+        if self.library:
+            return [self.comm.sum_z(parts[0])]
         return [parts[0]] + [self.comm.send_z(parts[k], k) for k in (1, 2, 3)]
 
 
@@ -423,39 +433,36 @@
     return split_call(terms, got, where, write, [(4,), (4,), (2,), (2,), (4,)], extra)
 
 
-def combine(halves, rows_of, where, us):
+def combine(halves, where, us, whole):
     arrays = []
     for array in [array for half in halves for array, _ in half]:
         if not any(array is other for other in arrays):
             arrays.append(array)
     index = lambda array: [array is other for other in arrays].index(True)
-    plans = [
-        [(index(array), rows_of[h][0] if rows_of else first) for array, first in half]
-        for h, half in enumerate(halves)
-    ]
+    plans = [[(index(array), first) for array, first in half] for half in halves]
     chunk = arrays[0].shape[2:]
 
     def kernel(where_ref, *refs):
-        o0, o1, o2, o3, total = refs[len(arrays) :]
+        outs, total = refs[len(arrays) :], refs[-1]
         for h, plan in enumerate(plans):
             for j in range(2):
                 number, first = plan[0]
                 value = refs[number][0, first + j].astype(F32)
                 for number, first in plan[1:]:
                     value = value + refs[number][0, first + j].astype(F32)
-                total[2 * h + j] = value
-        z = where_ref[0]
-        o0[...] = total[z]
-        o1[...] = total[z ^ 1].astype(BF)
-        o2[...] = total[z ^ 2].astype(BF)
-        o3[...] = total[z ^ 3].astype(BF)
-
+                total[2 * h + j] = value.astype(total.dtype)
+        if not whole:
+            z = where_ref[0]
+            outs[0][...] = total[z]
+            for k in (1, 2, 3):
+                outs[k][...] = total[z ^ k].astype(BF)
+
+    outs = [out((4,) + chunk, BF)] if whole else [out(chunk)] + [out(chunk, BF)] * 3
     return call(
         kernel, 1,
-        [SCALARS] + [full(1, *a.shape[1:]) for a in arrays],
-        [full(*chunk)] * 4,
-        [out(chunk), out(chunk, BF), out(chunk, BF), out(chunk, BF)],
-        [pltpu.VMEM((4,) + chunk, F32)],
+        [SCALARS] + [full(*a.shape) for a in arrays],
+        [full(*o.shape) for o in outs], outs,
+        [] if whole else [pltpu.VMEM((4,) + chunk, F32)],
         us=us,
     )(where, *arrays)
 
@@ -591,52 +598,42 @@
     )(*args)
 
 
-def ffn_up(pieces, low, wide_bias):
+def ffn_fwd(up, down, low, wide_bias, n1, cot, rows, with_odd):
     n, d = low.shape
-    blocks, units, count = pieces.blocks, pieces.lanes, len(pieces.arrays)
-
-    def kernel(where_ref, low_ref, bias_ref, *refs):
-        w_refs, (act_ref, slope_ref, w_ref, sems) = refs[:count], refs[count:]
+    blocks, units = up.blocks, up.lanes
+    up_count, down_count = len(up.arrays), len(down.arrays)
+
+    def kernel(where_ref, low_ref, bias_ref, n1_ref, cot_ref, rows_ref, *refs):
+        up_refs, down_refs = refs[:up_count], refs[up_count : up_count + down_count]
+        refs = refs[up_count + down_count :]
+        if with_odd:
+            odd_ref, kept_ref, refs = refs[0], refs[-1], refs[1:-1]
+        act_ref, slope_ref, y_ref, ds_ref, df_ref, df_t_ref, sum_ref = refs[:7]
+        acc_ref, wu_ref, sems_u, wd_ref, sems_d = refs[7:]
         step = pl.program_id(0)
 
         @pl.when(step == 0)
         def _():
-            pieces.start(w_refs, where_ref, w_ref, sems)
-
-        pieces.wait(w_refs, step, w_ref, sems)
-        h = mm(low_ref[...], pieces.read(w_ref, step, 0, units), NN) + bias_ref[0]
+            up.start(up_refs, where_ref, wu_ref, sems_u)
+            down.start(down_refs, where_ref, wd_ref, sems_d)
+            normed = n1_ref[...] * rows_ref[G1 : G1 + 1] + rows_ref[B1 : B1 + 1]
+            acc_ref[...] = normed + rows_ref[C2 : C2 + 1]
+
+        up.wait(up_refs, step, wu_ref, sems_u)
+        h = mm(low_ref[...], up.read(wu_ref, step, 0, units), NN) + bias_ref[0]
         cdf = 0.5 * (1.0 + lax.erf(h * (0.5**0.5)))
-        act_ref[0] = (h * cdf).astype(BF)
+        act = (h * cdf).astype(BF)
+        act_ref[0] = act
         density = jnp.exp(h * h * -0.5) * 0.3989422804014327
         slope_ref[0] = (cdf + h * density).astype(BF)
-
-    return call(
-        kernel, blocks,
-        [SCALARS, full(n, d), per(1, units)] + [ANY] * count,
-        [per(n, units), per(n, units)],
-        [out((blocks, n, units), BF), out((blocks, n, units), BF)],
-        pieces.scratch(),
-        us=8.5,
-    )(pieces.where, low, wide_bias, *pieces.arrays)
-
-
-def ffn_down(pieces, act, n1, cot, rows):
-    n, d = n1.shape
-    blocks, units, count = pieces.blocks, pieces.lanes, len(pieces.arrays)
-
-    def kernel(where_ref, act_ref, n1_ref, cot_ref, rows_ref, *refs):
-        w_refs, refs = refs[:count], refs[count:]
-        y_ref, ds_ref, df_ref, df_t_ref, sum_ref, acc_ref, w_ref, sems = refs
-        step = pl.program_id(0)
-
-        @pl.when(step == 0)
-        def _():
-            pieces.start(w_refs, where_ref, w_ref, sems)
-            normed = n1_ref[...] * rows_ref[G1 : G1 + 1] + rows_ref[B1 : B1 + 1]
-            acc_ref[...] = normed + rows_ref[C2 : C2 + 1]
-
-        pieces.wait(w_refs, step, w_ref, sems)
-        acc_ref[...] += mm(act_ref[0], pieces.read(w_ref, step, 0, units), NT)
+        if with_odd:
+
+            @pl.when(step % 2 == 1)
+            def _():
+                kept_ref[step // 2] = act
+
+        down.wait(down_refs, step, wd_ref, sems_d)
+        acc_ref[...] += mm(act, down.read(wd_ref, step, 0, units), NT)
 
         @pl.when(step == blocks - 1)
         def _():
@@ -648,20 +645,34 @@
             ds_ref[...] = ds
             df = ds.astype(BF)
             df_ref[...] = df
-            df_t_ref[...] = df.T
+            df_t = df.T
+            df_t_ref[...] = df_t
             sum_ref[...] = jnp.zeros_like(sum_ref)
             sum_ref[0:1] = jnp.sum(upstream * normal, axis=0, keepdims=True)
             sum_ref[1:2] = jnp.sum(upstream, axis=0, keepdims=True)
             sum_ref[2:3] = jnp.sum(ds, axis=0, keepdims=True)
-
+            if with_odd:
+                for k in range(2):
+                    odd_ref[k] = mm(df_t, kept_ref[k], NN).astype(BF)
+
+    outs = [
+        out((blocks, n, units), BF), out((blocks, n, units), BF), out((n, d), BF), out((n, d)),
+        out((n, d), BF), out((d, n), BF), out((8, d)),
+    ]
+    out_specs = [
+        per(n, units), per(n, units), full(n, d), full(n, d), full(n, d), full(d, n), full(8, d),
+    ]
+    scratch = [pltpu.VMEM((n, d), F32)] + up.scratch() + down.scratch()
+    if with_odd:
+        outs = [out((2, d, units), BF)] + outs
+        out_specs = [full(2, d, units)] + out_specs
+        scratch.append(pltpu.VMEM((2, n, units), BF))
     return call(
         kernel, blocks,
-        [SCALARS, per(n, units), full(n, d), full(n, d), full(*rows.shape)] + [ANY] * count,
-        [full(n, d), full(n, d), full(n, d), full(d, n), full(8, d)],
-        [out((n, d), BF), out((n, d)), out((n, d), BF), out((d, n), BF), out((8, d))],
-        [pltpu.VMEM((n, d), F32)] + pieces.scratch(),
-        us=10.5,
-    )(pieces.where, act, n1, cot, rows, *pieces.arrays)
+        [SCALARS, full(n, d), per(1, units), full(n, d), full(n, d), full(*rows.shape)]
+        + [ANY] * (up_count + down_count),
+        out_specs, outs, scratch, us=20,
+    )(up.where, low, wide_bias, n1, cot, rows, *up.arrays, *down.arrays)
 
 
 def ffn_bwd(up, down, df, slope, ds2, n1, rstd, rows, odd=None):
@@ -761,7 +772,7 @@
             rows_ref[c, at + 1 : at + 2, 0:rest] = row[:, first + EXTRA : first + own]
 
 
-def attn_bwd(pieces, width, ps, da, qkv, ctx, e, inv, back, last, vectors=None, tok_t=None):
+def attn_bwd(pieces, width, ps, da, qkv, ctx, e, inv, back, last, vectors=None, tok_t=None, carried=None):
     n, d = back.shape
     ps = list(ps)
     count = len(pieces.arrays)
@@ -775,6 +786,9 @@
         if tok_t is not None:
             tok_t_ref, refs = refs[0], refs[1:]
         w_refs, refs = refs[:count], refs[count:]
+        if carried is not None:
+            source_ref, target_ref, buffer_ref, copy_sems = refs[0], refs[5], refs[-2], refs[-1]
+            refs = refs[1:5] + refs[6:-2]
         if vectors is not None:
             first_ref, rows_ref, refs = refs[0], refs[-1], refs[1:-1]
         dqkv_ref, sum_ref, tg_ref, acc_ref, w_ref, sems = refs
@@ -784,6 +798,15 @@
         def _():
             pieces.start(w_refs, where_ref, w_ref, sems, ps)
             acc_ref[...] = back_ref[...]
+            if carried is not None:
+                pltpu.make_async_copy(source_ref, buffer_ref, copy_sems.at[0]).start()
+
+        if carried is not None:
+
+            @pl.when(step == len(ps) - 1)
+            def _():
+                pltpu.make_async_copy(source_ref, buffer_ref, copy_sems.at[0]).wait()
+                pltpu.make_async_copy(buffer_ref, target_ref, copy_sems.at[1]).start()
 
         pieces.wait(w_refs, at(step), w_ref, sems)
         dctx = mm(da_ref[...], pieces.read(w_ref, at(step), 3 * width, 4 * width), NN)
@@ -829,6 +852,8 @@
         @pl.when(step == len(ps) - 1)
         def _():
             tg_ref[...] = acc_ref[...].astype(tg_ref.dtype)
+            if carried is not None:
+                pltpu.make_async_copy(buffer_ref, target_ref, copy_sems.at[1]).wait()
 
     def of(*shape):
         return pl.BlockSpec((1,) + shape, lambda i: (at(i),) + (0,) * len(shape))
@@ -851,9 +876,15 @@
             first = (d, 3 * width + EXTRA)
         out_specs = [per(*first)] + out_specs
         outs = [out((len(ps),) + first, BF)] + outs
-    return call(
-        kernel, len(ps), specs + [ANY] * count, out_specs, outs, scratch, us=100,
-    )(*args, *pieces.arrays)
+    specs += [ANY] * count
+    args += pieces.arrays
+    if carried is not None:
+        specs.append(ANY)
+        args.append(carried)
+        out_specs.append(ANY)
+        outs.append(out(carried.shape, carried.dtype))
+        scratch += [pltpu.VMEM(carried.shape, carried.dtype), pltpu.SemaphoreType.DMA((2,))]
+    return call(kernel, len(ps), specs, out_specs, outs, scratch, us=100)(*args)
 
 
 def lamb(gradient, master, first, second):
@@ -868,7 +899,7 @@
 
 
 def chunk_sum(refs, lanes):
-    total = refs[0][:, lanes[0] : lanes[1]]
+    total = refs[0][:, lanes[0] : lanes[1]].astype(F32)
     for ref in refs[1:]:
         total = total + ref[:, lanes[0] : lanes[1]].astype(F32)
     return total
@@ -908,8 +939,9 @@
             at = 2 * number
             sum_ref[at : at + 1] = jnp.broadcast_to(whole_sum(m_ref[...]), (1, 128))
             sum_ref[at + 1 : at + 2] = jnp.broadcast_to(whole_sum(update), (1, 128))
+            if extra and number == 0:
+                turn()
         if extra:
-            turn()
             end()
 
     shapes = [entry[2].shape for entry in entries for _ in range(3)]
@@ -1149,12 +1181,16 @@
     qkv, ctx, e, inv, n1, rstd, low, low_t, tok_t, rows, wide_low = attn_fwd(
         attn_w, width, ((head_own, wide_own, gain_own, dp_size), small_all), tok, group_row, key_open
     )
-    act, slope = ffn_up(up_w, low, wide_low)
-    layer_out, ds2, df, df_t, sums_two = ffn_down(down_w, act, n1, cot, rows)
+    act, slope, layer_out, ds2, df, df_t, sums_two = (
+        ffn := ffn_fwd(up_w, down_w, low, wide_low, n1, cot, rows, comm.small_inside)
+    )[-7:]
     layer_out_all = lax.all_gather(layer_out, "tensor", axis=0, tiled=True)
 
-    down_red = comm.reduction([df_t])
-    df = tie(df, down_red.core([act]))
+    down_red = comm.reduction([df_t], library=True)
+    if comm.small_inside:
+        down_red.send_odd(ffn[0])
+    else:
+        down_red.core([act])
     up_red = comm.reduction([low_t, None])
     attn_red = comm.reduction([tok_t])
     sizes = (head_own, wide_own, gain_own, dp_size)
@@ -1178,15 +1214,16 @@
         done = down_red.neighbour([odd, layer_out_all], us=100)
         done = up_red.split([dh, ctx], deps=done + [attn_red.core_got])
         down_parts = down_red.last(done)
-        extra, dqkv, _, back = attn_bwd(
-            attn_w, width, (0, 2), tie(da, down_red.done), qkv, ctx, e, inv, back, True, vectors
+        extra, dqkv, _, back, layer_out_done = attn_bwd(
+            attn_w, width, (0, 2), tie(da, down_red.done), qkv, ctx, e, inv, back, True, vectors,
+            carried=layer_out_all,
         )
         done = attn_red.split([[([0, 2], dqkv)]], extra)
-        down_parts[1] = tie(down_parts[1], done)
-        down_done = lamb_matrices(down_parts, down_entries, layer_out_all)
+        down_parts[0] = tie(down_parts[0], done)
+        down_done = lamb_matrices(down_parts, down_entries)
         done = up_red.neighbour(down_done[3:4], us=100)
-        done = attn_red.neighbour(done)
         tokens_grad_all = lax.all_gather(tie(back, done), "tensor", axis=0, tiled=True)
+        done = attn_red.neighbour(done, us=100)
         up_parts = up_red.last(done)
         attn_parts = attn_red.last(up_red.done)
         up_parts[1] = tie(up_parts[1], attn_red.done)
@@ -1199,7 +1236,8 @@
         tokens_grad_all = lax.all_gather(back, "tensor", axis=0, tiled=True)
         up_red.core([dh, ctx])
         attn_red.core([dqkv])
-        down_done = lamb_matrices(down_red.last(), down_entries, layer_out_all)
+        layer_out_done = layer_out_all
+        down_done = lamb_matrices(down_red.last(), down_entries)
         up_done = lamb_matrices(up_red.last(), up_entries, tokens_grad_all)
         attn_parts = attn_red.last()
         small_sum = comm.scatter_small(
@@ -1220,7 +1258,7 @@
     )
     moments = [last[0:2], up_done[3:5], up_done[0:2], down_done[0:2]]
     moments += [small_moments[2 * k : 2 * k + 2] for k in range(4)]
-    result = [down_done[4], up_done[7]]
+    result = [layer_out_done, up_done[7]]
     for number, (first_new, second_new) in enumerate(moments):
         group = [done[number], first_new, second_new]
         if number == 3:

time: 302 us -> 292 us (0.967)
  Pallas kernels: 141 us -> 133 us
    ppermute x48 -> x45, waiting for transfers between devices: 62.5 us -> 55.8 us  [send(): return lax.ppermute(array, ('dp', 'tensor'), pairs)]
    all_gather x1, waiting for transfers between devices: 15.6 us -> 19.6 us  [gather_stacked(): everything = lax.all_gather(shard, ('dp', 'tensor'), axis=0, tiled=True)]
    pallas_call x8 -> x6, Pallas kernels: 58.7 us -> 54.9 us  [the longest x2 28.2 us: attn_bwd(): return call(kernel, len(ps), specs, out_specs, outs, scratch, us=100)(*args)]
    pallas_call x2, Pallas kernels: 12.1 us -> 8.49 us  [lamb_matrices(): call(kernel, 1, specs, out_specs, outs, scratch, us=0.01)(*args, *extra)]
    ppermute x48 -> x45, starting transfers between devices: 48.3 us -> 47.9 us  [send(): return lax.ppermute(array, ('dp', 'tensor'), pairs)]
    unnamed x66 -> x60, local copies, waits for them, and re-layouts: 11 us -> 11.4 us
  transfers between devices with their start and end apart: 51 -> 49, of which waited for: 17 -> 20; matrix products, arithmetic and copies ran while one was open for 2% -> 2% of each run, Pallas kernels for 36% -> 37%
where the time goes in v2:
time: 292 us; the launch traced here: 291 us
  Pallas kernels  133 us (46%)
  waiting for transfers between devices  75.5 us (26%)
  starting transfers between devices  48.5 us (17%)
  local copies, waits for them, and re-layouts  16.5 us (6%)
  between operations  14.2 us (5%)
  other arithmetic  3.2 us (1%)
    ppermute x45, waiting for transfers between devices, send(): return lax.ppermute(array, ('dp', 'tensor'), pairs)  55.8 us
    ppermute x45, starting transfers between devices, send(): return lax.ppermute(array, ('dp', 'tensor'), pairs)  47.9 us
    pallas_call x2, Pallas kernels, attn_bwd(): return call(kernel, len(ps), specs, out_specs, outs, scratch, us=100)(*args)  28.2 us
    all_gather x1, waiting for transfers between devices, gather_stacked(): everything = lax.all_gather(shard, ('dp', 'tensor'), axis=0, tiled=True)  19.6 us
    pallas_call x1, Pallas kernels, ffn_bwd(): call(kernel, blocks, specs + [ANY] * (up_count + down_count), out_specs,...  18.5 us
    pallas_call x1, Pallas kernels, ffn_fwd(): call(kernel, blocks, [SCALARS, full(n, d), per(1, units), full(n, d), ful...  18.3 us
    pallas_call x1, Pallas kernels, attn_fwd(): call(kernel, blocks, specs, [per(n, 3 * width), per(n, width), per(heads,...  17.2 us
    pallas_call x3, Pallas kernels, split_call(): call(kernel, 1, specs, [full(*shape) for shape in shapes], [out(shape, BF...  15.8 us
  transfers between devices with their start and end apart: 49, of which 20 were waited for; matrix products, arithmetic and copies ran while one was open for 2% of the time, Pallas kernels for 37%

profile of v2, /device:TPU:0, one launch (start us, length us, event | category | flops | bytes accessed | tf_op | source)
XLA Modules:
  0.0 291.1 jit_solution(5113231448893303780)
XLA Ops:
  9.6 3.1 %collective-permute-start = (bf16[96,896]{1,0:T(8,128)(2,1)}, bf16[96,896]{1,0:T(8,128)(2,1)S(1)}, u32[]{:S(2)}, u32[]{:S(2)}) collective-permute-start(bf16[96,896]{1,0:T(8,128)(2,1)} %get-tuple-element.137.first_ref), channel_id=1, source_target_pairs={{0,8},{1,9},{2,10},{3,11},{4,12},{5,13},{6,14},{7,15},{8,0},{9,1},... | collective-permute-start | bytes 516104 | tf_op jit(solution)/shard_map/ppermute | solution.py:187
  24.5 12.2 %collective-permute-done.1.first_ref = bf16[96,896]{1,0:T(8,128)(2,1)} collective-permute-done((bf16[96,896]{1,0:T(8,128)(2,1)}, bf16[96,896]{1,0:T(8,128)(2,1)}, u32[]{:S(2)}, u32[]{:S(2)}) %collective-permute-start.1) | collective-permute-done | bytes 172064 | tf_op jit(solution)/shard_map/ppermute | solution.py:187
  42.5 9.7 %collective-permute-done.10.refs_9_.refs_13_.refs_12_ = bf16[2,96,896]{2,1,0:T(8,128)(2,1)} collective-permute-done((bf16[2,96,896]{2,1,0:T(8,128)(2,1)}, bf16[2,96,896]{2,1,0:T(8,128)(2,1)}, u32[]{:S(2)}, u32[]{:S(2)}) %collective-permute-start.10) | collective-permute-done | bytes 344096 | tf_op jit(solution)/shard_map/ppermute | solution.py:187
  52.2 4.0 %collective-permute-start.12 = (bf16[2,96,896]{2,1,0:T(8,128)(2,1)}, bf16[2,96,896]{2,1,0:T(8,128)(2,1)}, u32[]{:S(2)}, u32[]{:S(2)}) collective-permute-start(bf16[2,96,896]{2,1,0:T(8,128)(2,1)} %collective-permute-done.10.refs_9_.refs_13_.refs_12_), channel_id=1, source_target_pairs={{0,4},{1,5},{2,6},{3,7},{4,0},{5,1},{6,2},{7,3},{8,12},{9,13},{10,... | collective-permute-start | bytes 1032200 | tf_op jit(solution)/shard_map/ppermute | solution.py:187
  59.2 2.7 collective-permute-done.11.refs_10_.refs_14_.refs_13_
  68.7 17.2 %shard_map.487 = (bf16[4,512,576]{2,1,0:T(8,128)(2,1)}, bf16[4,512,192]{2,1,0:T(8,128)(2,1)}, bf16[4,3,512,512]{3,2,1,0:T(8,128)(2,1)}, f32[4,512,128]{2,1,0:T(8...) custom-call(s32[3]{0:T(128)} %pad_add_fusion.where_ref, ...), custom_call_target="tpu_custom_call" | custom-call | flops 8499999744 | bytes 1000 | tf_op jit(solution)/shard_map/pallas_call | solution.py:584
  85.9 19.6 %all-gather.4.cloned.1.call-done = bf16[6144,768]{1,0:T(8,128)(2,1)} async-done(((bf16[192,768]{1,0:T(8,128)(2,1)}), bf16[6144,768]{1,0:T(8,128)(2,1)}) %all-gather.4.cloned.1.call-update) | async-done | bytes 9437200 | tf_op jit(solution)/shard_map/all_gather | solution.py:214
  105.4 18.3 %shard_map.488 = (bf16[2,768,768]{2,1,0:T(8,128)(2,1)}, bf16[4,512,768]{2,1,0:T(8,128)(2,1)}, bf16[4,512,768]{2,1,0:T(8,128)(2,1)}, bf16[512,768]{1,0:T(8,128)(2...) custom-call(s32[3]{0:T(128)} %pad_add_fusion.where_ref, ...), custom_call_target="tpu_custom_call" | custom-call | flops 10000000000 | bytes 1000 | tf_op jit(solution)/shard_map/pallas_call | solution.py:670
  124.3 18.5 %shard_map.489 = (bf16[2,768,1024]{2,1,0:T(8,128)(2,1)}, bf16[4,512,768]{2,1,0:T(8,128)(2,1)}, f32[4,1,768]{2,1,0:T(1,128)}, f32[512,768]{1,0:T(8,128)}, bf16[51...) custom-call(s32[3]{0:T(128)} %pad_add_fusion.where_ref, ...), custom_call_target="tpu_custom_call" | custom-call | flops 49999998976 | bytes 1000 | tf_op jit(solution)/shard_map/pallas_call | solution.py:749
  144.5 5.0 %shard_map.490 = (bf16[4,96,768]{2,1,0:T(8,128)(2,1)}, bf16[4,96,768]{2,1,0:T(8,128)(2,1)}, bf16[2,96,768]{2,1,0:T(8,128)(2,1)}, bf16[2,96,768]{2,1,0:T(8,128)(2,1)}, bf16[4,96,768]{2,1,0:T(8,128)(2,1)}) custom-call(s32[3]{0:T(128)} %pad_add_fusion.where_ref, bf16[4,2,96,512]{3,2,1,0:T(8,128)(2,1)} %bitcast.54, ...), custom_call_target="tpu_custom_call" | custom-call | flops 5000000 | bytes 1000 | tf_op jit(solution)/shard_map/pallas_call | solution.py:412
  151.4 14.3 %shard_map.491 = (bf16[2,768,640]{2,1,0:T(8,128)(2,1)}, bf16[2,512,576]{2,1,0:T(8,128)(2,1)}, f32[2,1,576]{2,1,0:T(1,128)}, f32[512,768]{1,0:T(8,128)}) custom-call(s32[3]{0:T(128)} %pad_add_fusion.where_ref, bf16[512,768]{1,0:T(8,128)(2,1)} %get-tuple-element.179.da_ref, bf16[4,512,576]{2,1,0:T(8,128)(2,1)} %get-tuple-element.160.qkv_ref, ...), custom_call_target="tpu_custom_call" | custom-call | flops 49999998976 | bytes 1000 | tf_op jit(solution)/shard_map/pallas_call | solution.py:887
  172.2 6.1 %shard_map.493 = (bf16[4,96,1024]{2,1,0:T(8,128)(2,1)}, bf16[4,96,1024]{2,1,0:T(8,128)(2,1)}, bf16[2,96,1024]{2,1,0:T(8,128)(2,1)}, bf16[2,96,1024]{2,1,0:T(8,128)(2,1)}, bf16[4,96,1024]{2,1,0:T(8,128)(2,1)}) custom-call(s32[3]{0:T(128)} %pad_add_fusion.where_ref, bf16[4,2,96,512]{3,2,1,0:T(8,128)(2,1)} %bitcast.52, ...), custom_call_target="tpu_custom_call" | custom-call | flops 5000000 | bytes 1000 | tf_op jit(solution)/shard_map/pallas_call | solution.py:412
  181.1 2.6 shard_map.494
  184.0 13.9 %shard_map.495 = (bf16[2,8,16,64]{3,2,1,0:T(8,128)(2,1)}, bf16[2,512,576]{2,1,0:T(8,128)(2,1)}, f32[2,1,576]{2,1,0:T(1,128)}, bf16[512,768]{1,0:T(8,128)(2,1)}, bf16[2048,768]{1,0:T(8,128)(2,1)}) custom-call(s32[3]{0:T(128)} %pad_add_fusion.where_ref, bf16[512,768]{1,0:T(8,128)(2,1)} %get-tuple-element.179.da_ref, ...), custom_call_target="tpu_custom_call" | custom-call | flops 49999998976 | bytes 1000 | tf_op jit(solution)/shard_map/pallas_call | solution.py:887
  198.0 4.7 %shard_map.496 = (bf16[4,96,640]{2,1,0:T(8,128)(2,1)}, bf16[4,96,640]{2,1,0:T(8,128)(2,1)}, bf16[2,96,640]{2,1,0:T(8,128)(2,1)}, bf16[2,96,640]{2,1,0:T(8,128)(2,1)}, bf16[4,96,640]{2,1,0:T(8,128)(2,1)}) custom-call(s32[3]{0:T(128)} %pad_add_fusion.where_ref, bf16[4,2,96,512]{3,2,1,0:T(8,128)(2,1)} %bitcast.55, ...), custom_call_target="tpu_custom_call" | custom-call | flops 5000000 | bytes 1000 | tf_op jit(solution)/shard_map/pallas_call | solution.py:412
  213.3 3.8 %collective-permute-done.26.xg_ref = bf16[4,96,640]{2,1,0:T(8,128)(2,1)S(1)} collective-permute-done((bf16[4,96,640]{2,1,0:T(8,128)(2,1)}, bf16[4,96,640]{2,1,0:T(8,128)(2,1)S(1)}, u32[]{:S(2)}, u32[]{:S(2)}) %collective-permute-start.26) | collective-permute-done | bytes 491552 | tf_op jit(solution)/shard_map/ppermute | solution.py:187
  223.0 6.4 %collective-permute-done.29 = bf16[2,96,1024]{2,1,0:T(8,128)(2,1)S(1)} collective-permute-done((bf16[2,96,1024]{2,1,0:T(8,128)(2,1)}, bf16[2,96,1024]{2,1,0:T(8,128)(2,1)S(1)}, u32[]{:S(2)}, u32[]{:S(2)}) %collective-permute-start.29) | collective-permute-done | bytes 393248 | tf_op jit(solution)/shard_map/ppermute | solution.py:187
  230.4 3.2 %shard_map.500 = (f32[96,1024]{1,0:T(8,128)}, bf16[96,1024]{1,0:T(8,128)(2,1)}, bf16[96,1024]{1,0:T(8,128)(2,1)}, bf16[96,1024]{1,0:T(8,128)(2,1)}) custom-call(s32[3]{0:T(128)} %pad_add_fusion.where_ref, bf16[1,4,96,1024]{3,2,1,0:T(8,128)(2,1)} %bitcast.56, bf16[1,4,96,1024]{3,2,1,0:T(8,128)(2,1)} %bitcast.57, bf16[1,2,96,1024]{3,2,1,0:T(8,128)(2,1)} %bitcast.64, ...), custom_call_target="tpu_custom_call" | custom-call | flops 5000000 | bytes 1000 | tf_op jit(solution)/shard_map/pallas_call | solution.py:461
  234.9 3.1 %collective-permute-start.34 = (bf16[96,1024]{1,0:T(8,128)(2,1)}, bf16[96,1024]{1,0:T(8,128)(2,1)S(1)}, u32[]{:S(2)}, u32[]{:S(2)}) collective-permute-start(bf16[96,1024]{1,0:T(8,128)(2,1)} %get-tuple-element.208), channel_id=1, source_target_pairs={{0,24},{1,25},{2,26},{3,27},{4,28},{5,29},{6,30},{7,31},{8,16},{9,... | collective-permute-start | bytes 589832 | tf_op jit(solution)/shard_map/ppermute | solution.py:187
  242.9 2.8 collective-permute-start.37
  245.7 7.7 %collective-permute-done.33.refs_2_ = bf16[96,1024]{1,0:T(8,128)(2,1)S(1)} collective-permute-done((bf16[96,1024]{1,0:T(8,128)(2,1)}, bf16[96,1024]{1,0:T(8,128)(2,1)S(1)}, u32[]{:S(2)}, u32[]{:S(2)}) %collective-permute-start.33) | collective-permute-done | bytes 196640 | tf_op jit(solution)/shard_map/ppermute | solution.py:187
  254.1 6.2 %shard_map.502 = (f32[96,768]{1,0:T(8,128)}, f32[96,768]{1,0:T(8,128)}, f32[96,768]{1,0:T(8,128)}, f32[192,96]{1,0:T(8,128)}, f32[192,96]{1,0:T(8,128)}, /*index...) custom-call(f32[96,1024]{1,0:T(8,128)} %get-tuple-element.202.refs_0_, bf16[96,1024]{1,0:T(8,128)(2,1)} %copy-done.14, ...), custom_call_target="tpu_custom_call" | custom-call | flops 5000000 | bytes 1000 | tf_op jit(solution)/shard_map/pallas_call | solution.py:956
  261.0 3.0 %shard_map.503 = (f32[3,96,192]{2,1,0:T(8,128)}, f32[3,96,192]{2,1,0:T(8,128)}, f32[3,96,192]{2,1,0:T(8,128)}, f32[2,24]{1,0:T(2,128)}, f32[2,24]{1,0:T(2,128)},...) custom-call(f32[96,640]{1,0:T(8,128)} %get-tuple-element.205.refs_0_, ...), custom_call_target="tpu_custom_call" | custom-call | flops 1550000000 | bytes 1000 | tf_op jit(solution)/shard_map/pallas_call | solution.py:1028
  272.8 4.9 %collective-permute-start.43 = (f32[8,128]{1,0:T(8,128)S(1)}, f32[8,128]{1,0:T(8,128)S(1)}, u32[]{:S(2)}, u32[]{:S(2)}) collective-permute-start(f32[8,128]{1,0:T(8,128)S(1)} %add_add_fusion.1), channel_id=1, source_target_pairs={{0,16},{1,17},{2,18},{3,19},{4,20},{5,21},{6,22},{7,23},{8,24},{9,... | collective-permute-start | bytes 12296 | tf_op jit(solution)/shard_map/ppermute | solution.py:187
  (173 shorter events, 84.0 us)
Async XLA Ops:
  7.2 98.2 %all-gather.4.cloned.1.call-start = ((), (), s32[]{:S(2)}) async-start(), calls=%async_computation.1 | async-start | bytes 9732096 | tf_op jit(solution)/shard_map/all_gather | solution.py:214
  9.5 156.3 %all-gather.6.cloned.1.call-start = ((), (), s32[]{:S(2)}) async-start(), calls=%async_computation.2 | async-start | bytes 3932160 | tf_op jit(solution)/shard_map/all_gather | solution.py:1187
  15.2 21.5 %collective-permute-start.1 = (bf16[96,896]{1,0:T(8,128)(2,1)}, bf16[96,896]{1,0:T(8,128)(2,1)}, u32[]{:S(2)}, u32[]{:S(2)}) collective-permute-start(bf16[96,896]{1,0:T(8,128)(2,1)} %get-tuple-element.137.first_ref), channel_id=1, source_target_pairs={{0,16},{1,17},{2,18},{3,19},{4,20},{5,21},{6,22},{7,23},{8,24},{9,... | collective-permute-start | bytes 516104 | tf_op jit(solution)/shard_map/ppermute | solution.py:187
  20.2 20.0 %collective-permute-start.9 = (bf16[2,96,896]{2,1,0:T(8,128)(2,1)}, bf16[2,96,896]{2,1,0:T(8,128)(2,1)S(1)}, u32[]{:S(2)}, u32[]{:S(2)}) collective-permute-start(bf16[2,96,896]{2,1,0:T(8,128)(2,1)} %shard_map.485.refs_0_.refs_4_.refs_3_), channel_id=1, source_target_pairs={{0,2},{1,3},{2,0},{3,1},{4,6},{5,7},{6,4},{7,5},{8,10},{9,11},{10,... | collective-permute-start | bytes 1032200 | tf_op jit(solution)/shard_map/ppermute | solution.py:187
  21.7 20.1 %collective-permute-start.5 = (bf16[2,96,896]{2,1,0:T(8,128)(2,1)}, bf16[2,96,896]{2,1,0:T(8,128)(2,1)}, u32[]{:S(2)}, u32[]{:S(2)}) collective-permute-start(bf16[2,96,896]{2,1,0:T(8,128)(2,1)} %shard_map.485.refs_0_.refs_4_.refs_3_), channel_id=1, source_target_pairs={{0,1},{1,0},{2,3},{3,2},{4,5},{5,4},{6,7},{7,6},{8,9},{9,8},{10,11... | collective-permute-start | bytes 1032200 | tf_op jit(solution)/shard_map/ppermute | solution.py:187
  21.7 20.3 %collective-permute-start.3 = (bf16[2,96,896]{2,1,0:T(8,128)(2,1)}, bf16[2,96,896]{2,1,0:T(8,128)(2,1)}, u32[]{:S(2)}, u32[]{:S(2)}) collective-permute-start(bf16[2,96,896]{2,1,0:T(8,128)(2,1)} %shard_map.485.refs_0_.refs_4_.refs_3_), channel_id=1, source_target_pairs={{0,4},{1,5},{2,6},{3,7},{4,0},{5,1},{6,2},{7,3},{8,12},{9,13},{10,... | collective-permute-start | bytes 1032200 | tf_op jit(solution)/shard_map/ppermute | solution.py:187
  40.1 18.4 %collective-permute-start.6 = (bf16[2,96,896]{2,1,0:T(8,128)(2,1)}, bf16[2,96,896]{2,1,0:T(8,128)(2,1)}, u32[]{:S(2)}, u32[]{:S(2)}) collective-permute-start(bf16[2,96,896]{2,1,0:T(8,128)(2,1)} %shard_map.486.refs_1_.refs_5_.refs_4_), channel_id=1, source_target_pairs={{0,1},{1,0},{2,3},{3,2},{4,5},{5,4},{6,7},{7,6},{8,9},{9,8},{10,11... | collective-permute-start | bytes 1032200 | tf_op jit(solution)/shard_map/ppermute | solution.py:187
  40.2 18.4 %collective-permute-start.4 = (bf16[2,96,896]{2,1,0:T(8,128)(2,1)}, bf16[2,96,896]{2,1,0:T(8,128)(2,1)}, u32[]{:S(2)}, u32[]{:S(2)}) collective-permute-start(bf16[2,96,896]{2,1,0:T(8,128)(2,1)} %shard_map.486.refs_1_.refs_5_.refs_4_), channel_id=1, source_target_pairs={{0,4},{1,5},{2,6},{3,7},{4,0},{5,1},{6,2},{7,3},{8,12},{9,13},{10,... | collective-permute-start | bytes 1032200 | tf_op jit(solution)/shard_map/ppermute | solution.py:187
  41.8 17.3 %collective-permute-start.13 = (bf16[2,96,896]{2,1,0:T(8,128)(2,1)S(1)}, bf16[2,96,896]{2,1,0:T(8,128)(2,1)}, u32[]{:S(2)}, u32[]{:S(2)}) collective-permute-start(bf16[2,96,896]{2,1,0:T(8,128)(2,1)S(1)} %collective-permute-done.9.refs_8_.refs_12_.refs_11_), channel_id=1, source_target_pairs={{0,1},{1,0},{2,3},{3,2},{4,5},{5,4},{6,7},{7,6},{8,9},{9,8},{10,11... | collective-permute-start | bytes 1032200 | tf_op jit(solution)/shard_map/ppermute | solution.py:187
  42.0 19.9 %collective-permute-start.11 = (bf16[2,96,896]{2,1,0:T(8,128)(2,1)}, bf16[2,96,896]{2,1,0:T(8,128)(2,1)}, u32[]{:S(2)}, u32[]{:S(2)}) collective-permute-start(bf16[2,96,896]{2,1,0:T(8,128)(2,1)} %collective-permute-done.3.refs_2_.refs_6_.refs_5_), channel_id=1, source_target_pairs={{0,2},{1,3},{2,0},{3,1},{4,6},{5,7},{6,4},{7,5},{8,10},{9,11},{10,... | collective-permute-start | bytes 1032200 | tf_op jit(solution)/shard_map/ppermute | solution.py:187
  123.7 81.0 %reduce-scatter.2.cloned.1.call-start = ((), (), s32[]{:S(2)}) async-start(), calls=%async_computation.3 | async-start | bytes 737280 | tf_op jit(solution)/shard_map/reduce_scatter | solution.py:208
  124.0 19.2 %collective-permute-start.17 = (bf16[2,768,768]{2,1,0:T(8,128)(2,1)}, bf16[2,768,768]{2,1,0:T(8,128)(2,1)S(1)}, u32[]{:S(2)}, u32[]{:S(2)}) collective-permute-start(bf16[2,768,768]{2,1,0:T(8,128)(2,1)} %get-tuple-element.152), channel_id=1, source_target_pairs={{0,1},{1,0},{2,3},{3,2},{4,5},{5,4},{6,7},{7,6},{8,9},{9,8},{10,11... | collective-permute-start | bytes 7077896 | tf_op jit(solution)/shard_map/ppermute | solution.py:187
  142.8 27.8 %collective-permute-start.18 = (bf16[2,768,1024]{2,1,0:T(8,128)(2,1)}, bf16[2,768,1024]{2,1,0:T(8,128)(2,1)S(1)}, u32[]{:S(2)}, u32[]{:S(2)}) collective-permute-start(bf16[2,768,1024]{2,1,0:T(8,128)(2,1)} %get-tuple-element.157), channel_id=1, source_target_pairs={{0,1},{1,0},{2,3},{3,2},{4,5},{5,4},{6,7},{7,6},{8,9},{9,8},{10,11... | collective-permute-start | bytes 9437192 | tf_op jit(solution)/shard_map/ppermute | solution.py:187
  178.3 28.7 %collective-permute-start.24 = (bf16[4,96,1024]{2,1,0:T(8,128)(2,1)}, bf16[4,96,1024]{2,1,0:T(8,128)(2,1)S(1)}, u32[]{:S(2)}, u32[]{:S(2)}) collective-permute-start(bf16[4,96,1024]{2,1,0:T(8,128)(2,1)} %get-tuple-element.191), channel_id=1, source_target_pairs={{0,2},{1,3},{2,0},{3,1},{4,6},{5,7},{6,4},{7,5},{8,10},{9,11},{10,... | collective-permute-start | bytes 2359304 | tf_op jit(solution)/shard_map/ppermute | solution.py:187
  179.2 27.9 %collective-permute-start.25 = (bf16[4,96,1024]{2,1,0:T(8,128)(2,1)}, bf16[4,96,1024]{2,1,0:T(8,128)(2,1)S(1)}, u32[]{:S(2)}, u32[]{:S(2)}) collective-permute-start(bf16[4,96,1024]{2,1,0:T(8,128)(2,1)} %get-tuple-element.192), channel_id=1, source_target_pairs={{0,4},{1,5},{2,6},{3,7},{4,0},{5,1},{6,2},{7,3},{8,12},{9,13},{10,... | collective-permute-start | bytes 2359304 | tf_op jit(solution)/shard_map/ppermute | solution.py:187
  183.8 69.7 %all-gather.8.cloned.1.call-start = ((), (), s32[]{:S(2)}) async-start(), calls=%async_computation.4 | async-start | bytes 3932160 | tf_op jit(solution)/shard_map/all_gather | solution.py:1225
  210.6 18.9 %collective-permute-start.29 = (bf16[2,96,1024]{2,1,0:T(8,128)(2,1)}, bf16[2,96,1024]{2,1,0:T(8,128)(2,1)S(1)}, u32[]{:S(2)}, u32[]{:S(2)}) collective-permute-start(bf16[2,96,1024]{2,1,0:T(8,128)(2,1)} %get-tuple-element.193), channel_id=1, source_target_pairs={{0,2},{1,3},{2,0},{3,1},{4,6},{5,7},{6,4},{7,5},{8,10},{9,11},{10,... | collective-permute-start | bytes 1179656 | tf_op jit(solution)/shard_map/ppermute | solution.py:187
  211.8 17.6 %collective-permute-start.28 = (bf16[2,96,1024]{2,1,0:T(8,128)(2,1)}, bf16[2,96,1024]{2,1,0:T(8,128)(2,1)S(1)}, u32[]{:S(2)}, u32[]{:S(2)}) collective-permute-start(bf16[2,96,1024]{2,1,0:T(8,128)(2,1)} %get-tuple-element.194), channel_id=1, source_target_pairs={{0,4},{1,5},{2,6},{3,7},{4,0},{5,1},{6,2},{7,3},{8,12},{9,13},{10,... | collective-permute-start | bytes 1179656 | tf_op jit(solution)/shard_map/ppermute | solution.py:187
  221.2 16.8 %collective-permute-start.32 = (bf16[2,96,640]{2,1,0:T(8,128)(2,1)}, bf16[2,96,640]{2,1,0:T(8,128)(2,1)S(1)}, u32[]{:S(2)}, u32[]{:S(2)}) collective-permute-start(bf16[2,96,640]{2,1,0:T(8,128)(2,1)} %get-tuple-element.199), channel_id=1, source_target_pairs={{0,2},{1,3},{2,0},{3,1},{4,6},{5,7},{6,4},{7,5},{8,10},{9,11},{10,... | collective-permute-start | bytes 737288 | tf_op jit(solution)/shard_map/ppermute | solution.py:187
  234.9 18.5 %collective-permute-start.33 = (bf16[96,1024]{1,0:T(8,128)(2,1)}, bf16[96,1024]{1,0:T(8,128)(2,1)S(1)}, u32[]{:S(2)}, u32[]{:S(2)}) collective-permute-start(bf16[96,1024]{1,0:T(8,128)(2,1)} %get-tuple-element.207), channel_id=1, source_target_pairs={{0,16},{1,17},{2,18},{3,19},{4,20},{5,21},{6,22},{7,23},{8,24},{9,... | collective-permute-start | bytes 589832 | tf_op jit(solution)/shard_map/ppermute | solution.py:187
  234.9 18.5 %collective-permute-start.34 = (bf16[96,1024]{1,0:T(8,128)(2,1)}, bf16[96,1024]{1,0:T(8,128)(2,1)S(1)}, u32[]{:S(2)}, u32[]{:S(2)}) collective-permute-start(bf16[96,1024]{1,0:T(8,128)(2,1)} %get-tuple-element.208), channel_id=1, source_target_pairs={{0,24},{1,25},{2,26},{3,27},{4,28},{5,29},{6,30},{7,31},{8,16},{9,... | collective-permute-start | bytes 589832 | tf_op jit(solution)/shard_map/ppermute | solution.py:187
  241.3 19.0 %collective-permute-start.35 = (bf16[96,640]{1,0:T(8,128)(2,1)}, bf16[96,640]{1,0:T(8,128)(2,1)S(1)}, u32[]{:S(2)}, u32[]{:S(2)}) collective-permute-start(bf16[96,640]{1,0:T(8,128)(2,1)} %get-tuple-element.212), channel_id=1, source_target_pairs={{0,8},{1,9},{2,10},{3,11},{4,12},{5,13},{6,14},{7,15},{8,0},{9,1},... | collective-permute-start | bytes 368648 | tf_op jit(solution)/shard_map/ppermute | solution.py:187
  242.3 18.0 %collective-permute-start.36 = (bf16[96,640]{1,0:T(8,128)(2,1)}, bf16[96,640]{1,0:T(8,128)(2,1)S(1)}, u32[]{:S(2)}, u32[]{:S(2)}) collective-permute-start(bf16[96,640]{1,0:T(8,128)(2,1)} %get-tuple-element.213), channel_id=1, source_target_pairs={{0,16},{1,17},{2,18},{3,19},{4,20},{5,21},{6,22},{7,23},{8,24},{9,... | collective-permute-start | bytes 368648 | tf_op jit(solution)/shard_map/ppermute | solution.py:187
  242.9 17.5 %collective-permute-start.37 = (bf16[96,640]{1,0:T(8,128)(2,1)}, bf16[96,640]{1,0:T(8,128)(2,1)S(1)}, u32[]{:S(2)}, u32[]{:S(2)}) collective-permute-start(bf16[96,640]{1,0:T(8,128)(2,1)} %get-tuple-element.214), channel_id=1, source_target_pairs={{0,24},{1,25},{2,26},{3,27},{4,28},{5,29},{6,30},{7,31},{8,16},{9,... | collective-permute-start | bytes 368648 | tf_op jit(solution)/shard_map/ppermute | solution.py:187
  (55 other events, 449.7 us)
Sparse Core Ops, SparseCore 0:
  11.5 93.8 all-gather.3
  123.8 27.1 all-gather.5
  183.9 20.6 reduce-scatter.1
  213.4 33.4 all-gather.7

commit v3 on v2

--- a/solution.py
+++ b/solution.py
@@ -15,6 +15,7 @@
 TN = (((0,), (0,)), ((), ()))
 VMEM_LIMIT = 58 << 20
 EXTRA = 64
+CHUNK = 256
 COST = 0.5e9
 
 
@@ -620,20 +621,24 @@
             acc_ref[...] = normed + rows_ref[C2 : C2 + 1]
 
         up.wait(up_refs, step, wu_ref, sems_u)
-        h = mm(low_ref[...], up.read(wu_ref, step, 0, units), NN) + bias_ref[0]
-        cdf = 0.5 * (1.0 + lax.erf(h * (0.5**0.5)))
-        act = (h * cdf).astype(BF)
-        act_ref[0] = act
-        density = jnp.exp(h * h * -0.5) * 0.3989422804014327
-        slope_ref[0] = (cdf + h * density).astype(BF)
+        down.wait(down_refs, step, wd_ref, sems_d)
+        low_all = low_ref[...]
+        parts = []
+        for first in range(0, units, CHUNK):
+            last = first + CHUNK
+            h = mm(low_all, up.read(wu_ref, step, first, last), NN) + bias_ref[0, :, first:last]
+            cdf = 0.5 * (1.0 + lax.erf(h * (0.5**0.5)))
+            act = (h * cdf).astype(BF)
+            act_ref[0, :, first:last] = act
+            density = jnp.exp(h * h * -0.5) * 0.3989422804014327
+            slope_ref[0, :, first:last] = (cdf + h * density).astype(BF)
+            parts.append(mm(act, down.read(wd_ref, step, first, last), NT))
+        acc_ref[...] += sum(parts[1:], parts[0])
         if with_odd:
 
             @pl.when(step % 2 == 1)
             def _():
-                kept_ref[step // 2] = act
-
-        down.wait(down_refs, step, wd_ref, sems_d)
-        acc_ref[...] += mm(act, down.read(wd_ref, step, 0, units), NT)
+                kept_ref[step // 2] = act_ref[0]
 
         @pl.when(step == blocks - 1)
         def _():
@@ -702,17 +707,22 @@
             acc_ref[...] = ds2_ref[...]
 
         down.wait(down_refs, step, wd_ref, sems_d)
-        dact = mm(df_ref[...], down.read(wd_ref, step, 0, units), NN)
-        dh = (dact * slope_ref[0].astype(F32)).astype(BF)
-        dh_ref[0] = dh
-        dc_ref[0] = jnp.sum(dh.astype(F32), axis=0, keepdims=True)
         up.wait(up_refs, step, wu_ref, sems_u)
-        acc_ref[...] += mm(dh, up.read(wu_ref, step, 0, units), NT)
+        df_all = df_ref[...]
+        parts = []
+        for first in range(0, units, CHUNK):
+            last = first + CHUNK
+            dact = mm(df_all, down.read(wd_ref, step, first, last), NN)
+            dh = (dact * slope_ref[0, :, first:last].astype(F32)).astype(BF)
+            dh_ref[0, :, first:last] = dh
+            dc_ref[0, :, first:last] = jnp.sum(dh.astype(F32), axis=0, keepdims=True)
+            parts.append(mm(dh, up.read(wu_ref, step, first, last), NT))
+        acc_ref[...] += sum(parts[1:], parts[0])
         if odd is not None:
 
             @pl.when(step % 2 == 1)
             def _():
-                odd_ref[step // 2, :, 0:units] = mm(low_t_ref[...], dh, NN).astype(BF)
+                odd_ref[step // 2, :, 0:units] = mm(low_t_ref[...], dh_ref[0], NN).astype(BF)
 
         @pl.when(step == blocks - 1)
         def _():
@@ -905,28 +915,36 @@
     return total
 
 
-def moved(source, target, buffer, sems):
-    into = pltpu.make_async_copy(source, buffer, sems.at[0])
-    back = pltpu.make_async_copy(buffer, target, sems.at[1])
-    into.start()
-
-    def turn():
-        into.wait()
-        back.start()
-
-    return turn, back.wait
-
-
-def lamb_matrices(parts, entries, carried=None):
+def copied(source, deps):
+    source = tie(source, deps)
+    count = 4
+    rows = source.shape[0] // count
+
+    def kernel(source_ref, target_ref, buffer_ref, sems):
+        ins, outs = [], []
+        for k in range(count):
+            part = pl.ds(k * rows, rows)
+            ins.append(pltpu.make_async_copy(source_ref.at[part], buffer_ref.at[part], sems.at[0, k]))
+            outs.append(pltpu.make_async_copy(buffer_ref.at[part], target_ref.at[part], sems.at[1, k]))
+            ins[k].start()
+        for k in range(count):
+            ins[k].wait()
+            outs[k].start()
+        for k in range(count):
+            outs[k].wait()
+
+    return call(
+        kernel, 1, [ANY], ANY, out(source.shape, source.dtype),
+        [pltpu.VMEM(source.shape, source.dtype), pltpu.SemaphoreType.DMA((2, count))], us=0.01,
+    )(source)
+
+
+def lamb_matrices(parts, entries):
     count = len(parts)
-    extra = [] if carried is None else [carried]
 
     def kernel(*refs):
         part_refs = refs[:count]
         ins, refs = refs[count : count + 3 * len(entries)], refs[count + 3 * len(entries) :]
-        if extra:
-            turn, end = moved(refs[0], refs[1 + 3 * len(entries) + 1], refs[-2], refs[-1])
-            refs = refs[1:]
         sum_ref = refs[3 * len(entries)]
         for number, (lane, turned, master, _, _) in enumerate(entries):
             m_ref, f_ref, s_ref = ins[3 * number : 3 * number + 3]
@@ -939,21 +957,13 @@
             at = 2 * number
             sum_ref[at : at + 1] = jnp.broadcast_to(whole_sum(m_ref[...]), (1, 128))
             sum_ref[at + 1 : at + 2] = jnp.broadcast_to(whole_sum(update), (1, 128))
-            if extra and number == 0:
-                turn()
-        if extra:
-            end()
 
     shapes = [entry[2].shape for entry in entries for _ in range(3)]
     args = list(parts) + [array for entry in entries for array in entry[2:]]
-    specs = [full(*a.shape) for a in args] + [ANY] * len(extra)
     outs = [out(shape) for shape in shapes] + [out((8, 128))]
-    out_specs = [full(*o.shape) for o in outs] + [ANY] * len(extra)
-    outs += [out(a.shape, a.dtype) for a in extra]
-    scratch = []
-    for a in extra:
-        scratch = [pltpu.VMEM(a.shape, a.dtype), pltpu.SemaphoreType.DMA((2,))]
-    return call(kernel, 1, specs, out_specs, outs, scratch, us=0.01)(*args, *extra)
+    return call(
+        kernel, 1, [full(*a.shape) for a in args], [full(*o.shape) for o in outs], outs, us=0.01,
+    )(*args)
 
 
 def lamb_last(parts, attn, small_grad, small, early, share):
@@ -1226,8 +1236,9 @@
         done = attn_red.neighbour(done, us=100)
         up_parts = up_red.last(done)
         attn_parts = attn_red.last(up_red.done)
-        up_parts[1] = tie(up_parts[1], attn_red.done)
-        up_done = lamb_matrices(up_parts, up_entries, tokens_grad_all)
+        tokens_grad_done = copied(tokens_grad_all, attn_red.done)
+        up_parts[1] = tie(up_parts[1], [tokens_grad_done])
+        up_done = lamb_matrices(up_parts, up_entries)
     else:
         blocks = range(tensor_size)
         dh, wide_grad, ds1, da, da_t, sums_one = ffn_bwd(*ffn_args)
@@ -1238,7 +1249,8 @@
         attn_red.core([dqkv])
         layer_out_done = layer_out_all
         down_done = lamb_matrices(down_red.last(), down_entries)
-        up_done = lamb_matrices(up_red.last(), up_entries, tokens_grad_all)
+        tokens_grad_done = tokens_grad_all
+        up_done = lamb_matrices(up_red.last(), up_entries)
         attn_parts = attn_red.last()
         small_sum = comm.scatter_small(
             spread_vectors(dqkv_sum, wide_grad, sums_one, sums_two, sizes)
@@ -1258,7 +1270,7 @@
     )
     moments = [last[0:2], up_done[3:5], up_done[0:2], down_done[0:2]]
     moments += [small_moments[2 * k : 2 * k + 2] for k in range(4)]
-    result = [layer_out_done, up_done[7]]
+    result = [layer_out_done, tokens_grad_done]
     for number, (first_new, second_new) in enumerate(moments):
         group = [done[number], first_new, second_new]
         if number == 3:

time: 292 us -> 287 us (0.983)
    ppermute x45, waiting for transfers between devices: 55.8 us -> 52.2 us  [send(): return lax.ppermute(array, ('dp', 'tensor'), pairs)]
    pallas_call x2 -> x3, Pallas kernels: 8.49 us -> 8.06 us  [the longest x2 5.2 us: lamb_matrices(): call(kernel, 1, [full(*a.shape) for a in args], [full(*o.shape) for o in...]
  transfers between devices with their start and end apart: 49 -> 49, of which waited for: 20 -> 21; matrix products, arithmetic and copies ran while one was open for 2% -> 2% of each run, Pallas kernels for 37% -> 37%
where the time goes in v3:
time: 287 us; the launch traced here: 286 us
  Pallas kernels  131 us (46%)
  waiting for transfers between devices  72.8 us (25%)
  starting transfers between devices  47.8 us (17%)
  local copies, waits for them, and re-layouts  17.2 us (6%)
  between operations  14.2 us (5%)
  other arithmetic  3.2 us (1%)
    ppermute x45, waiting for transfers between devices, send(): return lax.ppermute(array, ('dp', 'tensor'), pairs)  52.2 us
    ppermute x45, starting transfers between devices, send(): return lax.ppermute(array, ('dp', 'tensor'), pairs)  47.2 us
    pallas_call x2, Pallas kernels, attn_bwd(): return call(kernel, len(ps), specs, out_specs, outs, scratch, us=100)(*args)  28.2 us
    all_gather x1, waiting for transfers between devices, gather_stacked(): everything = lax.all_gather(shard, ('dp', 'tensor'), axis=0, tiled=True)  19.6 us
    pallas_call x1, Pallas kernels, ffn_bwd(): call(kernel, blocks, specs + [ANY] * (up_count + down_count), out_specs,...  17.6 us
    pallas_call x1, Pallas kernels, ffn_fwd(): call(kernel, blocks, [SCALARS, full(n, d), per(1, units), full(n, d), ful...  17.4 us
    pallas_call x1, Pallas kernels, attn_fwd(): call(kernel, blocks, specs, [per(n, 3 * width), per(n, width), per(heads,...  17.2 us
    pallas_call x3, Pallas kernels, split_call(): call(kernel, 1, specs, [full(*shape) for shape in shapes], [out(shape, BF...  15.8 us
  transfers between devices with their start and end apart: 49, of which 21 were waited for; matrix products, arithmetic and copies ran while one was open for 2% of the time, Pallas kernels for 37%

profile of v3, /device:TPU:0, one launch (start us, length us, event | category | flops | bytes accessed | tf_op | source)
XLA Modules:
  0.0 286.2 jit_solution(17442928579802541821)
XLA Ops:
  9.6 3.1 %collective-permute-start = (bf16[96,896]{1,0:T(8,128)(2,1)}, bf16[96,896]{1,0:T(8,128)(2,1)S(1)}, u32[]{:S(2)}, u32[]{:S(2)}) collective-permute-start(bf16[96,896]{1,0:T(8,128)(2,1)} %get-tuple-element.137.first_ref), channel_id=1, source_target_pairs={{0,8},{1,9},{2,10},{3,11},{4,12},{5,13},{6,14},{7,15},{8,0},{9,1},... | collective-permute-start | bytes 516104 | tf_op jit(solution)/shard_map/ppermute | solution.py:188
  24.5 12.2 %collective-permute-done.1.first_ref = bf16[96,896]{1,0:T(8,128)(2,1)} collective-permute-done((bf16[96,896]{1,0:T(8,128)(2,1)}, bf16[96,896]{1,0:T(8,128)(2,1)}, u32[]{:S(2)}, u32[]{:S(2)}) %collective-permute-start.1) | collective-permute-done | bytes 172064 | tf_op jit(solution)/shard_map/ppermute | solution.py:188
  42.5 9.7 %collective-permute-done.10.refs_9_.refs_13_.refs_12_ = bf16[2,96,896]{2,1,0:T(8,128)(2,1)} collective-permute-done((bf16[2,96,896]{2,1,0:T(8,128)(2,1)}, bf16[2,96,896]{2,1,0:T(8,128)(2,1)}, u32[]{:S(2)}, u32[]{:S(2)}) %collective-permute-start.10) | collective-permute-done | bytes 344096 | tf_op jit(solution)/shard_map/ppermute | solution.py:188
  52.2 4.0 %collective-permute-start.12 = (bf16[2,96,896]{2,1,0:T(8,128)(2,1)}, bf16[2,96,896]{2,1,0:T(8,128)(2,1)}, u32[]{:S(2)}, u32[]{:S(2)}) collective-permute-start(bf16[2,96,896]{2,1,0:T(8,128)(2,1)} %collective-permute-done.10.refs_9_.refs_13_.refs_12_), channel_id=1, source_target_pairs={{0,4},{1,5},{2,6},{3,7},{4,0},{5,1},{6,2},{7,3},{8,12},{9,13},{10,... | collective-permute-start | bytes 1032200 | tf_op jit(solution)/shard_map/ppermute | solution.py:188
  59.2 2.7 collective-permute-done.11.refs_10_.refs_14_.refs_13_
  68.7 17.2 %shard_map.487 = (bf16[4,512,576]{2,1,0:T(8,128)(2,1)}, bf16[4,512,192]{2,1,0:T(8,128)(2,1)}, bf16[4,3,512,512]{3,2,1,0:T(8,128)(2,1)}, f32[4,512,128]{2,1,0:T(8...) custom-call(s32[3]{0:T(128)} %pad_add_fusion.where_ref, ...), custom_call_target="tpu_custom_call" | custom-call | flops 8499999744 | bytes 1000 | tf_op jit(solution)/shard_map/pallas_call | solution.py:585
  85.9 19.6 %all-gather.4.cloned.1.call-done = bf16[6144,768]{1,0:T(8,128)(2,1)} async-done(((bf16[192,768]{1,0:T(8,128)(2,1)}), bf16[6144,768]{1,0:T(8,128)(2,1)}) %all-gather.4.cloned.1.call-update) | async-done | bytes 9437200 | tf_op jit(solution)/shard_map/all_gather | solution.py:215
  105.4 17.4 %shard_map.488 = (bf16[2,768,768]{2,1,0:T(8,128)(2,1)}, bf16[4,512,768]{2,1,0:T(8,128)(2,1)}, bf16[4,512,768]{2,1,0:T(8,128)(2,1)}, bf16[512,768]{1,0:T(8,128)(2...) custom-call(s32[3]{0:T(128)} %pad_add_fusion.where_ref, ...), custom_call_target="tpu_custom_call" | custom-call | flops 10000000000 | bytes 1000 | tf_op jit(solution)/shard_map/pallas_call | solution.py:675
  123.4 17.6 %shard_map.489 = (bf16[2,768,1024]{2,1,0:T(8,128)(2,1)}, bf16[4,512,768]{2,1,0:T(8,128)(2,1)}, f32[4,1,768]{2,1,0:T(1,128)}, f32[512,768]{1,0:T(8,128)}, bf16[51...) custom-call(s32[3]{0:T(128)} %pad_add_fusion.where_ref, ...), custom_call_target="tpu_custom_call" | custom-call | flops 49999998976 | bytes 1000 | tf_op jit(solution)/shard_map/pallas_call | solution.py:759
  142.7 5.0 %shard_map.490 = (bf16[4,96,768]{2,1,0:T(8,128)(2,1)}, bf16[4,96,768]{2,1,0:T(8,128)(2,1)}, bf16[2,96,768]{2,1,0:T(8,128)(2,1)}, bf16[2,96,768]{2,1,0:T(8,128)(2,1)}, bf16[4,96,768]{2,1,0:T(8,128)(2,1)}) custom-call(s32[3]{0:T(128)} %pad_add_fusion.where_ref, bf16[4,2,96,512]{3,2,1,0:T(8,128)(2,1)} %bitcast.54, ...), custom_call_target="tpu_custom_call" | custom-call | flops 5000000 | bytes 1000 | tf_op jit(solution)/shard_map/pallas_call | solution.py:413
  149.6 14.3 %shard_map.491 = (bf16[2,768,640]{2,1,0:T(8,128)(2,1)}, bf16[2,512,576]{2,1,0:T(8,128)(2,1)}, f32[2,1,576]{2,1,0:T(1,128)}, f32[512,768]{1,0:T(8,128)}) custom-call(s32[3]{0:T(128)} %pad_add_fusion.where_ref, bf16[512,768]{1,0:T(8,128)(2,1)} %get-tuple-element.179.da_ref, bf16[4,512,576]{2,1,0:T(8,128)(2,1)} %get-tuple-element.160.qkv_ref, ...), custom_call_target="tpu_custom_call" | custom-call | flops 49999998976 | bytes 1000 | tf_op jit(solution)/shard_map/pallas_call | solution.py:897
  170.4 6.1 %shard_map.493 = (bf16[4,96,1024]{2,1,0:T(8,128)(2,1)}, bf16[4,96,1024]{2,1,0:T(8,128)(2,1)}, bf16[2,96,1024]{2,1,0:T(8,128)(2,1)}, bf16[2,96,1024]{2,1,0:T(8,128)(2,1)}, bf16[4,96,1024]{2,1,0:T(8,128)(2,1)}) custom-call(s32[3]{0:T(128)} %pad_add_fusion.where_ref, bf16[4,2,96,512]{3,2,1,0:T(8,128)(2,1)} %bitcast.52, ...), custom_call_target="tpu_custom_call" | custom-call | flops 5000000 | bytes 1000 | tf_op jit(solution)/shard_map/pallas_call | solution.py:413
  182.3 14.0 %shard_map.495 = (bf16[2,8,16,64]{3,2,1,0:T(8,128)(2,1)}, bf16[2,512,576]{2,1,0:T(8,128)(2,1)}, f32[2,1,576]{2,1,0:T(1,128)}, bf16[512,768]{1,0:T(8,128)(2,1)}, bf16[2048,768]{1,0:T(8,128)(2,1)}) custom-call(s32[3]{0:T(128)} %pad_add_fusion.where_ref, bf16[512,768]{1,0:T(8,128)(2,1)} %get-tuple-element.179.da_ref, ...), custom_call_target="tpu_custom_call" | custom-call | flops 49999998976 | bytes 1000 | tf_op jit(solution)/shard_map/pallas_call | solution.py:897
  196.2 4.7 %shard_map.496 = (bf16[4,96,640]{2,1,0:T(8,128)(2,1)}, bf16[4,96,640]{2,1,0:T(8,128)(2,1)}, bf16[2,96,640]{2,1,0:T(8,128)(2,1)}, bf16[2,96,640]{2,1,0:T(8,128)(2,1)}, bf16[4,96,640]{2,1,0:T(8,128)(2,1)}) custom-call(s32[3]{0:T(128)} %pad_add_fusion.where_ref, bf16[4,2,96,512]{3,2,1,0:T(8,128)(2,1)} %bitcast.55, ...), custom_call_target="tpu_custom_call" | custom-call | flops 5000000 | bytes 1000 | tf_op jit(solution)/shard_map/pallas_call | solution.py:413
  211.5 3.8 %collective-permute-done.26.xg_ref = bf16[4,96,640]{2,1,0:T(8,128)(2,1)S(1)} collective-permute-done((bf16[4,96,640]{2,1,0:T(8,128)(2,1)}, bf16[4,96,640]{2,1,0:T(8,128)(2,1)S(1)}, u32[]{:S(2)}, u32[]{:S(2)}) %collective-permute-start.26) | collective-permute-done | bytes 491552 | tf_op jit(solution)/shard_map/ppermute | solution.py:188
  221.3 6.5 %collective-permute-done.29 = bf16[2,96,1024]{2,1,0:T(8,128)(2,1)S(1)} collective-permute-done((bf16[2,96,1024]{2,1,0:T(8,128)(2,1)}, bf16[2,96,1024]{2,1,0:T(8,128)(2,1)S(1)}, u32[]{:S(2)}, u32[]{:S(2)}) %collective-permute-start.29) | collective-permute-done | bytes 393248 | tf_op jit(solution)/shard_map/ppermute | solution.py:188
  228.8 3.2 %shard_map.500 = (f32[96,1024]{1,0:T(8,128)}, bf16[96,1024]{1,0:T(8,128)(2,1)}, bf16[96,1024]{1,0:T(8,128)(2,1)}, bf16[96,1024]{1,0:T(8,128)(2,1)}) custom-call(s32[3]{0:T(128)} %pad_add_fusion.where_ref, bf16[1,4,96,1024]{3,2,1,0:T(8,128)(2,1)} %bitcast.56, bf16[1,4,96,1024]{3,2,1,0:T(8,128)(2,1)} %bitcast.57, bf16[1,2,96,1024]{3,2,1,0:T(8,128)(2,1)} %bitcast.64, ...), custom_call_target="tpu_custom_call" | custom-call | flops 5000000 | bytes 1000 | tf_op jit(solution)/shard_map/pallas_call | solution.py:462
  233.3 3.1 %collective-permute-start.37 = (bf16[96,1024]{1,0:T(8,128)(2,1)}, bf16[96,1024]{1,0:T(8,128)(2,1)S(1)}, u32[]{:S(2)}, u32[]{:S(2)}) collective-permute-start(bf16[96,1024]{1,0:T(8,128)(2,1)} %get-tuple-element.214), channel_id=1, source_target_pairs={{0,24},{1,25},{2,26},{3,27},{4,28},{5,29},{6,30},{7,31},{8,16},{9,... | collective-permute-start | bytes 589832 | tf_op jit(solution)/shard_map/ppermute | solution.py:188
  241.0 3.1 %collective-permute-start.34 = (bf16[96,640]{1,0:T(8,128)(2,1)}, bf16[96,640]{1,0:T(8,128)(2,1)S(1)}, u32[]{:S(2)}, u32[]{:S(2)}) collective-permute-start(bf16[96,640]{1,0:T(8,128)(2,1)} %get-tuple-element.210), channel_id=1, source_target_pairs={{0,24},{1,25},{2,26},{3,27},{4,28},{5,29},{6,30},{7,31},{8,16},{9,... | collective-permute-start | bytes 368648 | tf_op jit(solution)/shard_map/ppermute | solution.py:188
  245.1 2.9 shard_map.502
  247.9 3.6 %collective-permute-done.36.refs_2_ = bf16[96,1024]{1,0:T(8,128)(2,1)S(1)} collective-permute-done((bf16[96,1024]{1,0:T(8,128)(2,1)}, bf16[96,1024]{1,0:T(8,128)(2,1)S(1)}, u32[]{:S(2)}, u32[]{:S(2)}) %collective-permute-start.36) | collective-permute-done | bytes 196640 | tf_op jit(solution)/shard_map/ppermute | solution.py:188
  252.9 2.9 %shard_map.503 = (f32[96,768]{1,0:T(8,128)}, f32[96,768]{1,0:T(8,128)}, f32[96,768]{1,0:T(8,128)}, f32[192,96]{1,0:T(8,128)}, f32[192,96]{1,0:T(8,128)}, /*index=5*/f32[192,96]{1,0:T(8,128)}, f32[8,128]{1,0:T(8,128)}) custom-call(f32[96,1024]{1,0:T(8,128)} %get-tuple-element.204.refs_0_, bf16[96,1024]{1,0:T(8,128)(2,1)} %copy-done.14, ...), custom_call_target="tpu_custom_call" | custom-call | flops 5000000 | bytes 1000 | tf_op jit(solution)/shard_map/pallas_call | solution.py:964
  256.5 3.0 %shard_map.504 = (f32[3,96,192]{2,1,0:T(8,128)}, f32[3,96,192]{2,1,0:T(8,128)}, f32[3,96,192]{2,1,0:T(8,128)}, f32[2,24]{1,0:T(2,128)}, f32[2,24]{1,0:T(2,128)},...) custom-call(f32[96,640]{1,0:T(8,128)} %get-tuple-element.206.refs_0_, ...), custom_call_target="tpu_custom_call" | custom-call | flops 1550000000 | bytes 1000 | tf_op jit(solution)/shard_map/pallas_call | solution.py:1038
  269.7 3.1 %collective-permute-start.43 = (f32[8,128]{1,0:T(8,128)S(1)}, f32[8,128]{1,0:T(8,128)S(1)}, u32[]{:S(2)}, u32[]{:S(2)}) collective-permute-start(f32[8,128]{1,0:T(8,128)S(1)} %add_add_fusion.1), channel_id=1, source_target_pairs={{0,16},{1,17},{2,18},{3,19},{4,20},{5,21},{6,22},{7,23},{8,24},{9,... | collective-permute-start | bytes 12296 | tf_op jit(solution)/shard_map/ppermute | solution.py:188
  (174 shorter events, 89.4 us)
Async XLA Ops:
  7.2 98.2 %all-gather.4.cloned.1.call-start = ((), (), s32[]{:S(2)}) async-start(), calls=%async_computation.1 | async-start | bytes 9732096 | tf_op jit(solution)/shard_map/all_gather | solution.py:215
  9.5 154.4 %all-gather.6.cloned.1.call-start = ((), (), s32[]{:S(2)}) async-start(), calls=%async_computation.2 | async-start | bytes 3932160 | tf_op jit(solution)/shard_map/all_gather | solution.py:1197
  15.2 21.5 %collective-permute-start.1 = (bf16[96,896]{1,0:T(8,128)(2,1)}, bf16[96,896]{1,0:T(8,128)(2,1)}, u32[]{:S(2)}, u32[]{:S(2)}) collective-permute-start(bf16[96,896]{1,0:T(8,128)(2,1)} %get-tuple-element.137.first_ref), channel_id=1, source_target_pairs={{0,16},{1,17},{2,18},{3,19},{4,20},{5,21},{6,22},{7,23},{8,24},{9,... | collective-permute-start | bytes 516104 | tf_op jit(solution)/shard_map/ppermute | solution.py:188
  20.2 20.0 %collective-permute-start.9 = (bf16[2,96,896]{2,1,0:T(8,128)(2,1)}, bf16[2,96,896]{2,1,0:T(8,128)(2,1)S(1)}, u32[]{:S(2)}, u32[]{:S(2)}) collective-permute-start(bf16[2,96,896]{2,1,0:T(8,128)(2,1)} %shard_map.485.refs_0_.refs_4_.refs_3_), channel_id=1, source_target_pairs={{0,2},{1,3},{2,0},{3,1},{4,6},{5,7},{6,4},{7,5},{8,10},{9,11},{10,... | collective-permute-start | bytes 1032200 | tf_op jit(solution)/shard_map/ppermute | solution.py:188
  21.7 20.1 %collective-permute-start.5 = (bf16[2,96,896]{2,1,0:T(8,128)(2,1)}, bf16[2,96,896]{2,1,0:T(8,128)(2,1)}, u32[]{:S(2)}, u32[]{:S(2)}) collective-permute-start(bf16[2,96,896]{2,1,0:T(8,128)(2,1)} %shard_map.485.refs_0_.refs_4_.refs_3_), channel_id=1, source_target_pairs={{0,1},{1,0},{2,3},{3,2},{4,5},{5,4},{6,7},{7,6},{8,9},{9,8},{10,11... | collective-permute-start | bytes 1032200 | tf_op jit(solution)/shard_map/ppermute | solution.py:188
  21.7 20.3 %collective-permute-start.3 = (bf16[2,96,896]{2,1,0:T(8,128)(2,1)}, bf16[2,96,896]{2,1,0:T(8,128)(2,1)}, u32[]{:S(2)}, u32[]{:S(2)}) collective-permute-start(bf16[2,96,896]{2,1,0:T(8,128)(2,1)} %shard_map.485.refs_0_.refs_4_.refs_3_), channel_id=1, source_target_pairs={{0,4},{1,5},{2,6},{3,7},{4,0},{5,1},{6,2},{7,3},{8,12},{9,13},{10,... | collective-permute-start | bytes 1032200 | tf_op jit(solution)/shard_map/ppermute | solution.py:188
  40.1 18.4 %collective-permute-start.6 = (bf16[2,96,896]{2,1,0:T(8,128)(2,1)}, bf16[2,96,896]{2,1,0:T(8,128)(2,1)}, u32[]{:S(2)}, u32[]{:S(2)}) collective-permute-start(bf16[2,96,896]{2,1,0:T(8,128)(2,1)} %shard_map.486.refs_1_.refs_5_.refs_4_), channel_id=1, source_target_pairs={{0,1},{1,0},{2,3},{3,2},{4,5},{5,4},{6,7},{7,6},{8,9},{9,8},{10,11... | collective-permute-start | bytes 1032200 | tf_op jit(solution)/shard_map/ppermute | solution.py:188
  40.2 18.4 %collective-permute-start.4 = (bf16[2,96,896]{2,1,0:T(8,128)(2,1)}, bf16[2,96,896]{2,1,0:T(8,128)(2,1)}, u32[]{:S(2)}, u32[]{:S(2)}) collective-permute-start(bf16[2,96,896]{2,1,0:T(8,128)(2,1)} %shard_map.486.refs_1_.refs_5_.refs_4_), channel_id=1, source_target_pairs={{0,4},{1,5},{2,6},{3,7},{4,0},{5,1},{6,2},{7,3},{8,12},{9,13},{10,... | collective-permute-start | bytes 1032200 | tf_op jit(solution)/shard_map/ppermute | solution.py:188
  41.8 17.3 %collective-permute-start.13 = (bf16[2,96,896]{2,1,0:T(8,128)(2,1)S(1)}, bf16[2,96,896]{2,1,0:T(8,128)(2,1)}, u32[]{:S(2)}, u32[]{:S(2)}) collective-permute-start(bf16[2,96,896]{2,1,0:T(8,128)(2,1)S(1)} %collective-permute-done.9.refs_8_.refs_12_.refs_11_), channel_id=1, source_target_pairs={{0,1},{1,0},{2,3},{3,2},{4,5},{5,4},{6,7},{7,6},{8,9},{9,8},{10,11... | collective-permute-start | bytes 1032200 | tf_op jit(solution)/shard_map/ppermute | solution.py:188
  42.0 19.9 %collective-permute-start.11 = (bf16[2,96,896]{2,1,0:T(8,128)(2,1)}, bf16[2,96,896]{2,1,0:T(8,128)(2,1)}, u32[]{:S(2)}, u32[]{:S(2)}) collective-permute-start(bf16[2,96,896]{2,1,0:T(8,128)(2,1)} %collective-permute-done.3.refs_2_.refs_6_.refs_5_), channel_id=1, source_target_pairs={{0,2},{1,3},{2,0},{3,1},{4,6},{5,7},{6,4},{7,5},{8,10},{9,11},{10,... | collective-permute-start | bytes 1032200 | tf_op jit(solution)/shard_map/ppermute | solution.py:188
  122.9 80.0 %reduce-scatter.2.cloned.1.call-start = ((), (), s32[]{:S(2)}) async-start(), calls=%async_computation.3 | async-start | bytes 737280 | tf_op jit(solution)/shard_map/reduce_scatter | solution.py:209
  123.1 18.2 %collective-permute-start.17 = (bf16[2,768,768]{2,1,0:T(8,128)(2,1)}, bf16[2,768,768]{2,1,0:T(8,128)(2,1)S(1)}, u32[]{:S(2)}, u32[]{:S(2)}) collective-permute-start(bf16[2,768,768]{2,1,0:T(8,128)(2,1)} %get-tuple-element.152), channel_id=1, source_target_pairs={{0,1},{1,0},{2,3},{3,2},{4,5},{5,4},{6,7},{7,6},{8,9},{9,8},{10,11... | collective-permute-start | bytes 7077896 | tf_op jit(solution)/shard_map/ppermute | solution.py:188
  141.0 27.7 %collective-permute-start.18 = (bf16[2,768,1024]{2,1,0:T(8,128)(2,1)}, bf16[2,768,1024]{2,1,0:T(8,128)(2,1)S(1)}, u32[]{:S(2)}, u32[]{:S(2)}) collective-permute-start(bf16[2,768,1024]{2,1,0:T(8,128)(2,1)} %get-tuple-element.157), channel_id=1, source_target_pairs={{0,1},{1,0},{2,3},{3,2},{4,5},{5,4},{6,7},{7,6},{8,9},{9,8},{10,11... | collective-permute-start | bytes 9437192 | tf_op jit(solution)/shard_map/ppermute | solution.py:188
  147.7 16.3 %collective-permute-start.19 = (bf16[4,96,768]{2,1,0:T(8,128)(2,1)}, bf16[4,96,768]{2,1,0:T(8,128)(2,1)}, u32[]{:S(2)}, u32[]{:S(2)}) collective-permute-start(bf16[4,96,768]{2,1,0:T(8,128)(2,1)} %get-tuple-element.172), channel_id=1, source_target_pairs={{0,2},{1,3},{2,0},{3,1},{4,6},{5,7},{6,4},{7,5},{8,10},{9,11},{10,... | collective-permute-start | bytes 1769480 | tf_op jit(solution)/shard_map/ppermute | solution.py:188
  176.5 28.7 %collective-permute-start.24 = (bf16[4,96,1024]{2,1,0:T(8,128)(2,1)}, bf16[4,96,1024]{2,1,0:T(8,128)(2,1)S(1)}, u32[]{:S(2)}, u32[]{:S(2)}) collective-permute-start(bf16[4,96,1024]{2,1,0:T(8,128)(2,1)} %get-tuple-element.191), channel_id=1, source_target_pairs={{0,2},{1,3},{2,0},{3,1},{4,6},{5,7},{6,4},{7,5},{8,10},{9,11},{10,... | collective-permute-start | bytes 2359304 | tf_op jit(solution)/shard_map/ppermute | solution.py:188
  177.4 27.8 %collective-permute-start.25 = (bf16[4,96,1024]{2,1,0:T(8,128)(2,1)}, bf16[4,96,1024]{2,1,0:T(8,128)(2,1)S(1)}, u32[]{:S(2)}, u32[]{:S(2)}) collective-permute-start(bf16[4,96,1024]{2,1,0:T(8,128)(2,1)} %get-tuple-element.192), channel_id=1, source_target_pairs={{0,4},{1,5},{2,6},{3,7},{4,0},{5,1},{6,2},{7,3},{8,12},{9,13},{10,... | collective-permute-start | bytes 2359304 | tf_op jit(solution)/shard_map/ppermute | solution.py:188
  182.0 63.1 %all-gather.8.cloned.1.call-start = ((), (), s32[]{:S(2)}) async-start(), calls=%async_computation.4 | async-start | bytes 3932160 | tf_op jit(solution)/shard_map/all_gather | solution.py:1235
  208.7 19.1 %collective-permute-start.29 = (bf16[2,96,1024]{2,1,0:T(8,128)(2,1)}, bf16[2,96,1024]{2,1,0:T(8,128)(2,1)S(1)}, u32[]{:S(2)}, u32[]{:S(2)}) collective-permute-start(bf16[2,96,1024]{2,1,0:T(8,128)(2,1)} %get-tuple-element.193), channel_id=1, source_target_pairs={{0,2},{1,3},{2,0},{3,1},{4,6},{5,7},{6,4},{7,5},{8,10},{9,11},{10,... | collective-permute-start | bytes 1179656 | tf_op jit(solution)/shard_map/ppermute | solution.py:188
  210.0 17.8 %collective-permute-start.28 = (bf16[2,96,1024]{2,1,0:T(8,128)(2,1)}, bf16[2,96,1024]{2,1,0:T(8,128)(2,1)S(1)}, u32[]{:S(2)}, u32[]{:S(2)}) collective-permute-start(bf16[2,96,1024]{2,1,0:T(8,128)(2,1)} %get-tuple-element.194), channel_id=1, source_target_pairs={{0,4},{1,5},{2,6},{3,7},{4,0},{5,1},{6,2},{7,3},{8,12},{9,13},{10,... | collective-permute-start | bytes 1179656 | tf_op jit(solution)/shard_map/ppermute | solution.py:188
  219.5 16.8 %collective-permute-start.31 = (bf16[2,96,640]{2,1,0:T(8,128)(2,1)}, bf16[2,96,640]{2,1,0:T(8,128)(2,1)S(1)}, u32[]{:S(2)}, u32[]{:S(2)}) collective-permute-start(bf16[2,96,640]{2,1,0:T(8,128)(2,1)} %get-tuple-element.201), channel_id=1, source_target_pairs={{0,2},{1,3},{2,0},{3,1},{4,6},{5,7},{6,4},{7,5},{8,10},{9,11},{10,... | collective-permute-start | bytes 737288 | tf_op jit(solution)/shard_map/ppermute | solution.py:188
  220.4 15.9 %collective-permute-start.30 = (bf16[2,96,640]{2,1,0:T(8,128)(2,1)}, bf16[2,96,640]{2,1,0:T(8,128)(2,1)S(1)}, u32[]{:S(2)}, u32[]{:S(2)}) collective-permute-start(bf16[2,96,640]{2,1,0:T(8,128)(2,1)} %get-tuple-element.202), channel_id=1, source_target_pairs={{0,4},{1,5},{2,6},{3,7},{4,0},{5,1},{6,2},{7,3},{8,12},{9,13},{10,... | collective-permute-start | bytes 737288 | tf_op jit(solution)/shard_map/ppermute | solution.py:188
  233.3 18.2 %collective-permute-start.36 = (bf16[96,1024]{1,0:T(8,128)(2,1)}, bf16[96,1024]{1,0:T(8,128)(2,1)S(1)}, u32[]{:S(2)}, u32[]{:S(2)}) collective-permute-start(bf16[96,1024]{1,0:T(8,128)(2,1)} %get-tuple-element.213), channel_id=1, source_target_pairs={{0,16},{1,17},{2,18},{3,19},{4,20},{5,21},{6,22},{7,23},{8,24},{9,... | collective-permute-start | bytes 589832 | tf_op jit(solution)/shard_map/ppermute | solution.py:188
  233.3 18.2 %collective-permute-start.37 = (bf16[96,1024]{1,0:T(8,128)(2,1)}, bf16[96,1024]{1,0:T(8,128)(2,1)S(1)}, u32[]{:S(2)}, u32[]{:S(2)}) collective-permute-start(bf16[96,1024]{1,0:T(8,128)(2,1)} %get-tuple-element.214), channel_id=1, source_target_pairs={{0,24},{1,25},{2,26},{3,27},{4,28},{5,29},{6,30},{7,31},{8,16},{9,... | collective-permute-start | bytes 589832 | tf_op jit(solution)/shard_map/ppermute | solution.py:188
  239.7 16.1 %collective-permute-start.32 = (bf16[96,640]{1,0:T(8,128)(2,1)}, bf16[96,640]{1,0:T(8,128)(2,1)S(1)}, u32[]{:S(2)}, u32[]{:S(2)}) collective-permute-start(bf16[96,640]{1,0:T(8,128)(2,1)} %get-tuple-element.208), channel_id=1, source_target_pairs={{0,8},{1,9},{2,10},{3,11},{4,12},{5,13},{6,14},{7,15},{8,0},{9,1},... | collective-permute-start | bytes 368648 | tf_op jit(solution)/shard_map/ppermute | solution.py:188
  (55 other events, 441.5 us)
Sparse Core Ops, SparseCore 0:
  11.5 93.8 all-gather.3
  123.0 27.1 all-gather.5
  182.1 20.5 reduce-scatter.1
  211.6 33.3 all-gather.7

commit v4 on v3

--- a/solution.py
+++ b/solution.py
@@ -1074,20 +1074,29 @@
     )(*args)
 
 
-def prepare(attn, mix, up, down_rows, small, inside):
+def prepare_ffn(up, down_rows):
+    rows, units = up.shape
+
+    def kernel(up_ref, down_ref, out_ref):
+        out_ref[0:rows] = up_ref[...].astype(BF)
+        out_ref[rows : 2 * rows] = down_ref[...].astype(BF)
+
+    return call(
+        kernel, 1, [full(rows, units)] * 2, full(2 * rows, units), out((2 * rows, units), BF), us=0.01,
+    )(up, down_rows)
+
+
+def prepare(attn, mix, small, inside):
     rows, width = attn.shape[1:]
-    units = up.shape[1]
     lanes = 4 * width + (128 if inside else 0)
 
-    def kernel(attn_ref, mix_ref, up_ref, down_ref, *refs):
-        attn_out, ffn_out = refs[len(small)], refs[len(small) + 1]
+    def kernel(attn_ref, mix_ref, *refs):
+        attn_out = refs[len(small)]
         for k in range(3):
             attn_out[:, k * width : (k + 1) * width] = attn_ref[k].astype(BF)
         attn_out[:, 3 * width : 4 * width] = mix_ref[...].T.astype(BF)
-        ffn_out[0:rows] = up_ref[...].astype(BF)
-        ffn_out[rows : 2 * rows] = down_ref[...].astype(BF)
         if inside:
-            pack = refs[len(small) + 2]
+            pack = refs[len(small) + 1]
             pack[...] = jnp.zeros_like(pack)
             at = 0
             for ref in refs[: len(small)]:
@@ -1095,8 +1104,8 @@
                 at += ref.shape[0]
             attn_out[:, 4 * width :] = pack[...].astype(BF)
 
-    args = [attn, mix, up, down_rows] + list(small)
-    outs = [out((rows, lanes), BF), out((2 * rows, units), BF)]
+    args = [attn, mix] + list(small)
+    outs = [out((rows, lanes), BF)]
     return call(
         kernel, 1, [full(*a.shape) for a in args], [full(*o.shape) for o in outs], outs,
         [pltpu.VMEM((rows, 128), F32)], us=2.1,
@@ -1167,8 +1176,9 @@
     small_all = None
     if not comm.small_inside:
         small_all = comm.gather_small(pack_rows(small_masters).astype(BF).astype(F32))
-    attn_shard, ffn_shard = prepare(
-        attn_weight, mix_weight, up_weight, down_rows, small_masters, comm.small_inside
+    ffn_shard = prepare_ffn(up_weight, down_rows)
+    (attn_shard,) = prepare(
+        attn_weight, mix_weight, small_masters, comm.small_inside
     )
     attn_g = comm.gather(attn_shard)
     attn_g.z([])

time: 287 us -> 289 us (level)
  no operation moved by 1% of the time
where the time goes in v4:
time: 289 us; the launch traced here: 288 us
  Pallas kernels  133 us (46%)
  waiting for transfers between devices  73.9 us (26%)
  starting transfers between devices  47 us (16%)
  local copies, waits for them, and re-layouts  17.2 us (6%)
  between operations  14.2 us (5%)
  other arithmetic  3.19 us (1%)
    ppermute x45, waiting for transfers between devices, send(): return lax.ppermute(array, ('dp', 'tensor'), pairs)  53.2 us
    ppermute x45, starting transfers between devices, send(): return lax.ppermute(array, ('dp', 'tensor'), pairs)  46.5 us
    pallas_call x2, Pallas kernels, attn_bwd(): return call(kernel, len(ps), specs, out_specs, outs, scratch, us=100)(*args)  28.2 us
    all_gather x1, waiting for transfers between devices, gather_stacked(): everything = lax.all_gather(shard, ('dp', 'tensor'), axis=0, tiled=True)  19.5 us
    pallas_call x1, Pallas kernels, ffn_bwd(): call(kernel, blocks, specs + [ANY] * (up_count + down_count), out_specs,...  17.6 us
    pallas_call x1, Pallas kernels, ffn_fwd(): call(kernel, blocks, [SCALARS, full(n, d), per(1, units), full(n, d), ful...  17.4 us
    pallas_call x1, Pallas kernels, attn_fwd(): call(kernel, blocks, specs, [per(n, 3 * width), per(n, width), per(heads,...  17.2 us
    pallas_call x3, Pallas kernels, split_call(): call(kernel, 1, specs, [full(*shape) for shape in shapes], [out(shape, BF...  15.8 us
  transfers between devices with their start and end apart: 49, of which 21 were waited for; matrix products, arithmetic and copies ran while one was open for 2% of the time, Pallas kernels for 37%

profile of v4, /device:TPU:0, one launch (start us, length us, event | category | flops | bytes accessed | tf_op | source)
XLA Modules:
  0.0 288.1 jit_solution(9702008491275887285)
XLA Ops:
  11.2 3.0 %collective-permute-start = (bf16[96,896]{1,0:T(8,128)(2,1)}, bf16[96,896]{1,0:T(8,128)(2,1)S(1)}, u32[]{:S(2)}, u32[]{:S(2)}) collective-permute-start(bf16[96,896]{1,0:T(8,128)(2,1)} %shard_map.484.first_ref), channel_id=1, source_target_pairs={{0,8},{1,9},{2,10},{3,11},{4,12},{5,13},{6,14},{7,15},{8,0},{9,1},... | collective-permute-start | bytes 516104 | tf_op jit(solution)/shard_map/ppermute | solution.py:188
  26.0 12.5 %collective-permute-done.1.first_ref = bf16[96,896]{1,0:T(8,128)(2,1)} collective-permute-done((bf16[96,896]{1,0:T(8,128)(2,1)}, bf16[96,896]{1,0:T(8,128)(2,1)}, u32[]{:S(2)}, u32[]{:S(2)}) %collective-permute-start.1) | collective-permute-done | bytes 172064 | tf_op jit(solution)/shard_map/ppermute | solution.py:188
  44.2 10.0 %collective-permute-done.10.refs_9_.refs_13_.refs_12_ = bf16[2,96,896]{2,1,0:T(8,128)(2,1)} collective-permute-done((bf16[2,96,896]{2,1,0:T(8,128)(2,1)}, bf16[2,96,896]{2,1,0:T(8,128)(2,1)}, u32[]{:S(2)}, u32[]{:S(2)}) %collective-permute-start.10) | collective-permute-done | bytes 344096 | tf_op jit(solution)/shard_map/ppermute | solution.py:188
  54.3 3.2 %collective-permute-start.12 = (bf16[2,96,896]{2,1,0:T(8,128)(2,1)}, bf16[2,96,896]{2,1,0:T(8,128)(2,1)}, u32[]{:S(2)}, u32[]{:S(2)}) collective-permute-start(bf16[2,96,896]{2,1,0:T(8,128)(2,1)} %collective-permute-done.10.refs_9_.refs_13_.refs_12_), channel_id=1, source_target_pairs={{0,4},{1,5},{2,6},{3,7},{4,0},{5,1},{6,2},{7,3},{8,12},{9,13},{10,... | collective-permute-start | bytes 1032200 | tf_op jit(solution)/shard_map/ppermute | solution.py:188
  60.4 3.6 %collective-permute-done.11.refs_10_.refs_14_.refs_13_ = bf16[2,96,896]{2,1,0:T(8,128)(2,1)} collective-permute-done((bf16[2,96,896]{2,1,0:T(8,128)(2,1)}, bf16[2,96,896]{2,1,0:T(8,128)(2,1)}, u32[]{:S(2)}, u32[]{:S(2)}) %collective-permute-start.11) | collective-permute-done | bytes 344096 | tf_op jit(solution)/shard_map/ppermute | solution.py:188
  70.6 17.2 %shard_map.487 = (bf16[4,512,576]{2,1,0:T(8,128)(2,1)}, bf16[4,512,192]{2,1,0:T(8,128)(2,1)}, bf16[4,3,512,512]{3,2,1,0:T(8,128)(2,1)}, f32[4,512,128]{2,1,0:T(8...) custom-call(s32[3]{0:T(128)} %pad_add_fusion.where_ref, ...), custom_call_target="tpu_custom_call" | custom-call | flops 8499999744 | bytes 1000 | tf_op jit(solution)/shard_map/pallas_call | solution.py:585
  87.8 19.5 %all-gather.4.cloned.1.call-done = bf16[6144,768]{1,0:T(8,128)(2,1)} async-done(((bf16[192,768]{1,0:T(8,128)(2,1)}), bf16[6144,768]{1,0:T(8,128)(2,1)}) %all-gather.4.cloned.1.call-update) | async-done | bytes 9437200 | tf_op jit(solution)/shard_map/all_gather | solution.py:215
  107.3 17.4 %shard_map.489 = (bf16[2,768,768]{2,1,0:T(8,128)(2,1)}, bf16[4,512,768]{2,1,0:T(8,128)(2,1)}, bf16[4,512,768]{2,1,0:T(8,128)(2,1)}, bf16[512,768]{1,0:T(8,128)(2...) custom-call(s32[3]{0:T(128)} %pad_add_fusion.where_ref, ...), custom_call_target="tpu_custom_call" | custom-call | flops 10000000000 | bytes 1000 | tf_op jit(solution)/shard_map/pallas_call | solution.py:675
  125.4 17.6 %shard_map.490 = (bf16[2,768,1024]{2,1,0:T(8,128)(2,1)}, bf16[4,512,768]{2,1,0:T(8,128)(2,1)}, f32[4,1,768]{2,1,0:T(1,128)}, f32[512,768]{1,0:T(8,128)}, bf16[51...) custom-call(s32[3]{0:T(128)} %pad_add_fusion.where_ref, ...), custom_call_target="tpu_custom_call" | custom-call | flops 49999998976 | bytes 1000 | tf_op jit(solution)/shard_map/pallas_call | solution.py:759
  144.7 5.0 %shard_map.491 = (bf16[4,96,768]{2,1,0:T(8,128)(2,1)}, bf16[4,96,768]{2,1,0:T(8,128)(2,1)}, bf16[2,96,768]{2,1,0:T(8,128)(2,1)}, bf16[2,96,768]{2,1,0:T(8,128)(2,1)}, bf16[4,96,768]{2,1,0:T(8,128)(2,1)}) custom-call(s32[3]{0:T(128)} %pad_add_fusion.where_ref, bf16[4,2,96,512]{3,2,1,0:T(8,128)(2,1)} %bitcast.54, ...), custom_call_target="tpu_custom_call" | custom-call | flops 5000000 | bytes 1000 | tf_op jit(solution)/shard_map/pallas_call | solution.py:413
  151.5 14.3 %shard_map.492 = (bf16[2,768,640]{2,1,0:T(8,128)(2,1)}, bf16[2,512,576]{2,1,0:T(8,128)(2,1)}, f32[2,1,576]{2,1,0:T(1,128)}, f32[512,768]{1,0:T(8,128)}) custom-call(s32[3]{0:T(128)} %pad_add_fusion.where_ref, bf16[512,768]{1,0:T(8,128)(2,1)} %get-tuple-element.175.da_ref, bf16[4,512,576]{2,1,0:T(8,128)(2,1)} %get-tuple-element.156.qkv_ref, ...), custom_call_target="tpu_custom_call" | custom-call | flops 49999998976 | bytes 1000 | tf_op jit(solution)/shard_map/pallas_call | solution.py:897
  172.3 6.1 %shard_map.494 = (bf16[4,96,1024]{2,1,0:T(8,128)(2,1)}, bf16[4,96,1024]{2,1,0:T(8,128)(2,1)}, bf16[2,96,1024]{2,1,0:T(8,128)(2,1)}, bf16[2,96,1024]{2,1,0:T(8,128)(2,1)}, bf16[4,96,1024]{2,1,0:T(8,128)(2,1)}) custom-call(s32[3]{0:T(128)} %pad_add_fusion.where_ref, bf16[4,2,96,512]{3,2,1,0:T(8,128)(2,1)} %bitcast.52, ...), custom_call_target="tpu_custom_call" | custom-call | flops 5000000 | bytes 1000 | tf_op jit(solution)/shard_map/pallas_call | solution.py:413
  184.1 13.9 %shard_map.496 = (bf16[2,8,16,64]{3,2,1,0:T(8,128)(2,1)}, bf16[2,512,576]{2,1,0:T(8,128)(2,1)}, f32[2,1,576]{2,1,0:T(1,128)}, bf16[512,768]{1,0:T(8,128)(2,1)}, bf16[2048,768]{1,0:T(8,128)(2,1)}) custom-call(s32[3]{0:T(128)} %pad_add_fusion.where_ref, bf16[512,768]{1,0:T(8,128)(2,1)} %get-tuple-element.175.da_ref, ...), custom_call_target="tpu_custom_call" | custom-call | flops 49999998976 | bytes 1000 | tf_op jit(solution)/shard_map/pallas_call | solution.py:897
  198.1 4.7 %shard_map.497 = (bf16[4,96,640]{2,1,0:T(8,128)(2,1)}, bf16[4,96,640]{2,1,0:T(8,128)(2,1)}, bf16[2,96,640]{2,1,0:T(8,128)(2,1)}, bf16[2,96,640]{2,1,0:T(8,128)(2,1)}, bf16[4,96,640]{2,1,0:T(8,128)(2,1)}) custom-call(s32[3]{0:T(128)} %pad_add_fusion.where_ref, bf16[4,2,96,512]{3,2,1,0:T(8,128)(2,1)} %bitcast.55, ...), custom_call_target="tpu_custom_call" | custom-call | flops 5000000 | bytes 1000 | tf_op jit(solution)/shard_map/pallas_call | solution.py:413
  213.5 3.7 %collective-permute-done.26.xg_ref = bf16[4,96,640]{2,1,0:T(8,128)(2,1)S(1)} collective-permute-done((bf16[4,96,640]{2,1,0:T(8,128)(2,1)}, bf16[4,96,640]{2,1,0:T(8,128)(2,1)S(1)}, u32[]{:S(2)}, u32[]{:S(2)}) %collective-permute-start.26) | collective-permute-done | bytes 491552 | tf_op jit(solution)/shard_map/ppermute | solution.py:188
  223.2 6.5 %collective-permute-done.29 = bf16[2,96,1024]{2,1,0:T(8,128)(2,1)S(1)} collective-permute-done((bf16[2,96,1024]{2,1,0:T(8,128)(2,1)}, bf16[2,96,1024]{2,1,0:T(8,128)(2,1)S(1)}, u32[]{:S(2)}, u32[]{:S(2)}) %collective-permute-start.29) | collective-permute-done | bytes 393248 | tf_op jit(solution)/shard_map/ppermute | solution.py:188
  230.6 3.2 %shard_map.501 = (f32[96,1024]{1,0:T(8,128)}, bf16[96,1024]{1,0:T(8,128)(2,1)}, bf16[96,1024]{1,0:T(8,128)(2,1)}, bf16[96,1024]{1,0:T(8,128)(2,1)}) custom-call(s32[3]{0:T(128)} %pad_add_fusion.where_ref, bf16[1,4,96,1024]{3,2,1,0:T(8,128)(2,1)} %bitcast.56, bf16[1,4,96,1024]{3,2,1,0:T(8,128)(2,1)} %bitcast.57, bf16[1,2,96,1024]{3,2,1,0:T(8,128)(2,1)} %bitcast.64, ...), custom_call_target="tpu_custom_call" | custom-call | flops 5000000 | bytes 1000 | tf_op jit(solution)/shard_map/pallas_call | solution.py:462
  235.2 3.0 %collective-permute-start.37 = (bf16[96,1024]{1,0:T(8,128)(2,1)}, bf16[96,1024]{1,0:T(8,128)(2,1)S(1)}, u32[]{:S(2)}, u32[]{:S(2)}) collective-permute-start(bf16[96,1024]{1,0:T(8,128)(2,1)} %get-tuple-element.210), channel_id=1, source_target_pairs={{0,24},{1,25},{2,26},{3,27},{4,28},{5,29},{6,30},{7,31},{8,16},{9,... | collective-permute-start | bytes 589832 | tf_op jit(solution)/shard_map/ppermute | solution.py:188
  242.9 3.1 %collective-permute-start.34 = (bf16[96,640]{1,0:T(8,128)(2,1)}, bf16[96,640]{1,0:T(8,128)(2,1)S(1)}, u32[]{:S(2)}, u32[]{:S(2)}) collective-permute-start(bf16[96,640]{1,0:T(8,128)(2,1)} %get-tuple-element.206), channel_id=1, source_target_pairs={{0,24},{1,25},{2,26},{3,27},{4,28},{5,29},{6,30},{7,31},{8,16},{9,... | collective-permute-start | bytes 368648 | tf_op jit(solution)/shard_map/ppermute | solution.py:188
  247.0 2.9 shard_map.503
  249.8 3.6 %collective-permute-done.36.refs_2_ = bf16[96,1024]{1,0:T(8,128)(2,1)S(1)} collective-permute-done((bf16[96,1024]{1,0:T(8,128)(2,1)}, bf16[96,1024]{1,0:T(8,128)(2,1)S(1)}, u32[]{:S(2)}, u32[]{:S(2)}) %collective-permute-start.36) | collective-permute-done | bytes 196640 | tf_op jit(solution)/shard_map/ppermute | solution.py:188
  254.8 2.9 %shard_map.504 = (f32[96,768]{1,0:T(8,128)}, f32[96,768]{1,0:T(8,128)}, f32[96,768]{1,0:T(8,128)}, f32[192,96]{1,0:T(8,128)}, f32[192,96]{1,0:T(8,128)}, /*index=5*/f32[192,96]{1,0:T(8,128)}, f32[8,128]{1,0:T(8,128)}) custom-call(f32[96,1024]{1,0:T(8,128)} %get-tuple-element.200.refs_0_, bf16[96,1024]{1,0:T(8,128)(2,1)} %copy-done.14, ...), custom_call_target="tpu_custom_call" | custom-call | flops 5000000 | bytes 1000 | tf_op jit(solution)/shard_map/pallas_call | solution.py:964
  258.5 3.1 %shard_map.505 = (f32[3,96,192]{2,1,0:T(8,128)}, f32[3,96,192]{2,1,0:T(8,128)}, f32[3,96,192]{2,1,0:T(8,128)}, f32[2,24]{1,0:T(2,128)}, f32[2,24]{1,0:T(2,128)},...) custom-call(f32[96,640]{1,0:T(8,128)} %get-tuple-element.202.refs_0_, ...), custom_call_target="tpu_custom_call" | custom-call | flops 1550000000 | bytes 1000 | tf_op jit(solution)/shard_map/pallas_call | solution.py:1038
  271.6 3.1 %collective-permute-start.43 = (f32[8,128]{1,0:T(8,128)S(1)}, f32[8,128]{1,0:T(8,128)S(1)}, u32[]{:S(2)}, u32[]{:S(2)}) collective-permute-start(f32[8,128]{1,0:T(8,128)S(1)} %add_add_fusion.1), channel_id=1, source_target_pairs={{0,16},{1,17},{2,18},{3,19},{4,20},{5,21},{6,22},{7,23},{8,24},{9,... | collective-permute-start | bytes 12296 | tf_op jit(solution)/shard_map/ppermute | solution.py:188
  (175 shorter events, 90.8 us)
Async XLA Ops:
  7.2 100.1 %all-gather.4.cloned.1.call-start = ((), (), s32[]{:S(2)}) async-start(), calls=%async_computation.1 | async-start | bytes 9732096 | tf_op jit(solution)/shard_map/all_gather | solution.py:215
  9.2 156.7 %all-gather.6.cloned.1.call-start = ((), (), s32[]{:S(2)}) async-start(), calls=%async_computation.2 | async-start | bytes 3932160 | tf_op jit(solution)/shard_map/all_gather | solution.py:1207
  16.7 21.9 %collective-permute-start.1 = (bf16[96,896]{1,0:T(8,128)(2,1)}, bf16[96,896]{1,0:T(8,128)(2,1)}, u32[]{:S(2)}, u32[]{:S(2)}) collective-permute-start(bf16[96,896]{1,0:T(8,128)(2,1)} %shard_map.484.first_ref), channel_id=1, source_target_pairs={{0,16},{1,17},{2,18},{3,19},{4,20},{5,21},{6,22},{7,23},{8,24},{9,... | collective-permute-start | bytes 516104 | tf_op jit(solution)/shard_map/ppermute | solution.py:188
  21.7 20.2 %collective-permute-start.9 = (bf16[2,96,896]{2,1,0:T(8,128)(2,1)}, bf16[2,96,896]{2,1,0:T(8,128)(2,1)S(1)}, u32[]{:S(2)}, u32[]{:S(2)}) collective-permute-start(bf16[2,96,896]{2,1,0:T(8,128)(2,1)} %shard_map.485.refs_0_.refs_4_.refs_3_), channel_id=1, source_target_pairs={{0,2},{1,3},{2,0},{3,1},{4,6},{5,7},{6,4},{7,5},{8,10},{9,11},{10,... | collective-permute-start | bytes 1032200 | tf_op jit(solution)/shard_map/ppermute | solution.py:188
  23.2 20.2 %collective-permute-start.5 = (bf16[2,96,896]{2,1,0:T(8,128)(2,1)}, bf16[2,96,896]{2,1,0:T(8,128)(2,1)}, u32[]{:S(2)}, u32[]{:S(2)}) collective-permute-start(bf16[2,96,896]{2,1,0:T(8,128)(2,1)} %shard_map.485.refs_0_.refs_4_.refs_3_), channel_id=1, source_target_pairs={{0,1},{1,0},{2,3},{3,2},{4,5},{5,4},{6,7},{7,6},{8,9},{9,8},{10,11... | collective-permute-start | bytes 1032200 | tf_op jit(solution)/shard_map/ppermute | solution.py:188
  23.2 20.3 %collective-permute-start.3 = (bf16[2,96,896]{2,1,0:T(8,128)(2,1)}, bf16[2,96,896]{2,1,0:T(8,128)(2,1)}, u32[]{:S(2)}, u32[]{:S(2)}) collective-permute-start(bf16[2,96,896]{2,1,0:T(8,128)(2,1)} %shard_map.485.refs_0_.refs_4_.refs_3_), channel_id=1, source_target_pairs={{0,4},{1,5},{2,6},{3,7},{4,0},{5,1},{6,2},{7,3},{8,12},{9,13},{10,... | collective-permute-start | bytes 1032200 | tf_op jit(solution)/shard_map/ppermute | solution.py:188
  41.8 17.9 %collective-permute-start.6 = (bf16[2,96,896]{2,1,0:T(8,128)(2,1)}, bf16[2,96,896]{2,1,0:T(8,128)(2,1)}, u32[]{:S(2)}, u32[]{:S(2)}) collective-permute-start(bf16[2,96,896]{2,1,0:T(8,128)(2,1)} %shard_map.486.refs_1_.refs_5_.refs_4_), channel_id=1, source_target_pairs={{0,1},{1,0},{2,3},{3,2},{4,5},{5,4},{6,7},{7,6},{8,9},{9,8},{10,11... | collective-permute-start | bytes 1032200 | tf_op jit(solution)/shard_map/ppermute | solution.py:188
  41.9 17.9 %collective-permute-start.4 = (bf16[2,96,896]{2,1,0:T(8,128)(2,1)}, bf16[2,96,896]{2,1,0:T(8,128)(2,1)}, u32[]{:S(2)}, u32[]{:S(2)}) collective-permute-start(bf16[2,96,896]{2,1,0:T(8,128)(2,1)} %shard_map.486.refs_1_.refs_5_.refs_4_), channel_id=1, source_target_pairs={{0,4},{1,5},{2,6},{3,7},{4,0},{5,1},{6,2},{7,3},{8,12},{9,13},{10,... | collective-permute-start | bytes 1032200 | tf_op jit(solution)/shard_map/ppermute | solution.py:188
  43.4 16.9 %collective-permute-start.13 = (bf16[2,96,896]{2,1,0:T(8,128)(2,1)S(1)}, bf16[2,96,896]{2,1,0:T(8,128)(2,1)}, u32[]{:S(2)}, u32[]{:S(2)}) collective-permute-start(bf16[2,96,896]{2,1,0:T(8,128)(2,1)S(1)} %collective-permute-done.9.refs_8_.refs_12_.refs_11_), channel_id=1, source_target_pairs={{0,1},{1,0},{2,3},{3,2},{4,5},{5,4},{6,7},{7,6},{8,9},{9,8},{10,11... | collective-permute-start | bytes 1032200 | tf_op jit(solution)/shard_map/ppermute | solution.py:188
  43.5 20.5 %collective-permute-start.11 = (bf16[2,96,896]{2,1,0:T(8,128)(2,1)}, bf16[2,96,896]{2,1,0:T(8,128)(2,1)}, u32[]{:S(2)}, u32[]{:S(2)}) collective-permute-start(bf16[2,96,896]{2,1,0:T(8,128)(2,1)} %collective-permute-done.3.refs_2_.refs_6_.refs_5_), channel_id=1, source_target_pairs={{0,2},{1,3},{2,0},{3,1},{4,6},{5,7},{6,4},{7,5},{8,10},{9,11},{10,... | collective-permute-start | bytes 1032200 | tf_op jit(solution)/shard_map/ppermute | solution.py:188
  124.8 80.0 %reduce-scatter.2.cloned.1.call-start = ((), (), s32[]{:S(2)}) async-start(), calls=%async_computation.3 | async-start | bytes 737280 | tf_op jit(solution)/shard_map/reduce_scatter | solution.py:209
  125.0 18.2 %collective-permute-start.17 = (bf16[2,768,768]{2,1,0:T(8,128)(2,1)}, bf16[2,768,768]{2,1,0:T(8,128)(2,1)S(1)}, u32[]{:S(2)}, u32[]{:S(2)}) collective-permute-start(bf16[2,768,768]{2,1,0:T(8,128)(2,1)} %get-tuple-element.148), channel_id=1, source_target_pairs={{0,1},{1,0},{2,3},{3,2},{4,5},{5,4},{6,7},{7,6},{8,9},{9,8},{10,11... | collective-permute-start | bytes 7077896 | tf_op jit(solution)/shard_map/ppermute | solution.py:188
  143.0 27.7 %collective-permute-start.18 = (bf16[2,768,1024]{2,1,0:T(8,128)(2,1)}, bf16[2,768,1024]{2,1,0:T(8,128)(2,1)S(1)}, u32[]{:S(2)}, u32[]{:S(2)}) collective-permute-start(bf16[2,768,1024]{2,1,0:T(8,128)(2,1)} %get-tuple-element.153), channel_id=1, source_target_pairs={{0,1},{1,0},{2,3},{3,2},{4,5},{5,4},{6,7},{7,6},{8,9},{9,8},{10,11... | collective-permute-start | bytes 9437192 | tf_op jit(solution)/shard_map/ppermute | solution.py:188
  149.6 16.3 %collective-permute-start.19 = (bf16[4,96,768]{2,1,0:T(8,128)(2,1)}, bf16[4,96,768]{2,1,0:T(8,128)(2,1)}, u32[]{:S(2)}, u32[]{:S(2)}) collective-permute-start(bf16[4,96,768]{2,1,0:T(8,128)(2,1)} %get-tuple-element.168), channel_id=1, source_target_pairs={{0,2},{1,3},{2,0},{3,1},{4,6},{5,7},{6,4},{7,5},{8,10},{9,11},{10,... | collective-permute-start | bytes 1769480 | tf_op jit(solution)/shard_map/ppermute | solution.py:188
  178.4 28.7 %collective-permute-start.24 = (bf16[4,96,1024]{2,1,0:T(8,128)(2,1)}, bf16[4,96,1024]{2,1,0:T(8,128)(2,1)S(1)}, u32[]{:S(2)}, u32[]{:S(2)}) collective-permute-start(bf16[4,96,1024]{2,1,0:T(8,128)(2,1)} %get-tuple-element.187), channel_id=1, source_target_pairs={{0,2},{1,3},{2,0},{3,1},{4,6},{5,7},{6,4},{7,5},{8,10},{9,11},{10,... | collective-permute-start | bytes 2359304 | tf_op jit(solution)/shard_map/ppermute | solution.py:188
  179.3 27.8 %collective-permute-start.25 = (bf16[4,96,1024]{2,1,0:T(8,128)(2,1)}, bf16[4,96,1024]{2,1,0:T(8,128)(2,1)S(1)}, u32[]{:S(2)}, u32[]{:S(2)}) collective-permute-start(bf16[4,96,1024]{2,1,0:T(8,128)(2,1)} %get-tuple-element.188), channel_id=1, source_target_pairs={{0,4},{1,5},{2,6},{3,7},{4,0},{5,1},{6,2},{7,3},{8,12},{9,13},{10,... | collective-permute-start | bytes 2359304 | tf_op jit(solution)/shard_map/ppermute | solution.py:188
  183.9 63.1 %all-gather.8.cloned.1.call-start = ((), (), s32[]{:S(2)}) async-start(), calls=%async_computation.4 | async-start | bytes 3932160 | tf_op jit(solution)/shard_map/all_gather | solution.py:1245
  210.7 19.0 %collective-permute-start.29 = (bf16[2,96,1024]{2,1,0:T(8,128)(2,1)}, bf16[2,96,1024]{2,1,0:T(8,128)(2,1)S(1)}, u32[]{:S(2)}, u32[]{:S(2)}) collective-permute-start(bf16[2,96,1024]{2,1,0:T(8,128)(2,1)} %get-tuple-element.189), channel_id=1, source_target_pairs={{0,2},{1,3},{2,0},{3,1},{4,6},{5,7},{6,4},{7,5},{8,10},{9,11},{10,... | collective-permute-start | bytes 1179656 | tf_op jit(solution)/shard_map/ppermute | solution.py:188
  211.8 17.8 %collective-permute-start.28 = (bf16[2,96,1024]{2,1,0:T(8,128)(2,1)}, bf16[2,96,1024]{2,1,0:T(8,128)(2,1)S(1)}, u32[]{:S(2)}, u32[]{:S(2)}) collective-permute-start(bf16[2,96,1024]{2,1,0:T(8,128)(2,1)} %get-tuple-element.190), channel_id=1, source_target_pairs={{0,4},{1,5},{2,6},{3,7},{4,0},{5,1},{6,2},{7,3},{8,12},{9,13},{10,... | collective-permute-start | bytes 1179656 | tf_op jit(solution)/shard_map/ppermute | solution.py:188
  221.4 16.8 %collective-permute-start.31 = (bf16[2,96,640]{2,1,0:T(8,128)(2,1)}, bf16[2,96,640]{2,1,0:T(8,128)(2,1)S(1)}, u32[]{:S(2)}, u32[]{:S(2)}) collective-permute-start(bf16[2,96,640]{2,1,0:T(8,128)(2,1)} %get-tuple-element.197), channel_id=1, source_target_pairs={{0,2},{1,3},{2,0},{3,1},{4,6},{5,7},{6,4},{7,5},{8,10},{9,11},{10,... | collective-permute-start | bytes 737288 | tf_op jit(solution)/shard_map/ppermute | solution.py:188
  222.3 15.9 %collective-permute-start.30 = (bf16[2,96,640]{2,1,0:T(8,128)(2,1)}, bf16[2,96,640]{2,1,0:T(8,128)(2,1)S(1)}, u32[]{:S(2)}, u32[]{:S(2)}) collective-permute-start(bf16[2,96,640]{2,1,0:T(8,128)(2,1)} %get-tuple-element.198), channel_id=1, source_target_pairs={{0,4},{1,5},{2,6},{3,7},{4,0},{5,1},{6,2},{7,3},{8,12},{9,13},{10,... | collective-permute-start | bytes 737288 | tf_op jit(solution)/shard_map/ppermute | solution.py:188
  235.1 18.3 %collective-permute-start.36 = (bf16[96,1024]{1,0:T(8,128)(2,1)}, bf16[96,1024]{1,0:T(8,128)(2,1)S(1)}, u32[]{:S(2)}, u32[]{:S(2)}) collective-permute-start(bf16[96,1024]{1,0:T(8,128)(2,1)} %get-tuple-element.209), channel_id=1, source_target_pairs={{0,16},{1,17},{2,18},{3,19},{4,20},{5,21},{6,22},{7,23},{8,24},{9,... | collective-permute-start | bytes 589832 | tf_op jit(solution)/shard_map/ppermute | solution.py:188
  235.2 18.3 %collective-permute-start.37 = (bf16[96,1024]{1,0:T(8,128)(2,1)}, bf16[96,1024]{1,0:T(8,128)(2,1)S(1)}, u32[]{:S(2)}, u32[]{:S(2)}) collective-permute-start(bf16[96,1024]{1,0:T(8,128)(2,1)} %get-tuple-element.210), channel_id=1, source_target_pairs={{0,24},{1,25},{2,26},{3,27},{4,28},{5,29},{6,30},{7,31},{8,16},{9,... | collective-permute-start | bytes 589832 | tf_op jit(solution)/shard_map/ppermute | solution.py:188
  241.5 16.1 %collective-permute-start.32 = (bf16[96,640]{1,0:T(8,128)(2,1)}, bf16[96,640]{1,0:T(8,128)(2,1)S(1)}, u32[]{:S(2)}, u32[]{:S(2)}) collective-permute-start(bf16[96,640]{1,0:T(8,128)(2,1)} %get-tuple-element.204), channel_id=1, source_target_pairs={{0,8},{1,9},{2,10},{3,11},{4,12},{5,13},{6,14},{7,15},{8,0},{9,1},... | collective-permute-start | bytes 368648 | tf_op jit(solution)/shard_map/ppermute | solution.py:188
  (55 other events, 445.9 us)
Sparse Core Ops, SparseCore 0:
  11.5 95.7 all-gather.3
  124.9 27.1 all-gather.5
  184.0 20.5 reduce-scatter.1
  213.6 33.3 all-gather.7
